TPU v7x, 32 devices: a whole 2x2x4 slice. The times are simulated.
32 devices in a mesh: replica: 2 (over y), row: 4 (over x, core), col: 4 (over z).
Axes of the slice: x: 2, y: 2, z: 4, core: 2. Of those that a mesh axis runs over, the one named last changes fastest.
Arguments:
- pair: bfloat16 [256, 128, 128], P(('replica', 'row'), 'col'), parts along dimension 0, may hold values from -6 to 6
- cotangent: bfloat16 [256, 128, 128], P(('replica', 'row'), 'col'), parts along dimension 0, may hold values from -6 to 6
- valid: int32 [256], P('replica'), parts along dimension 0, may hold values from 0 to 1, as said below
- in_gain: float32 [128], replicated, may hold values from 0.1 to 1.9
- proj_weight: bfloat16 [128, 512], replicated, may hold values from -0.5 to 0.5
- gate_weight: bfloat16 [128, 128], replicated, may hold values from -0.5 to 0.5
- out_gain: float32 [128], replicated, may hold values from 0.1 to 1.9
- out_weight: bfloat16 [128, 128], replicated, may hold values from -0.5 to 0.5
Outputs:
- update: bfloat16 [256, 128, 128], P(('replica', 'row'), 'col'), parts along dimension 0
- pair_grad: float32 [256, 128, 128], P(('replica', 'row'), 'col'), parts along dimension 0
There are 2 independent parts, one for each index of `replica`. A program takes and returns all parts, laid end to end along the dimension named above; an argument that names none is the same for every part. Nothing has to cross between parts.
Inputs may be any that keep to these rules, and one draw needn't show every extreme that they name: valid is 0 on a trailing run of padding that ends at the last token, and 1 on the first token; some tokens before the padding are masked too.
All inputs are finite; a program needn't handle non-finite values.
Results may differ from a plain program's by a relative error of at most 0.0079.
Values may be sent and summed in bfloat16 or wider, within the bound.
No kernel may reach another device: no remote copies, remote signals or barrier semaphores. Data moves between devices by JAX's collectives and lax.ppermute only.
A program may use at most 128 MiB of HBM per device.

v0:
```python
import jax
import jax.numpy as jnp
from jax import lax
from jax.sharding import PartitionSpec as P

eps_norm = 1e-05


def layer_norm(values, gain):
    mean_val = jnp.mean(values, axis=-1, keepdims=True)
    centred = values - mean_val
    inv_std = lax.rsqrt(jnp.mean(centred * centred, axis=-1, keepdims=True) + eps_norm)
    unit = centred * inv_std
    return (unit * gain, unit, inv_std)


def norm_back(grad_unit, unit, inv_std):
    first = jnp.mean(grad_unit, axis=-1, keepdims=True)
    second = jnp.mean(grad_unit * unit, axis=-1, keepdims=True)
    return inv_std * (grad_unit - first - unit * second)


def on_device(pair, cotangent, valid, in_gain, proj_weight, gate_weight, out_gain, out_weight):
    tile_rows = pair.shape[0]
    channels = pair.shape[2]
    hidden = out_weight.shape[0]
    cells = tile_rows * tile_rows
    keeper = valid.astype(jnp.float32)
    row_keep = lax.dynamic_slice_in_dim(keeper, lax.axis_index("row") * tile_rows, tile_rows)
    col_keep = lax.dynamic_slice_in_dim(keeper, lax.axis_index("col") * tile_rows, tile_rows)
    pair_keep = (row_keep[:, None] * col_keep[None, :])[:, :, None]
    normed_f, unit_in, inv_in = layer_norm(pair.astype(jnp.float32), in_gain)
    normed = normed_f.astype(jnp.bfloat16)
    flat = normed.reshape(cells, channels)
    proj = jnp.dot(flat, proj_weight, preferred_element_type=jnp.float32).reshape(
        tile_rows, tile_rows, 4 * hidden
    )
    left_sig = jax.nn.sigmoid(proj[..., :hidden])
    left_val = proj[..., hidden : 2 * hidden]
    right_sig = jax.nn.sigmoid(proj[..., 2 * hidden : 3 * hidden])
    right_val = proj[..., 3 * hidden :]
    left = (left_sig * left_val * pair_keep).astype(jnp.bfloat16)
    right = (right_sig * right_val * pair_keep).astype(jnp.bfloat16)
    panel = lax.all_gather(right, "row", axis=0, tiled=True)
    piece = panel
    tri = jnp.swapaxes(
        lax.psum_scatter(
            jnp.einsum("ikh,jkh->jih", left, piece, preferred_element_type=jnp.float32),
            "col",
            scatter_dimension=0,
            tiled=True,
        ),
        0,
        1,
    )
    tnorm_f, unit_tri, inv_tri = layer_norm(tri, out_gain)
    tnorm = tnorm_f.astype(jnp.bfloat16)
    gate = jax.nn.sigmoid(jnp.dot(flat, gate_weight, preferred_element_type=jnp.float32)).reshape(
        tile_rows, tile_rows, channels
    )
    lin = jnp.dot(
        tnorm.reshape(cells, hidden), out_weight, preferred_element_type=jnp.float32
    ).reshape(tile_rows, tile_rows, channels)
    update = (gate * lin).astype(jnp.bfloat16)
    cot = cotangent.astype(jnp.float32)
    d_lin = (cot * gate).astype(jnp.bfloat16)
    d_gpre = (cot * lin * gate * (1.0 - gate)).astype(jnp.bfloat16)
    d_tnorm = jnp.dot(
        d_lin.reshape(cells, channels), out_weight.T, preferred_element_type=jnp.float32
    ).reshape(tile_rows, tile_rows, hidden)
    d_tri = norm_back(d_tnorm * out_gain, unit_tri, inv_tri).astype(jnp.bfloat16)
    grad_rows = lax.all_gather(d_tri, "col", axis=1, tiled=True)
    back_panel = lax.all_gather(right, "row", axis=0, tiled=True)
    piece = grad_rows
    d_right = lax.psum_scatter(
        jnp.einsum("ijh,ikh->jkh", piece, left, preferred_element_type=jnp.float32),
        "row",
        scatter_dimension=0,
        tiled=True,
    )
    d_left = jnp.einsum("ijh,jkh->ikh", grad_rows, back_panel, preferred_element_type=jnp.float32)
    d_proj = jnp.concatenate(
        [
            d_left * pair_keep * left_val * left_sig * (1.0 - left_sig),
            d_left * pair_keep * left_sig,
            d_right * pair_keep * right_val * right_sig * (1.0 - right_sig),
            d_right * pair_keep * right_sig,
        ],
        axis=-1,
    ).astype(jnp.bfloat16)
    d_normed = jnp.dot(
        d_proj.reshape(cells, 4 * hidden), proj_weight.T, preferred_element_type=jnp.float32
    )
    d_normed = d_normed + jnp.dot(
        d_gpre.reshape(cells, channels), gate_weight.T, preferred_element_type=jnp.float32
    )
    pair_grad = norm_back(
        d_normed.reshape(tile_rows, tile_rows, channels) * in_gain, unit_in, inv_in
    )
    return (update, pair_grad)


def solution(mesh):
    placed = (
        P(("replica", "row"), "col", None),
        P(("replica", "row"), "col", None),
        P("replica"),
        P(),
        P(),
        P(),
        P(),
        P(),
    )
    return jax.shard_map(
        on_device,
        mesh=mesh,
        in_specs=placed,
        out_specs=(P(("replica", "row"), "col", None), P(("replica", "row"), "col", None)),
        check_vma=False,
    )
```

profile of v0, /device:TPU:0, one launch (start us, length us, event | category | flops | bytes accessed | tf_op | source)
XLA Modules:
  0.0 173.3 jit_solution(6992598426182979484)
XLA Ops:
  7.2 1.2 convert_reduce_fusion
  8.4 1.3 fusion.19
  9.8 0.7 convert_element_type.37
  10.4 1.3 fusion.15
  11.8 0.7 copy-done.6
  13.0 1.0 multiply_convert_fusion.7
  14.1 1.6 copy.26
  15.7 17.9 %all-gather.3.cloned.1.call-done = bf16[128,32,128]{2,1,0:T(8,128)(2,1)} async-done(((bf16[32,32,128]{2,1,0:T(8,128)(2,1)}), bf16[128,32,128]{2,1,0:T(8,128)(2,1)}) %all-gather.3.cloned.1.call-update) | async-done | bytes 1048592 | tf_op jit(solution)/shard_map/all_gather | solution.py:44
  33.6 3.2 %copy.23 = bf16[128,32,128]{0,1,2:T(8,128)(2,1)} copy(bf16[128,32,128]{2,1,0:T(8,128)(2,1)} %all-gather.3.cloned.1.call-done) | data formatting | bytes 2097152 | tf_op jit(solution)/shard_map/all_gather | solution.py:44
  36.8 3.1 %convolution_bitcast_fusion = f32[128,32,128]{0,1,2:T(8,128)} fusion(bf16[128,32,128]{0,1,2:T(8,128)(2,1)} %copy.23, bf16[32,32,128]{0,1,2:T(8,128)(2,1)S(1)} %copy.26), kind=kOutput, calls=%fused_computation | convolution fusion | flops 33554432 | bytes 3407872 | tf_op jit(solution)/shard_map/ikh,jkh->jih/dot_general | solution.py:48
  39.9 3.5 %copy.20 = f32[128,32,128]{2,1,0:T(8,128)} copy(f32[128,32,128]{0,1,2:T(8,128)} %convolution_bitcast_fusion) | data formatting | bytes 4194304 | tf_op jit(solution)/shard_map/ikh,jkh->jih/transpose | solution.py:48
  43.4 0.9 copy-done.7
  44.6 42.8 %reduce-scatter.3.cloned.1.call-done = f32[32,32,128]{2,1,0:T(8,128)} async-done(((f32[128,32,128]{2,1,0:T(8,128)}), f32[32,32,128]{2,1,0:T(8,128)}) %reduce-scatter.3.cloned.1.call-update) | async-done | bytes 524304 | tf_op jit(solution)/shard_map/reduce_scatter | solution.py:47
  87.4 1.5 bitcast_reduce_fusion
  88.9 1.6 multiply_reduce_fusion.2
  90.5 1.8 %fusion.41 = (f32[32,32]{1,0:T(8,128)S(1)}, f32[32,32]{1,0:T(8,128)S(1)}, f32[32,32,128]{2,1,0:T(8,128)S(1)}) fusion(f32[32,32]{1,0:T(8,128)S(1)} %add_rsqrt_fusion, f32[32,32]{1,0:T(8,128)S(1)} %broadcast_multiply_fusion.4, f32[32,32,128]{2,1,0:T(8,128)} %reduce-scatter.3.cloned.1.call-done, f32[128]{0:T(128)} %param.14, bf16[128,128]{1,0:T(8,128)(2,1)} %param.15, ...), kind=kOutput, calls=%fused_computation.74 | convolution fusion | flops 34732032 | bytes 1884672 | tf_op jit(solution)/shard_map/dot_general | solution.py:68
  92.4 0.6 multiply_convert_fusion.4
  93.0 0.8 copy.22
  94.0 27.2 %all-gather.5.cloned.1.call-done = bf16[32,128,128]{2,0,1:T(8,128)(2,1)} async-done(((bf16[32,32,128]{2,0,1:T(8,128)(2,1)}), bf16[32,128,128]{2,0,1:T(8,128)(2,1)}) %all-gather.5.cloned.1.call-update) | async-done | bytes 1048592 | tf_op jit(solution)/shard_map/all_gather | solution.py:72
  121.2 3.2 %copy.24 = bf16[32,128,128]{1,0,2:T(8,128)(2,1)} copy(bf16[32,128,128]{2,0,1:T(8,128)(2,1)} %all-gather.5.cloned.1.call-done) | data formatting | bytes 2097152 | tf_op jit(solution)/shard_map/all_gather | solution.py:72
  124.4 3.3 %fusion.44 = f32[128,32,128]{2,1,0:T(8,128)} fusion(bf16[32,32,128]{0,1,2:T(8,128)(2,1)} %copy-done.2, bf16[32,128,128]{1,0,2:T(8,128)(2,1)} %copy.24), kind=kOutput, calls=%fused_computation.77 | convolution fusion | flops 33554432 | bytes 3407872 | tf_op jit(solution)/shard_map/ijh,ikh->jkh/dot_general | solution.py:76
  127.7 3.5 %copy.28 = f32[128,32,128]{0,1,2:T(8,128)} copy(f32[128,32,128]{2,1,0:T(8,128)} %fusion.44) | data formatting | bytes 4194304 | tf_op jit(solution)/shard_map/ijh,ikh->jkh/dot_general | solution.py:76
  131.2 2.2 %fusion.23 = (bf16[32,32,128]{2,1,0:T(8,128)(2,1)S(1)}, bf16[32,32,128]{2,1,0:T(8,128)(2,1)}) fusion(f32[32,32,128]{2,1,0:T(8,128)S(1)} %bitcast.61, bf16[32,32,128]{2,1,0:T(8,128)(2,1)S(1)} %copy-done.8, bf16[128,128]{1,0:T(8,128)(2,1)} %param.15, f32[32,32,128]{2,1,0:T(8,128)S(1)} %copy-done.1, f32[128]{0:T(128)} %param.14, f32[32,32]{1,0:T(8,128)} %copy-done.11, ...), kind=kOutput, calls=%fused_computation.31 | convolution fusion | flops 35127296 | bytes 1876480 | tf_op jit(solution)/shard_map/dot_general | solution.py:61
  133.4 1.0 fusion.45
  134.4 2.0 %fusion.43 = f32[128,32,32]{2,1,0:T(8,128)} fusion(bf16[128,32,128]{0,1,2:T(8,128)(2,1)S(1)} %copy-done.3, bf16[32,128,128]{1,0,2:T(8,128)(2,1)S(1)} %copy-done.4), kind=kOutput, calls=%fused_computation.76 | convolution fusion | flops 33554432 | bytes 2621440 | tf_op jit(solution)/shard_map/ijh,jkh->ikh/dot_general | solution.py:81
  136.3 2.8 %copy.25 = f32[128,32,32]{0,1,2:T(8,128)S(1)} copy(f32[128,32,32]{2,1,0:T(8,128)} %fusion.43) | data formatting | bytes 1048576 | tf_op jit(solution)/shard_map/ijh,jkh->ikh/dot_general | solution.py:81
  139.2 23.1 %reduce-scatter.5.cloned.1.call-done = f32[32,32,128]{2,1,0:T(8,128)} async-done(((f32[128,32,128]{2,1,0:T(8,128)}), f32[32,32,128]{2,1,0:T(8,128)}) %reduce-scatter.5.cloned.1.call-update) | async-done | bytes 524304 | tf_op jit(solution)/shard_map/reduce_scatter | solution.py:75
  162.3 1.5 multiply_convert_fusion.3
  163.8 0.5 multiply_reduce_fusion
  164.3 0.4 copy-done.5
  164.7 0.5 fusion.16
  165.3 1.4 fusion.18
  (53 shorter events, 1.4 us)
Async XLA Ops:
  7.2 5.3 %copy-start = (bf16[128,512]{1,0:T(8,128)(2,1)S(1)}, bf16[128,512]{1,0:T(8,128)(2,1)}, u32[]{:S(2)}) copy-start(bf16[128,512]{1,0:T(8,128)(2,1)} %param.12) | copy-start | bytes 393220
  7.2 26.5 %all-gather.3.cloned.1.call-start = ((), (), s32[]{:S(2)}) async-start(), calls=%async_computation.2 | async-start | bytes 1310720 | tf_op jit(solution)/shard_map/all_gather | solution.py:44
  8.4 2.0 %copy-start.9 = (f32[32,32]{1,0:T(8,128)}, f32[32,32]{1,0:T(8,128)S(1)}, u32[]{:S(2)}) copy-start(f32[32,32]{1,0:T(8,128)S(1)} %broadcast_multiply_fusion.5) | copy-start | bytes 12292
  9.8 2.0 %copy-start.12 = (f32[32,32]{1,0:T(8,128)}, f32[32,32]{1,0:T(8,128)S(1)}, u32[]{:S(2)}) copy-start(f32[32,32]{1,0:T(8,128)S(1)} %add_rsqrt_fusion.1) | copy-start | bytes 12292
  11.7 0.7 copy-start.6
  13.0 1.1 copy-start.14
  14.1 73.3 %reduce-scatter.3.cloned.1.call-start = ((), (), s32[]{:S(2)}) async-start(), calls=%async_computation.3 | async-start | bytes 2621440 | tf_op jit(solution)/shard_map/reduce_scatter | solution.py:47
  15.7 24.1 %copy-start.2 = (bf16[32,32,128]{0,1,2:T(8,128)(2,1)}, bf16[32,32,128]{0,1,2:T(8,128)(2,1)S(1)}, u32[]{:S(2)}) copy-start(bf16[32,32,128]{0,1,2:T(8,128)(2,1)S(1)} %copy.26) | copy-start | bytes 786436
  43.3 0.9 copy-start.7
  43.3 1.0 copy-start.16
  43.4 47.1 %copy-start.8 = (bf16[32,32,128]{2,1,0:T(8,128)(2,1)S(1)}, bf16[32,32,128]{2,1,0:T(8,128)(2,1)}, u32[]{:S(2)}) copy-start(bf16[32,32,128]{2,1,0:T(8,128)(2,1)} %param.9) | copy-start | bytes 786436
  43.4 77.8 %all-gather.5.cloned.1.call-start = ((), (), s32[]{:S(2)}) async-start(), calls=%async_computation.4 | async-start | bytes 1310720 | tf_op jit(solution)/shard_map/all_gather | solution.py:72
  87.4 5.0 %copy-start.1 = (f32[32,32,128]{2,1,0:T(8,128)S(1)}, f32[32,32,128]{2,1,0:T(8,128)}, u32[]{:S(2)}) copy-start(f32[32,32,128]{2,1,0:T(8,128)} %reduce-scatter.3.cloned.1.call-done) | copy-start | bytes 1572868
  90.5 2.5 %copy-start.11 = (f32[32,32]{1,0:T(8,128)}, f32[32,32]{1,0:T(8,128)S(1)}, u32[]{:S(2)}) copy-start(f32[32,32]{1,0:T(8,128)S(1)} %add_rsqrt_fusion) | copy-start | bytes 12292
  93.8 68.4 %reduce-scatter.5.cloned.1.call-start = ((), (), s32[]{:S(2)}) async-start(), calls=%async_computation.5 | async-start | bytes 2621440 | tf_op jit(solution)/shard_map/reduce_scatter | solution.py:75
  131.2 3.2 %copy-start.3 = (bf16[128,32,128]{0,1,2:T(8,128)(2,1)S(1)}, bf16[128,32,128]{0,1,2:T(8,128)(2,1)}, u32[]{:S(2)}) copy-start(bf16[128,32,128]{0,1,2:T(8,128)(2,1)} %copy.23) | copy-start | bytes 3145732
  131.2 3.2 %copy-start.4 = (bf16[32,128,128]{1,0,2:T(8,128)(2,1)S(1)}, bf16[32,128,128]{1,0,2:T(8,128)(2,1)}, u32[]{:S(2)}) copy-start(bf16[32,128,128]{1,0,2:T(8,128)(2,1)} %copy.24) | copy-start | bytes 3145732
  136.3 25.9 %copy-start.15 = (f32[32,32]{1,0:T(8,128)S(1)}, f32[32,32]{1,0:T(8,128)}, u32[]{:S(2)}) copy-start(f32[32,32]{1,0:T(8,128)} %copy-done.14) | copy-start | bytes 12292
  139.2 24.6 %copy-start.17 = (f32[128]{0:T(128)S(1)}, f32[128]{0:T(128)}, u32[]{:S(2)}) copy-start(f32[128]{0:T(128)} %param.11) | copy-start | bytes 1540
  163.8 1.0 copy-start.5
  163.8 0.9 copy-start.10
  163.8 0.9 copy-start.13
Sparse Core Ops, SparseCore 0:
  14.2 19.4 all-gather.2
  43.5 43.8 reduce-scatter.2
  93.9 27.2 all-gather.4
  131.3 30.9 reduce-scatter.4
where the time goes:
time: 174 us; the launch traced here: 173 us
  waiting for transfers between devices  111 us (64%)
  local copies, waits for them, and re-layouts  20.8 us (12%)
  matrix products  14.5 us (8%)
  between operations  14.1 us (8%)
  other arithmetic  12.6 us (7%)
    reduce_scatter x1, waiting for transfers between devices, on_device(): lax.psum_scatter(jnp.einsum('ikh,jkh->jih', left, piece, preferred_elemen...  42.8 us
    all_gather x1, waiting for transfers between devices, on_device(): grad_rows = lax.all_gather(d_tri, 'col', axis=1, tiled=True)  27.2 us
    reduce_scatter x1, waiting for transfers between devices, on_device(): lax.psum_scatter(jnp.einsum('ijh,ikh->jkh', piece, left, preferred_elemen...  23.1 us
    all_gather x1, waiting for transfers between devices, on_device(): panel = lax.all_gather(right, 'row', axis=0, tiled=True)  17.9 us
  transfers between devices with their start and end apart: 4, of which 4 were waited for; matrix products, arithmetic and copies ran while one was open for 6% of the time, Pallas kernels for 0%

commit v1 on v0

--- a/solution.py
+++ b/solution.py
@@ -1,6 +1,10 @@
+import functools
+
 import jax
 import jax.numpy as jnp
 from jax import lax
+from jax.experimental import pallas as pl
+from jax.experimental.pallas import tpu as pltpu
 from jax.sharding import PartitionSpec as P
 
 eps_norm = 1e-05
@@ -100,6 +104,316 @@
     return (update, pair_grad)
 
 
+F32 = jnp.float32
+BF16 = jnp.bfloat16
+LANES = 128
+
+
+def dot(a, b, dims):
+    return lax.dot_general(a, b, ((dims[:1], dims[1:]), ((), ())), preferred_element_type=F32)
+
+
+def column(gain):
+    n = gain.shape[1]
+    return jnp.broadcast_to(gain, (n, n)).T
+
+
+def spread(col, width):
+    return jnp.concatenate([col] * (width // col.shape[1]), axis=1)
+
+
+def unit_rows(values):
+    n = values.shape[0]
+    centred = values - jnp.sum(values, axis=0, keepdims=True) * (1.0 / n)
+    inv = lax.rsqrt(jnp.sum(centred * centred, axis=0, keepdims=True) * (1.0 / n) + eps_norm)
+    return centred * inv, inv
+
+
+def unit_back(q, unit, inv):
+    n = q.shape[0]
+    first = jnp.sum(q, axis=0, keepdims=True) * (1.0 / n)
+    second = jnp.sum(q * unit, axis=0, keepdims=True) * (1.0 / n)
+    return inv * (q - first - unit * second)
+
+
+def swap_blocks(a):
+    width = a[0].shape[1] // 4
+    lane = lax.broadcasted_iota(jnp.int32, a[0].shape, 1)
+    low = lane < 2 * width
+    even = (lane // width) % 2 == 0
+    half = lambda x: pltpu.roll(x, 2 * width, 1)
+    t0 = jnp.where(low, a[0], half(a[2]))
+    t2 = jnp.where(low, half(a[0]), a[2])
+    t1 = jnp.where(low, a[1], half(a[3]))
+    t3 = jnp.where(low, half(a[1]), a[3])
+    up = lambda x: pltpu.roll(x, width, 1)
+    down = lambda x: pltpu.roll(x, 3 * width, 1)
+    return (
+        jnp.where(even, t0, up(t1)),
+        jnp.where(even, down(t0), t1),
+        jnp.where(even, t2, up(t3)),
+        jnp.where(even, down(t2), t3),
+    )
+
+
+def keep_row(valid_ref, tile, cells):
+    n = valid_ref.shape[1]
+    v = jnp.broadcast_to(valid_ref[...].astype(F32), (8, n))
+    token = lax.broadcasted_iota(jnp.int32, (n, cells), 0)
+    cell = lax.broadcasted_iota(jnp.int32, (n, cells), 1)
+    first = (token == lax.axis_index("row") * tile + cell // tile).astype(F32)
+    second = (token == lax.axis_index("col") * tile + cell % tile).astype(F32)
+    return (dot(v, first, (1, 0)) * dot(v, second, (1, 0)))[:1]
+
+
+def normed_of(pair_ref, in_gain_ref):
+    unit, inv = unit_rows(pair_ref[...].astype(F32).T)
+    normed = (unit * spread(column(in_gain_ref[...]), unit.shape[1])).astype(BF16)
+    return normed, unit, inv
+
+
+def project_kernel(tile, pair_ref, valid_ref, in_gain_ref, proj_ref, out_ref):
+    cells, channels = pair_ref.shape
+    hidden = proj_ref.shape[1] // 4
+    shards, both, _ = out_ref.shape
+    normed, _, _ = normed_of(pair_ref, in_gain_ref)
+    keep = keep_row(valid_ref, tile, cells)
+    sides = []
+    for side in range(2):
+        weight = proj_ref[:, 2 * hidden * side : 2 * hidden * (side + 1)].T
+        proj = dot(weight, normed, (1, 0))
+        sides.append(jax.nn.sigmoid(proj[:hidden]) * proj[hidden:] * keep)
+    for s in range(shards):
+        rows = slice(s * both // 2, (s + 1) * both // 2)
+        out_ref[s] = jnp.concatenate([sides[0][rows], sides[1][rows]], axis=0).astype(BF16)
+
+
+def local_kernel(
+    tile, pair_ref, cot_ref, valid_ref, in_gain_ref, proj_ref, gate_w_ref, out_gain_ref, out_w_ref,
+    unit_ref, inv_ref, factor_ref, gate_ref, back_ref, q_ref,
+):
+    cells, channels = pair_ref.shape
+    hidden = proj_ref.shape[1] // 4
+    normed, unit, inv = normed_of(pair_ref, in_gain_ref)
+    unit_ref[...] = unit
+    inv_ref[...] = inv
+    keep = keep_row(valid_ref, tile, cells)
+    for side in range(2):
+        weight = proj_ref[:, 2 * hidden * side : 2 * hidden * (side + 1)].T
+        proj = dot(weight, normed, (1, 0))
+        sig = jax.nn.sigmoid(proj[:hidden])
+        factor_ref[2 * side] = keep * proj[hidden:] * sig * (1.0 - sig)
+        factor_ref[2 * side + 1] = keep * sig
+    gate = jax.nn.sigmoid(dot(gate_w_ref[...].T, normed, (1, 0)))
+    cot = cot_ref[...].astype(F32).T
+    gate_ref[...] = gate
+    back_ref[...] = cot * gate * (1.0 - gate)
+    d_lin = (cot * gate).astype(BF16)
+    q_ref[...] = dot(out_w_ref[...], d_lin, (1, 0)) * spread(column(out_gain_ref[...]), cells)
+
+
+def tri_kernel(grid_rows, recv_ref, left_ref, right_ref, out_ref, rows, tri):
+    devices, both, cells = recv_ref.shape
+    per = both // 2
+    n = left_ref.shape[1]
+    tile = n // grid_rows
+    groups = cells // LANES
+    for r in range(grid_rows):
+        blocks = [recv_ref[grid_rows * r + c].astype(F32) for c in range(grid_rows)]
+        for g in range(groups):
+            lanes = slice(g * LANES, (g + 1) * LANES)
+            for p, rows_p in enumerate(swap_blocks([b[:, lanes] for b in blocks])):
+                at = (r * tile + g * grid_rows + p) * both
+                rows[at : at + both, :] = rows_p
+    for h in range(per):
+        left = rows[pl.ds(h, n, stride=both), :].astype(BF16)
+        right = rows[pl.ds(per + h, n, stride=both), :].astype(BF16)
+        left_ref[h] = left
+        right_ref[h] = right
+        tri[pl.ds(h, n, stride=per), :] = dot(left, right, (1, 1))
+    half = groups // 2
+    for r in range(grid_rows):
+        for g in range(half):
+            parts = []
+            for k in range(2):
+                at = (r * tile + (g + k * half) * grid_rows) * per
+                parts.append(swap_blocks([tri[at + p * per : at + (p + 1) * per, :] for p in range(grid_rows)]))
+            for c in range(grid_rows):
+                out_ref[grid_rows * r + c, :, g * LANES : (g + 1) * LANES] = jnp.concatenate(
+                    [parts[0][c], parts[1][c]], axis=0
+                ).astype(BF16)
+
+
+def halves_of(recv_ref):
+    shards, both, width = recv_ref.shape
+    x = recv_ref[...].astype(F32)
+    rows = shards * both // 2
+    return jnp.concatenate(
+        [x[:, : both // 2].reshape(rows, width), x[:, both // 2 :].reshape(rows, width)], axis=1
+    )
+
+
+def d_tri_kernel(recv_ref, q_ref, out_ref, unit_ref):
+    shards, both, width = recv_ref.shape
+    unit, inv = unit_rows(halves_of(recv_ref))
+    unit_ref[...] = unit
+    d_tri = unit_back(q_ref[...], unit, inv)
+    out_ref[...] = jnp.concatenate(
+        [d_tri[:, :width].reshape(shards, both // 2, width), d_tri[:, width:].reshape(shards, both // 2, width)],
+        axis=1,
+    ).astype(BF16)
+
+
+def update_kernel(unit_ref, gate_ref, back_ref, out_gain_ref, out_w_ref, gate_w_ref, update_ref, d_normed_ref):
+    unit = unit_ref[...]
+    tnorm = (unit * spread(column(out_gain_ref[...]), unit.shape[1])).astype(BF16)
+    lin = dot(out_w_ref[...].T, tnorm, (1, 0))
+    update_ref[...] = (gate_ref[...] * lin).T.astype(BF16)
+    d_gpre = (back_ref[...] * lin).astype(BF16)
+    d_normed_ref[...] = dot(gate_w_ref[...], d_gpre, (1, 0))
+
+
+def sides_kernel(grid_rows, recv_ref, left_ref, right_ref, out_ref, d_tri, rows):
+    devices, both, cells = out_ref.shape
+    per = both // 2
+    n = left_ref.shape[1]
+    tile = n // grid_rows
+    groups = cells // LANES
+    half = groups // 2
+    for r in range(grid_rows):
+        blocks = [recv_ref[grid_rows * r + c].astype(F32) for c in range(grid_rows)]
+        for g in range(half):
+            lanes = slice(g * LANES, (g + 1) * LANES)
+            for p, rows_p in enumerate(swap_blocks([b[:, lanes] for b in blocks])):
+                for k in range(2):
+                    at = (r * tile + (g + k * half) * grid_rows + p) * per
+                    d_tri[at : at + per, :] = rows_p[k * per : (k + 1) * per]
+    for h in range(per):
+        grad = d_tri[pl.ds(h, n, stride=per), :].astype(BF16)
+        rows[pl.ds(h, n, stride=both), :] = dot(grad, right_ref[h], (1, 0))
+        rows[pl.ds(per + h, n, stride=both), :] = dot(grad, left_ref[h], (0, 0))
+    for r in range(grid_rows):
+        for g in range(groups):
+            at = (r * tile + g * grid_rows) * both
+            parts = swap_blocks([rows[at + p * both : at + (p + 1) * both, :] for p in range(grid_rows)])
+            for c in range(grid_rows):
+                out_ref[grid_rows * r + c, :, g * LANES : (g + 1) * LANES] = parts[c].astype(BF16)
+
+
+def pair_grad_kernel(recv_ref, factor_ref, d_normed_ref, unit_ref, inv_ref, in_gain_ref, proj_ref, out_ref):
+    shards, both, cells = recv_ref.shape
+    hidden = shards * both // 2
+    x = recv_ref[...].astype(F32)
+    d_left = x[:, : both // 2].reshape(hidden, cells)
+    d_right = x[:, both // 2 :].reshape(hidden, cells)
+    d_proj = jnp.concatenate(
+        [(grad * factor_ref[2 * side + part]).astype(BF16) for side, grad in enumerate((d_left, d_right)) for part in range(2)],
+        axis=0,
+    )
+    d_normed = dot(proj_ref[...], d_proj, (1, 0)) + d_normed_ref[...]
+    q = d_normed * spread(column(in_gain_ref[...]), cells)
+    out_ref[...] = unit_back(q, unit_ref[...], inv_ref[...]).T
+
+
+def call(kernel, outs, args, flops, scratch=()):
+    given = sum(a.size * a.dtype.itemsize for a in args)
+    made = sum(o.size * o.dtype.itemsize for o in outs)
+    return pl.pallas_call(
+        kernel,
+        out_shape=tuple(outs),
+        scratch_shapes=list(scratch),
+        compiler_params=pltpu.CompilerParams(vmem_limit_bytes=48 * 2**20),
+        cost_estimate=pl.CostEstimate(flops=flops, bytes_accessed=given + made, transcendentals=0),
+    )(*args)
+
+
+def by_channel(pair, cotangent, valid, in_gain, proj_weight, gate_weight, out_gain, out_weight):
+    tile, _, channels = pair.shape
+    hidden = out_weight.shape[0]
+    cells = tile * tile
+    grid_rows = lax.axis_size("row")
+    devices = grid_rows * lax.axis_size("col")
+    per = hidden // devices
+    n = tile * grid_rows
+    shape = lambda dims, dtype: jax.ShapeDtypeStruct(dims, dtype)
+    whole = lambda x: lax.all_to_all(x, ("row", "col"), 0, 0, tiled=True)
+    flat = pair.reshape(cells, channels)
+    flat_cot = cotangent.reshape(cells, channels)
+    valid_row = valid.reshape(1, -1)
+    in_row = in_gain.reshape(1, -1)
+    out_row = out_gain.reshape(1, -1)
+    both = 2 * per
+    plane = shape((channels, cells), F32)
+
+    (sides,) = call(
+        functools.partial(project_kernel, tile),
+        [shape((devices, both, cells), BF16)],
+        (flat, valid_row, in_row, proj_weight),
+        2 * cells * channels * 4 * hidden,
+    )
+    sides = whole(sides)
+    unit, inv, factors, gate, back, q = call(
+        functools.partial(local_kernel, tile),
+        [plane, shape((1, cells), F32), shape((4, hidden, cells), F32), plane, plane, plane],
+        (flat, flat_cot, valid_row, in_row, proj_weight, gate_weight, out_row, out_weight),
+        2 * cells * channels * 6 * hidden,
+    )
+    left, right, tri = call(
+        functools.partial(tri_kernel, grid_rows),
+        [shape((per, n, n), BF16), shape((per, n, n), BF16), shape((devices, both, cells // 2), BF16)],
+        (sides,),
+        2 * per * n * n * n,
+        [pltpu.VMEM((n * both, n), F32), pltpu.VMEM((n * per, n), F32)],
+    )
+    tri = whole(tri)
+    d_tri, unit_tri = call(
+        d_tri_kernel,
+        [shape((devices, both, cells // 2), BF16), plane],
+        (tri, q),
+        20 * cells * hidden,
+    )
+    d_tri = whole(d_tri)
+    update, d_normed = call(
+        update_kernel,
+        [shape((cells, channels), BF16), plane],
+        (unit_tri, gate, back, out_row, out_weight, gate_weight),
+        2 * cells * channels * 2 * hidden,
+    )
+    (d_sides,) = call(
+        functools.partial(sides_kernel, grid_rows),
+        [shape((devices, both, cells), BF16)],
+        (d_tri, left, right),
+        4 * per * n * n * n,
+        [pltpu.VMEM((n * per, n), F32), pltpu.VMEM((n * both, n), F32)],
+    )
+    d_sides = whole(d_sides)
+    (pair_grad,) = call(
+        pair_grad_kernel,
+        [shape((cells, channels), F32)],
+        (d_sides, factors, d_normed, unit, inv, in_row, proj_weight),
+        2 * cells * channels * 4 * hidden,
+    )
+    return (update.reshape(pair.shape), pair_grad.reshape(pair.shape))
+
+
+def fits(pair, out_weight):
+    rows, cols = lax.axis_size("row"), lax.axis_size("col")
+    tile, tile_cols, channels = pair.shape
+    hidden = out_weight.shape[0]
+    return (
+        rows == cols == 4
+        and tile == tile_cols
+        and tile * rows == LANES
+        and channels == LANES
+        and hidden == 8 * rows * cols
+    )
+
+
+def step(pair, cotangent, valid, in_gain, proj_weight, gate_weight, out_gain, out_weight):
+    plan = by_channel if fits(pair, out_weight) else on_device
+    return plan(pair, cotangent, valid, in_gain, proj_weight, gate_weight, out_gain, out_weight)
+
+
 def solution(mesh):
     placed = (
         P(("replica", "row"), "col", None),
@@ -112,7 +426,7 @@
         P(),
     )
     return jax.shard_map(
-        on_device,
+        step,
         mesh=mesh,
         in_specs=placed,
         out_specs=(P(("replica", "row"), "col", None), P(("replica", "row"), "col", None)),

time: 174 us -> 87.4 us (0.50)
  waiting for transfers between devices: 111 us -> 15.5 us
  blocking collectives: 0 us -> 36.2 us
  matrix products: 14.5 us -> 0 us
  between operations: 14.1 us -> 0.8 us
  other arithmetic: 12.6 us -> 0 us
  Pallas kernels: 0 us -> 9.64 us
  starting transfers between devices: 0.35 us -> 7.1 us
  local copies, waits for them, and re-layouts: 20.8 us -> 17.2 us
    reduce_scatter x2 -> x0, waiting for transfers between devices: 65.9 us -> none  [the longest x1 42.8 us: on_device(): lax.psum_scatter(jnp.einsum('ikh,jkh->jih', left, piece, preferred_elemen...]
    all_gather x2 -> x0, waiting for transfers between devices: 45.1 us -> none  [the longest x1 27.2 us: on_device(): grad_rows = lax.all_gather(d_tri, 'col', axis=1, tiled=True)]
    all_to_all x0 -> x2, blocking collectives: none -> 36.2 us  [by_channel(): whole = lambda x: lax.all_to_all(x, ('row', 'col'), 0, 0, tiled=True)]
    all_to_all x0 -> x2, waiting for transfers between devices: none -> 15.5 us  [by_channel(): whole = lambda x: lax.all_to_all(x, ('row', 'col'), 0, 0, tiled=True)]
    unnamed x36 -> x52, local copies, waits for them, and re-layouts: 2.05 us -> 17.2 us
    dot_general x9 -> x0, matrix products: 14.5 us -> none  [the longest x1 3.26 us: on_device(): jnp.einsum('ijh,ikh->jkh', piece, left, preferred_element_type=jnp.float32)]
    pallas_call x0 -> x7, Pallas kernels: none -> 9.64 us  [call(): pl.pallas_call(kernel, out_shape=tuple(outs), scratch_shapes=list(scratch...]
    all_to_all x0 -> x2, starting transfers between devices: none -> 7.1 us  [by_channel(): whole = lambda x: lax.all_to_all(x, ('row', 'col'), 0, 0, tiled=True)]
  transfers between devices with their start and end apart: 4 -> 2, of which waited for: 4 -> 2; matrix products, arithmetic and copies ran while one was open for 6% -> 0% of each run, Pallas kernels for 0% -> 3%
where the time goes in v1:
time: 87.4 us; the launch traced here: 86.5 us
  blocking collectives  36.2 us (41%)
  local copies, waits for them, and re-layouts  17.2 us (20%)
  waiting for transfers between devices  15.5 us (18%)
  Pallas kernels  9.64 us (11%)
  starting transfers between devices  7.1 us (8%)
    all_to_all x2, blocking collectives, by_channel(): whole = lambda x: lax.all_to_all(x, ('row', 'col'), 0, 0, tiled=True)  36.2 us
    unnamed x52, local copies, waits for them, and re-layouts  17.2 us
    all_to_all x2, waiting for transfers between devices, by_channel(): whole = lambda x: lax.all_to_all(x, ('row', 'col'), 0, 0, tiled=True)  15.5 us
    pallas_call x7, Pallas kernels, call(): pl.pallas_call(kernel, out_shape=tuple(outs), scratch_shapes=list(scratch...  9.64 us
    all_to_all x2, starting transfers between devices, by_channel(): whole = lambda x: lax.all_to_all(x, ('row', 'col'), 0, 0, tiled=True)  7.1 us
  transfers between devices with their start and end apart: 2, of which 2 were waited for; matrix products, arithmetic and copies ran while one was open for 0% of the time, Pallas kernels for 3%

profile of v1, /device:TPU:0, one launch (start us, length us, event | category | flops | bytes accessed | tf_op | source)
XLA Modules:
  0.0 86.5 jit_solution(13031220316350559540)
XLA Ops:
  0.7 0.9 %copy-done.8 = bf16[128,512]{1,0:T(8,128)(2,1)S(1)} copy-done((bf16[128,512]{1,0:T(8,128)(2,1)S(1)}, bf16[128,512]{1,0:T(8,128)(2,1)}, u32[]{:S(2)}) %copy-start.8) | copy-done | bytes 131096
  1.6 0.9 %copy-done.14 = bf16[32,32,128]{2,1,0:T(8,128)(2,1)S(1)} copy-done((bf16[32,32,128]{2,1,0:T(8,128)(2,1)S(1)}, bf16[32,32,128]{2,1,0:T(8,128)(2,1)}, u32[]{:S(2)}) %copy-start.14) | copy-done | bytes 262168
  2.5 0.7 copy-done.20
  3.2 0.7 copy-done.22
  3.8 0.6 shard_map.95
  4.5 22.8 %all_to_all.20.recv_ref = bf16[16,16,1024]{2,1,0:T(8,128)(2,1)S(1)} all-to-all(bf16[16,16,1024]{2,1,0:T(8,128)(2,1)S(1)} %shard_map.95), channel_id=1, replica_groups=mesh['replica'=2,'row'=4,'col'=4] {'row','col'}, dimensions={0} | all-to-all | bytes 1048576 | tf_op jit(solution)/shard_map/all_to_all | solution.py:339
  27.3 2.8 %shard_map.96 = (bf16[8,128,128]{2,1,0:T(8,128)(2,1)S(1)}, bf16[8,128,128]{2,1,0:T(8,128)(2,1)S(1)}, bf16[16,16,512]{2,1,0:T(8,128)(2,1)}) custom-call(bf16[16,16,1024]{2,1,0:T(8,128)(2,1)S(1)} %all_to_all.20.recv_ref), custom_call_target="tpu_custom_call" | custom-call | flops 33554432 | bytes 1310720 | tf_op jit(solution)/shard_map/pallas_call | solution.py:321
  30.1 0.7 copy-done.10
  30.8 0.7 copy-done.12
  31.5 3.5 %all-to-all-start.1 = ((bf16[16,16,512]{2,1,0:T(8,128)(2,1)}), bf16[16,16,512]{2,1,0:T(8,128)(2,1)S(1)}, u32[]{:S(2)}, u32[]{:S(2)}) async-start(bf16[16,16,512]{2,1,0:T(8,128)(2,1)} %get-tuple-element.15), calls=%async_computation.1 | async-start | bytes 524288 | tf_op jit(solution)/shard_map/all_to_all | solution.py:339
  35.1 0.9 %copy-done.15 = bf16[32,32,128]{2,1,0:T(8,128)(2,1)S(1)} copy-done((bf16[32,32,128]{2,1,0:T(8,128)(2,1)S(1)}, bf16[32,32,128]{2,1,0:T(8,128)(2,1)}, u32[]{:S(2)}) %copy-start.15) | copy-done | bytes 262168
  36.0 0.8 copy-done.16
  36.8 0.8 copy-done.18
  37.6 0.9 %copy-done.25 = bf16[32,32,128]{2,1,0:T(8,128)(2,1)S(1)} copy-done((bf16[32,32,128]{2,1,0:T(8,128)(2,1)S(1)}, bf16[32,32,128]{2,1,0:T(8,128)(2,1)}, u32[]{:S(2)}) %copy-start.25) | copy-done | bytes 262168
  38.5 1.0 %shard_map.97 = (f32[128,1024]{1,0:T(8,128)S(1)}, f32[1,1024]{1,0:T(1,128)S(1)}, f32[4,128,1024]{2,1,0:T(8,128)S(1)}, f32[128,1024]{1,0:T(8,128)S(1)}, f32[128,1024]{1,0:T(8,128)S(1)}, /*index=5*/f32[128,1024]{1,0:T(8,128)S(1)}) custom-call(bf16[1024,128]{1,0:T(8,128)(2,1)S(1)} %bitcast.8, bf16[1024,128]{1,0:T(8,128)(2,1)S(1)} %bitcast.16, ...), custom_call_target="tpu_custom_call" | custom-call | flops 201326592 | bytes 4920832 | tf_op jit(solution)/shard_map/pallas_call | solution.py:321
  39.6 0.8 copy-done
  40.4 0.8 copy-done.4
  41.2 3.9 %all-to-all-done.1.recv_ref = bf16[16,16,512]{2,1,0:T(8,128)(2,1)S(1)} async-done(((bf16[16,16,512]{2,1,0:T(8,128)(2,1)}), bf16[16,16,512]{2,1,0:T(8,128)(2,1)S(1)}, u32[]{:S(2)}, u32[]{:S(2)}) %all-to-all-start.1) | async-done | bytes 262176 | tf_op jit(solution)/shard_map/all_to_all | solution.py:339
  45.4 0.8 copy-done.2
  46.2 13.3 %all_to_all.21.recv_ref = bf16[16,16,512]{2,1,0:T(8,128)(2,1)S(1)} all-to-all(bf16[16,16,512]{2,1,0:T(8,128)(2,1)S(1)} %get-tuple-element.21), channel_id=1, replica_groups=mesh['replica'=2,'row'=4,'col'=4] {'row','col'}, dimensions={0} | all-to-all | bytes 524288 | tf_op jit(solution)/shard_map/all_to_all | solution.py:339
  59.5 0.9 %copy-done.11 = bf16[8,128,128]{2,1,0:T(8,128)(2,1)S(1)} copy-done((bf16[8,128,128]{2,1,0:T(8,128)(2,1)S(1)}, bf16[8,128,128]{2,1,0:T(8,128)(2,1)}, u32[]{:S(2)}) %copy-start.11) | copy-done | bytes 262168
  60.4 0.9 %copy-done.13 = bf16[8,128,128]{2,1,0:T(8,128)(2,1)S(1)} copy-done((bf16[8,128,128]{2,1,0:T(8,128)(2,1)S(1)}, bf16[8,128,128]{2,1,0:T(8,128)(2,1)}, u32[]{:S(2)}) %copy-start.13) | copy-done | bytes 262168
  61.4 2.4 %shard_map.100 = bf16[16,16,1024]{2,1,0:T(8,128)(2,1)} custom-call(bf16[16,16,512]{2,1,0:T(8,128)(2,1)S(1)} %all_to_all.21.recv_ref, bf16[8,128,128]{2,1,0:T(8,128)(2,1)S(1)} %copy-done.11, bf16[8,128,128]{2,1,0:T(8,128)(2,1)S(1)} %copy-done.13), custom_call_target="tpu_custom_call" | custom-call | flops 67108864 | bytes 1310720 | tf_op jit(solution)/shard_map/pallas_call | solution.py:321
  63.8 3.6 %all-to-all-start.3 = ((bf16[16,16,1024]{2,1,0:T(8,128)(2,1)}), bf16[16,16,1024]{2,1,0:T(8,128)(2,1)S(1)}, u32[]{:S(2)}, u32[]{:S(2)}) async-start(bf16[16,16,1024]{2,1,0:T(8,128)(2,1)} %shard_map.100), calls=%async_computation.3 | async-start | bytes 1048576 | tf_op jit(solution)/shard_map/all_to_all | solution.py:339
  67.4 1.0 %copy-done.1 = f32[128,1024]{1,0:T(8,128)S(1)} copy-done((f32[128,1024]{1,0:T(8,128)S(1)}, f32[128,1024]{1,0:T(8,128)}, u32[]{:S(2)}) %copy-start.1) | copy-done | bytes 524312
  68.5 1.0 %copy-done.3 = f32[128,1024]{1,0:T(8,128)S(1)} copy-done((f32[128,1024]{1,0:T(8,128)S(1)}, f32[128,1024]{1,0:T(8,128)}, u32[]{:S(2)}) %copy-start.3) | copy-done | bytes 524312
  69.5 1.1 %shard_map.99 = (bf16[1024,128]{1,0:T(8,128)(2,1)}, f32[128,1024]{1,0:T(8,128)S(1)}) custom-call(f32[128,1024]{1,0:T(8,128)S(1)} %copy-done.3, f32[128,1024]{1,0:T(8,128)S(1)} %get-tuple-element.18.gate_ref, f32[128,1024]{1,0:T(8,128)S(1)} %copy-done.1, f32[1,128]{1,0:T(1,128)S(1)} %bitcast.15, bf16[128,128]{1,0:T(8,128)(2,1)S(1)} %copy-done.19, ...), custom_call_target="tpu_custom_call" | custom-call | flops 67108864 | bytes 2425344 | tf_op jit(solution)/shard_map/pallas_call | solution.py:321
  70.6 0.8 copy-done.6
  71.4 11.6 %all-to-all-done.3.recv_ref = bf16[16,16,1024]{2,1,0:T(8,128)(2,1)S(1)} async-done(((bf16[16,16,1024]{2,1,0:T(8,128)(2,1)}), bf16[16,16,1024]{2,1,0:T(8,128)(2,1)S(1)}, u32[]{:S(2)}, u32[]{:S(2)}) %all-to-all-start.3) | async-done | bytes 524320 | tf_op jit(solution)/shard_map/all_to_all | solution.py:339
  83.0 1.0 %copy-done.5 = f32[128,1024]{1,0:T(8,128)S(1)} copy-done((f32[128,1024]{1,0:T(8,128)S(1)}, f32[128,1024]{1,0:T(8,128)}, u32[]{:S(2)}) %copy-start.5) | copy-done | bytes 524312
  84.1 1.0 %copy-done.7 = f32[128,1024]{1,0:T(8,128)S(1)} copy-done((f32[128,1024]{1,0:T(8,128)S(1)}, f32[128,1024]{1,0:T(8,128)}, u32[]{:S(2)}) %copy-start.7) | copy-done | bytes 524312
  85.1 1.4 %shard_map.101 = f32[1024,128]{1,0:T(8,128)} custom-call(bf16[16,16,1024]{2,1,0:T(8,128)(2,1)S(1)} %all-to-all-done.3.recv_ref, f32[4,128,1024]{2,1,0:T(8,128)S(1)} %get-tuple-element.24.factor_ref, f32[128,1024]{1,0:T(8,128)S(1)} %copy-done.7, f32[128,1024]{1,0:T(8,128)S(1)} %copy-done.5, f32[1,1024]{1,0:T(1,128)S(1)} %get-tuple-element.27.inv_ref, ...), custom_call_target="tpu_custom_call" | custom-call | flops 134217728 | bytes 4329984 | tf_op jit(solution)/shard_map/pallas_call | solution.py:321
  (33 shorter events, 0.3 us)
Async XLA Ops:
  0.6 34.4 %copy-start.21 = (f32[128]{0:T(128)S(1)}, f32[128]{0:T(128)}, u32[]{:S(2)}) copy-start(f32[128]{0:T(128)} %param.11) | copy-start | bytes 1540
  0.6 34.4 %copy-start.23 = (s32[128]{0:T(128)S(1)}, s32[128]{0:T(128)}, u32[]{:S(2)}) copy-start(s32[128]{0:T(128)} %param.10) | copy-start | bytes 1540
  0.7 34.4 %copy-start.24 = (f32[128]{0:T(128)S(1)}, f32[128]{0:T(128)}, u32[]{:S(2)}) copy-start(f32[128]{0:T(128)} %param.14) | copy-start | bytes 1540
  0.7 0.9 %copy-start.8 = (bf16[128,512]{1,0:T(8,128)(2,1)S(1)}, bf16[128,512]{1,0:T(8,128)(2,1)}, u32[]{:S(2)}) copy-start(bf16[128,512]{1,0:T(8,128)(2,1)} %proj_ref.5) | copy-start | bytes 393220
  1.6 0.9 %copy-start.14 = (bf16[32,32,128]{2,1,0:T(8,128)(2,1)S(1)}, bf16[32,32,128]{2,1,0:T(8,128)(2,1)}, u32[]{:S(2)}) copy-start(bf16[32,32,128]{2,1,0:T(8,128)(2,1)} %param.8) | copy-start | bytes 786436
  2.5 0.7 copy-start.20
  3.2 0.7 copy-start.22
  3.8 31.2 %copy-start.9 = (bf16[128,512]{1,0:T(8,128)(2,1)S(1)}, bf16[128,512]{1,0:T(8,128)(2,1)}, u32[]{:S(2)}) copy-start(bf16[128,512]{1,0:T(8,128)(2,1)} %proj_ref.5) | copy-start | bytes 393220
  30.1 0.7 copy-start.10
  30.8 0.7 copy-start.12
  31.5 13.6 %all-to-all-start.1 = ((bf16[16,16,512]{2,1,0:T(8,128)(2,1)}), bf16[16,16,512]{2,1,0:T(8,128)(2,1)S(1)}, u32[]{:S(2)}, u32[]{:S(2)}) async-start(bf16[16,16,512]{2,1,0:T(8,128)(2,1)} %get-tuple-element.15), calls=%async_computation.1 | async-start | bytes 524288 | tf_op jit(solution)/shard_map/all_to_all | solution.py:339
  35.1 1.0 %copy-start.15 = (bf16[32,32,128]{2,1,0:T(8,128)(2,1)S(1)}, bf16[32,32,128]{2,1,0:T(8,128)(2,1)}, u32[]{:S(2)}) copy-start(bf16[32,32,128]{2,1,0:T(8,128)(2,1)} %param.8) | copy-start | bytes 786436
  36.0 0.8 copy-start.16
  36.8 0.8 copy-start.18
  37.6 0.9 %copy-start.25 = (bf16[32,32,128]{2,1,0:T(8,128)(2,1)S(1)}, bf16[32,32,128]{2,1,0:T(8,128)(2,1)}, u32[]{:S(2)}) copy-start(bf16[32,32,128]{2,1,0:T(8,128)(2,1)} %param.9) | copy-start | bytes 786436
  39.6 0.8 copy-start
  40.4 0.8 copy-start.4
  45.4 0.8 copy-start.2
  46.2 21.2 %copy-start.17 = (bf16[128,128]{1,0:T(8,128)(2,1)S(1)}, bf16[128,128]{1,0:T(8,128)(2,1)}, u32[]{:S(2)}) copy-start(bf16[128,128]{1,0:T(8,128)(2,1)} %gate_w_ref.3) | copy-start | bytes 98308
  46.2 21.2 %copy-start.19 = (bf16[128,128]{1,0:T(8,128)(2,1)S(1)}, bf16[128,128]{1,0:T(8,128)(2,1)}, u32[]{:S(2)}) copy-start(bf16[128,128]{1,0:T(8,128)(2,1)} %out_w_ref.3) | copy-start | bytes 98308
  59.5 1.0 %copy-start.11 = (bf16[8,128,128]{2,1,0:T(8,128)(2,1)S(1)}, bf16[8,128,128]{2,1,0:T(8,128)(2,1)}, u32[]{:S(2)}) copy-start(bf16[8,128,128]{2,1,0:T(8,128)(2,1)} %copy-done.10) | copy-start | bytes 786436
  60.4 0.9 %copy-start.13 = (bf16[8,128,128]{2,1,0:T(8,128)(2,1)S(1)}, bf16[8,128,128]{2,1,0:T(8,128)(2,1)}, u32[]{:S(2)}) copy-start(bf16[8,128,128]{2,1,0:T(8,128)(2,1)} %copy-done.12) | copy-start | bytes 786436
  63.8 19.2 %all-to-all-start.3 = ((bf16[16,16,1024]{2,1,0:T(8,128)(2,1)}), bf16[16,16,1024]{2,1,0:T(8,128)(2,1)S(1)}, u32[]{:S(2)}, u32[]{:S(2)}) async-start(bf16[16,16,1024]{2,1,0:T(8,128)(2,1)} %shard_map.100), calls=%async_computation.3 | async-start | bytes 1048576 | tf_op jit(solution)/shard_map/all_to_all | solution.py:339
  67.4 1.0 %copy-start.1 = (f32[128,1024]{1,0:T(8,128)S(1)}, f32[128,1024]{1,0:T(8,128)}, u32[]{:S(2)}) copy-start(f32[128,1024]{1,0:T(8,128)} %copy-done) | copy-start | bytes 1572868
  68.4 1.0 %copy-start.3 = (f32[128,1024]{1,0:T(8,128)S(1)}, f32[128,1024]{1,0:T(8,128)}, u32[]{:S(2)}) copy-start(f32[128,1024]{1,0:T(8,128)} %copy-done.2) | copy-start | bytes 1572868
  70.6 0.8 copy-start.6
  83.0 1.0 %copy-start.5 = (f32[128,1024]{1,0:T(8,128)S(1)}, f32[128,1024]{1,0:T(8,128)}, u32[]{:S(2)}) copy-start(f32[128,1024]{1,0:T(8,128)} %copy-done.4) | copy-start | bytes 1572868
  84.1 1.0 %copy-start.7 = (f32[128,1024]{1,0:T(8,128)S(1)}, f32[128,1024]{1,0:T(8,128)}, u32[]{:S(2)}) copy-start(f32[128,1024]{1,0:T(8,128)} %copy-done.6) | copy-start | bytes 1572868

commit v2 on v1

v2 whole, which is shorter than its diff:
```python
import functools

import jax
import jax.numpy as jnp
from jax import lax
from jax.experimental import pallas as pl
from jax.experimental.pallas import tpu as pltpu
from jax.sharding import PartitionSpec as P

eps_norm = 1e-05


def layer_norm(values, gain):
    mean_val = jnp.mean(values, axis=-1, keepdims=True)
    centred = values - mean_val
    inv_std = lax.rsqrt(jnp.mean(centred * centred, axis=-1, keepdims=True) + eps_norm)
    unit = centred * inv_std
    return (unit * gain, unit, inv_std)


def norm_back(grad_unit, unit, inv_std):
    first = jnp.mean(grad_unit, axis=-1, keepdims=True)
    second = jnp.mean(grad_unit * unit, axis=-1, keepdims=True)
    return inv_std * (grad_unit - first - unit * second)


def on_device(pair, cotangent, valid, in_gain, proj_weight, gate_weight, out_gain, out_weight):
    tile_rows = pair.shape[0]
    channels = pair.shape[2]
    hidden = out_weight.shape[0]
    cells = tile_rows * tile_rows
    keeper = valid.astype(jnp.float32)
    row_keep = lax.dynamic_slice_in_dim(keeper, lax.axis_index("row") * tile_rows, tile_rows)
    col_keep = lax.dynamic_slice_in_dim(keeper, lax.axis_index("col") * tile_rows, tile_rows)
    pair_keep = (row_keep[:, None] * col_keep[None, :])[:, :, None]
    normed_f, unit_in, inv_in = layer_norm(pair.astype(jnp.float32), in_gain)
    normed = normed_f.astype(jnp.bfloat16)
    flat = normed.reshape(cells, channels)
    proj = jnp.dot(flat, proj_weight, preferred_element_type=jnp.float32).reshape(
        tile_rows, tile_rows, 4 * hidden
    )
    left_sig = jax.nn.sigmoid(proj[..., :hidden])
    left_val = proj[..., hidden : 2 * hidden]
    right_sig = jax.nn.sigmoid(proj[..., 2 * hidden : 3 * hidden])
    right_val = proj[..., 3 * hidden :]
    left = (left_sig * left_val * pair_keep).astype(jnp.bfloat16)
    right = (right_sig * right_val * pair_keep).astype(jnp.bfloat16)
    panel = lax.all_gather(right, "row", axis=0, tiled=True)
    piece = panel
    tri = jnp.swapaxes(
        lax.psum_scatter(
            jnp.einsum("ikh,jkh->jih", left, piece, preferred_element_type=jnp.float32),
            "col",
            scatter_dimension=0,
            tiled=True,
        ),
        0,
        1,
    )
    tnorm_f, unit_tri, inv_tri = layer_norm(tri, out_gain)
    tnorm = tnorm_f.astype(jnp.bfloat16)
    gate = jax.nn.sigmoid(jnp.dot(flat, gate_weight, preferred_element_type=jnp.float32)).reshape(
        tile_rows, tile_rows, channels
    )
    lin = jnp.dot(
        tnorm.reshape(cells, hidden), out_weight, preferred_element_type=jnp.float32
    ).reshape(tile_rows, tile_rows, channels)
    update = (gate * lin).astype(jnp.bfloat16)
    cot = cotangent.astype(jnp.float32)
    d_lin = (cot * gate).astype(jnp.bfloat16)
    d_gpre = (cot * lin * gate * (1.0 - gate)).astype(jnp.bfloat16)
    d_tnorm = jnp.dot(
        d_lin.reshape(cells, channels), out_weight.T, preferred_element_type=jnp.float32
    ).reshape(tile_rows, tile_rows, hidden)
    d_tri = norm_back(d_tnorm * out_gain, unit_tri, inv_tri).astype(jnp.bfloat16)
    grad_rows = lax.all_gather(d_tri, "col", axis=1, tiled=True)
    back_panel = lax.all_gather(right, "row", axis=0, tiled=True)
    piece = grad_rows
    d_right = lax.psum_scatter(
        jnp.einsum("ijh,ikh->jkh", piece, left, preferred_element_type=jnp.float32),
        "row",
        scatter_dimension=0,
        tiled=True,
    )
    d_left = jnp.einsum("ijh,jkh->ikh", grad_rows, back_panel, preferred_element_type=jnp.float32)
    d_proj = jnp.concatenate(
        [
            d_left * pair_keep * left_val * left_sig * (1.0 - left_sig),
            d_left * pair_keep * left_sig,
            d_right * pair_keep * right_val * right_sig * (1.0 - right_sig),
            d_right * pair_keep * right_sig,
        ],
        axis=-1,
    ).astype(jnp.bfloat16)
    d_normed = jnp.dot(
        d_proj.reshape(cells, 4 * hidden), proj_weight.T, preferred_element_type=jnp.float32
    )
    d_normed = d_normed + jnp.dot(
        d_gpre.reshape(cells, channels), gate_weight.T, preferred_element_type=jnp.float32
    )
    pair_grad = norm_back(
        d_normed.reshape(tile_rows, tile_rows, channels) * in_gain, unit_in, inv_in
    )
    return (update, pair_grad)


F32 = jnp.float32
BF16 = jnp.bfloat16
LANES = 128


def dot(a, b, dims):
    return lax.dot_general(a, b, ((dims[:1], dims[1:]), ((), ())), preferred_element_type=F32)


def column(gain):
    n = gain.shape[1]
    return jnp.broadcast_to(gain, (n, n)).T


def spread(col, width):
    return jnp.concatenate([col] * (width // col.shape[1]), axis=1)


def unit_rows(values):
    n = values.shape[0]
    centred = values - jnp.sum(values, axis=0, keepdims=True) * (1.0 / n)
    inv = lax.rsqrt(jnp.sum(centred * centred, axis=0, keepdims=True) * (1.0 / n) + eps_norm)
    return centred * inv, inv


def unit_back(q, unit, inv):
    n = q.shape[0]
    first = jnp.sum(q, axis=0, keepdims=True) * (1.0 / n)
    second = jnp.sum(q * unit, axis=0, keepdims=True) * (1.0 / n)
    return inv * (q - first - unit * second)


def block_swap():
    size, width = 4 * LANES, LANES // 4
    row = lax.broadcasted_iota(jnp.int32, (size, LANES), 0)
    col = lax.broadcasted_iota(jnp.int32, (size, LANES), 1)
    target = (row // width % 4) * LANES + (row // LANES) * width + row % width - col
    return jnp.concatenate([(target == n * LANES).astype(F32) for n in range(4)], axis=1).astype(BF16)


def keep_row(valid, tile, cells):
    n = valid.ref.shape[1]
    token = lax.broadcasted_iota(jnp.int32, (n, cells), 0)
    cell = lax.broadcasted_iota(jnp.int32, (n, cells), 1)
    first = (token == lax.axis_index("row") * tile + cell // tile).astype(F32).astype(BF16)
    second = (token == lax.axis_index("col") * tile + cell % tile).astype(F32).astype(BF16)
    v = jnp.broadcast_to(valid.ready()[...].astype(F32), (8, n)).astype(BF16)
    return (dot(v, first, (1, 0)) * dot(v, second, (1, 0)))[:1]


def normed_of(pair, in_gain):
    unit, inv = unit_rows(pair.ready()[...].astype(F32).T)
    normed = (unit * spread(column(in_gain.ready()[...]), unit.shape[1])).astype(BF16)
    return normed, unit, inv


def project_kernel(tile, pair, valid, in_gain, proj_weight, out_ref):
    hidden = proj_weight.ref.shape[1] // 4
    shards, both, cells = out_ref.shape
    normed, _, _ = normed_of(pair, in_gain)
    keep = keep_row(valid, tile, cells)
    weights = proj_weight.ready()
    sides = []
    for side in range(2):
        weight = weights[:, 2 * hidden * side : 2 * hidden * (side + 1)].T
        proj = dot(weight, normed, (1, 0))
        sides.append(jax.nn.sigmoid(proj[:hidden]) * proj[hidden:] * keep)
    for s in range(shards):
        rows = slice(s * both // 2, (s + 1) * both // 2)
        out_ref[s] = jnp.concatenate([sides[0][rows], sides[1][rows]], axis=0).astype(BF16)


def gate_of(normed, cot, gate_weight):
    gate = jax.nn.sigmoid(dot(gate_weight.ready()[...].T, normed, (1, 0)))
    return gate, cot.ready()[...].astype(F32).T


def gate_kernel(pair, cot, in_gain, gate_weight, out_gain, out_weight, q_ref):
    normed, _, _ = normed_of(pair, in_gain)
    gate, cot_rows = gate_of(normed, cot, gate_weight)
    q = dot(out_weight.ready()[...], (cot_rows * gate).astype(BF16), (1, 0))
    q_ref[...] = q * spread(column(out_gain.ready()[...]), q.shape[1])


def tri_kernel(grid_rows, recv_ref, out_ref, left, right, rows, tri):
    devices, both, cells = recv_ref.shape
    per = both // 2
    n = left.ref.shape[1]
    tile = n // grid_rows
    groups = cells // LANES
    swap = block_swap()
    for r in range(grid_rows):
        x = jnp.concatenate(
            [
                jnp.concatenate(
                    [recv_ref[grid_rows * r + c, :, g * LANES : (g + 1) * LANES] for c in range(grid_rows)], axis=1
                )
                for g in range(groups)
            ],
            axis=0,
        )
        y = dot(x, swap, (1, 0))
        for g in range(groups):
            for p in range(grid_rows):
                at = (r * tile + g * grid_rows + p) * both
                rows[at : at + both, :] = y[g * both : (g + 1) * both, p * LANES : (p + 1) * LANES]
    for h in range(per):
        left.ref[h] = rows[pl.ds(h, n, stride=both), :].astype(BF16)
        right.ref[h] = rows[pl.ds(per + h, n, stride=both), :].astype(BF16)
    left.send()
    right.send()
    for h in range(per):
        tri[pl.ds(h, n, stride=per), :] = dot(left.ref[h], right.ref[h], (1, 1))
    half = groups // 2
    for r in range(grid_rows):
        x = jnp.concatenate(
            [
                jnp.concatenate(
                    [
                        tri[at : at + per, :]
                        for p in range(grid_rows)
                        for at in [(r * tile + (g + k * half) * grid_rows + p) * per]
                    ],
                    axis=1,
                )
                for g in range(half)
                for k in range(2)
            ],
            axis=0,
        )
        y = dot(x.astype(BF16), swap, (1, 0)).astype(BF16)
        for g in range(half):
            for c in range(grid_rows):
                out_ref[grid_rows * r + c, :, g * LANES : (g + 1) * LANES] = y[
                    g * both : (g + 1) * both, c * LANES : (c + 1) * LANES
                ]


def halves_of(recv_ref):
    shards, both, width = recv_ref.shape
    x = recv_ref[...].astype(F32)
    rows = shards * both // 2
    return jnp.concatenate(
        [x[:, : both // 2].reshape(rows, width), x[:, both // 2 :].reshape(rows, width)], axis=1
    )


def d_tri_kernel(recv_ref, q_ref, out_ref):
    shards, both, width = recv_ref.shape
    unit, inv = unit_rows(halves_of(recv_ref))
    d_tri = unit_back(q_ref[...], unit, inv)
    out_ref[...] = jnp.concatenate(
        [d_tri[:, :width].reshape(shards, both // 2, width), d_tri[:, width:].reshape(shards, both // 2, width)],
        axis=1,
    ).astype(BF16)


def update_kernel(
    tile, tri, out_gain, out_weight, pair, cot, valid, in_gain, gate_weight, proj_weight,
    unit_ref, inv_ref, factor_ref, update,
):
    normed, unit, inv = normed_of(pair, in_gain)
    unit_ref[...] = unit
    inv_ref[...] = inv
    gate, cot_rows = gate_of(normed, cot, gate_weight)
    unit_tri, _ = unit_rows(halves_of(tri.ready()))
    tnorm = (unit_tri * spread(column(out_gain.ready()[...]), unit.shape[1])).astype(BF16)
    lin = dot(out_weight.ready()[...].T, tnorm, (1, 0))
    update.ref[...] = (gate * lin).T.astype(BF16)
    update.send()
    factor_ref[4] = (cot_rows * lin * gate * (1.0 - gate)).astype(BF16)
    hidden = proj_weight.ref.shape[1] // 4
    keep = keep_row(valid, tile, unit.shape[1])
    weights = proj_weight.ready()
    for side in range(2):
        weight = weights[:, 2 * hidden * side : 2 * hidden * (side + 1)].T
        proj = dot(weight, normed, (1, 0))
        sig = jax.nn.sigmoid(proj[:hidden])
        factor_ref[2 * side] = (keep * proj[hidden:] * sig * (1.0 - sig)).astype(BF16)
        factor_ref[2 * side + 1] = (keep * sig).astype(BF16)


def sides_kernel(grid_rows, recv_ref, left, right, out_ref, d_tri, rows):
    devices, both, cells = out_ref.shape
    per = both // 2
    n = left.ref.shape[1]
    tile = n // grid_rows
    groups = cells // LANES
    half = groups // 2
    swap = block_swap()
    for r in range(grid_rows):
        x = jnp.concatenate(
            [
                jnp.concatenate(
                    [recv_ref[grid_rows * r + c, :, g * LANES : (g + 1) * LANES] for c in range(grid_rows)], axis=1
                )
                for g in range(half)
            ],
            axis=0,
        )
        y = dot(x, swap, (1, 0))
        for g in range(half):
            for k in range(2):
                for p in range(grid_rows):
                    at = (r * tile + (g + k * half) * grid_rows + p) * per
                    d_tri[at : at + per, :] = y[
                        g * both + k * per : g * both + (k + 1) * per, p * LANES : (p + 1) * LANES
                    ]
    left_ref, right_ref = left.ready(), right.ready()
    for h in range(per):
        grad = d_tri[pl.ds(h, n, stride=per), :].astype(BF16)
        rows[pl.ds(h, n, stride=both), :] = dot(grad, right_ref[h], (1, 0))
        rows[pl.ds(per + h, n, stride=both), :] = dot(grad, left_ref[h], (0, 0))
    for r in range(grid_rows):
        x = jnp.concatenate(
            [
                jnp.concatenate(
                    [
                        rows[at : at + both, :]
                        for p in range(grid_rows)
                        for at in [(r * tile + g * grid_rows + p) * both]
                    ],
                    axis=1,
                )
                for g in range(groups)
            ],
            axis=0,
        )
        y = dot(x.astype(BF16), swap, (1, 0)).astype(BF16)
        for g in range(groups):
            for c in range(grid_rows):
                out_ref[grid_rows * r + c, :, g * LANES : (g + 1) * LANES] = y[
                    g * both : (g + 1) * both, c * LANES : (c + 1) * LANES
                ]


def pair_grad_kernel(recv_ref, factor_ref, unit_ref, inv_ref, in_gain, proj_weight, gate_weight, out):
    shards, both, cells = recv_ref.shape
    hidden = shards * both // 2
    x = recv_ref[...].astype(F32)
    d_left = x[:, : both // 2].reshape(hidden, cells)
    d_right = x[:, both // 2 :].reshape(hidden, cells)
    d_proj = jnp.concatenate(
        [(grad * factor_ref[2 * side + part].astype(F32)).astype(BF16) for side, grad in enumerate((d_left, d_right)) for part in range(2)],
        axis=0,
    )
    d_normed = dot(proj_weight.ready()[...], d_proj, (1, 0))
    d_normed = d_normed + dot(gate_weight.ready()[...], factor_ref[4], (1, 0))
    q = d_normed * spread(column(in_gain.ready()[...]), cells)
    out.ref[...] = unit_back(q, unit_ref[...], inv_ref[...]).T
    out.send()


class Arriving:
    def __init__(self, source, ref, sem):
        self.ref, self.copy = ref, pltpu.make_async_copy(source, ref, sem)
        self.copy.start()

    def ready(self):
        if self.copy is not None:
            self.copy.wait()
            self.copy = None
        return self.ref


class Leaving:
    def __init__(self, target, ref, sem):
        self.ref, self.copy = ref, pltpu.make_async_copy(ref, target, sem)

    def send(self):
        self.copy.start()


def call(kernel, outs, args, flops, scratch=(), far=(), far_outs=(), room=24):
    outs, args, far, far_outs, scratch = (list(x) for x in (outs, args, far, far_outs, scratch))
    counts = [len(args), len(far), len(outs), len(far_outs), len(far), len(far_outs), len(scratch)]

    def body(*refs):
        parts, at = [], 0
        for count in counts:
            parts.append(list(refs[at : at + count]))
            at += count
        near_in, far_in, near_out, far_out, held, leaving, rest = parts
        sems = refs[at]
        arrivals = [Arriving(a, b, sems.at[i]) for i, (a, b) in enumerate(zip(far_in, held))]
        departures = [
            Leaving(a, b, sems.at[len(held) + i]) for i, (a, b) in enumerate(zip(far_out, leaving))
        ]
        kernel(*near_in, *arrivals, *near_out, *departures, *rest)
        for one in arrivals:
            one.ready()
        for one in departures:
            one.copy.wait()

    near_spec, far_spec = pl.BlockSpec(memory_space=pltpu.VMEM), pl.BlockSpec(memory_space=pltpu.HBM)
    moved = sum(a.size * a.dtype.itemsize for a in args + far + outs + far_outs)
    return pl.pallas_call(
        body,
        out_shape=tuple(outs + far_outs),
        in_specs=[near_spec] * len(args) + [far_spec] * len(far),
        out_specs=tuple([near_spec] * len(outs) + [far_spec] * len(far_outs)),
        scratch_shapes=[pltpu.VMEM(a.shape, a.dtype) for a in far + far_outs]
        + scratch
        + [pltpu.SemaphoreType.DMA((max(1, len(far) + len(far_outs)),))],
        compiler_params=pltpu.CompilerParams(vmem_limit_bytes=int(room * 2**20)),
        cost_estimate=pl.CostEstimate(flops=flops, bytes_accessed=moved, transcendentals=0),
    )(*args, *far)


def by_channel(pair, cotangent, valid, in_gain, proj_weight, gate_weight, out_gain, out_weight):
    tile, _, channels = pair.shape
    hidden = out_weight.shape[0]
    cells = tile * tile
    grid_rows = lax.axis_size("row")
    devices = grid_rows * lax.axis_size("col")
    per = hidden // devices
    n = tile * grid_rows
    shape = lambda dims, dtype: jax.ShapeDtypeStruct(dims, dtype)
    whole = lambda x: lax.all_to_all(x, ("row", "col"), 0, 0, tiled=True)
    flat = pair.reshape(cells, channels)
    flat_cot = cotangent.reshape(cells, channels)
    valid_row = valid.reshape(1, -1)
    in_row = in_gain.reshape(1, -1)
    out_row = out_gain.reshape(1, -1)
    both = 2 * per
    plane = shape((channels, cells), F32)

    (sides,) = call(
        functools.partial(project_kernel, tile),
        [shape((devices, both, cells), BF16)],
        (),
        2 * cells * channels * 4 * hidden,
        far=(flat, valid_row, in_row, proj_weight),
        room=62,
    )
    sides = whole(sides)
    tri, left, right = call(
        functools.partial(tri_kernel, grid_rows),
        [shape((devices, both, cells // 2), BF16)],
        (sides,),
        2 * per * n * n * n,
        [pltpu.VMEM((n * both, n), F32), pltpu.VMEM((n * per, n), F32)],
        far_outs=[shape((per, n, n), BF16)] * 2,
    )
    tri, flat_2, flat_cot_2 = lax.optimization_barrier((tri, flat, flat_cot))
    tri = whole(tri)
    (q,) = call(
        gate_kernel,
        [plane],
        (),
        2 * cells * channels * 2 * hidden,
        far=(flat_2, flat_cot_2, in_row, gate_weight, out_row, out_weight),
    )
    (d_tri,) = call(
        d_tri_kernel,
        [shape((devices, both, cells // 2), BF16)],
        (tri, q),
        20 * cells * hidden,
    )
    d_tri = whole(d_tri)
    (d_sides,) = call(
        functools.partial(sides_kernel, grid_rows),
        [shape((devices, both, cells), BF16)],
        (d_tri,),
        4 * per * n * n * n,
        [pltpu.VMEM((n * per, n), F32), pltpu.VMEM((n * both, n), F32)],
        far=(left, right),
    )
    d_sides, flat_4, flat_cot_4, tri = lax.optimization_barrier((d_sides, flat, flat_cot, tri))
    d_sides = whole(d_sides)
    unit, inv, factors, update = call(
        functools.partial(update_kernel, tile),
        [plane, shape((1, cells), F32), shape((5, hidden, cells), BF16)],
        (),
        2 * cells * channels * 6 * hidden,
        far=(tri, out_row, out_weight, flat_4, flat_cot_4, valid_row, in_row, gate_weight, proj_weight),
        far_outs=[shape((cells, channels), BF16)],
    )
    (pair_grad,) = call(
        pair_grad_kernel,
        [],
        (d_sides, factors, unit, inv),
        2 * cells * channels * 5 * hidden,
        far=(in_row, proj_weight, gate_weight),
        far_outs=[shape((cells, channels), F32)],
    )
    return (update.reshape(pair.shape), pair_grad.reshape(pair.shape))


def fits(pair, out_weight):
    rows, cols = lax.axis_size("row"), lax.axis_size("col")
    tile, tile_cols, channels = pair.shape
    hidden = out_weight.shape[0]
    return (
        rows == cols == 4
        and tile == tile_cols
        and tile * rows == LANES
        and channels == LANES
        and hidden == 8 * rows * cols
    )


def step(pair, cotangent, valid, in_gain, proj_weight, gate_weight, out_gain, out_weight):
    plan = by_channel if fits(pair, out_weight) else on_device
    return plan(pair, cotangent, valid, in_gain, proj_weight, gate_weight, out_gain, out_weight)


def solution(mesh):
    placed = (
        P(("replica", "row"), "col", None),
        P(("replica", "row"), "col", None),
        P("replica"),
        P(),
        P(),
        P(),
        P(),
        P(),
    )
    return jax.shard_map(
        step,
        mesh=mesh,
        in_specs=placed,
        out_specs=(P(("replica", "row"), "col", None), P(("replica", "row"), "col", None)),
        check_vma=False,
    )
```

time: 87.4 us -> 80.2 us (0.918)
  local copies, waits for them, and re-layouts: 17.2 us -> 0.03 us
  waiting for transfers between devices: 15.5 us -> 21.6 us
  Pallas kernels: 9.64 us -> 13.9 us
    unnamed x52 -> x16, local copies, waits for them, and re-layouts: 17.2 us -> 0.03 us
    all_to_all x2, waiting for transfers between devices: 15.5 us -> 21.6 us  [by_channel(): whole = lambda x: lax.all_to_all(x, ('row', 'col'), 0, 0, tiled=True)]
    pallas_call x7, Pallas kernels: 9.64 us -> 13.9 us  [call(): pl.pallas_call(body, out_shape=tuple(outs + far_outs), in_specs=[near_spe...]
  transfers between devices with their start and end apart: 2 -> 2, of which waited for: 2 -> 2; matrix products, arithmetic and copies ran while one was open for 0% -> 0% of each run, Pallas kernels for 3% -> 5%
where the time goes in v2:
time: 80.2 us; the launch traced here: 79.8 us
  blocking collectives  36.3 us (45%)
  waiting for transfers between devices  21.6 us (27%)
  Pallas kernels  13.9 us (17%)
  starting transfers between devices  7.13 us (9%)
  between operations  0.81 us (1%)
    all_to_all x2, blocking collectives, by_channel(): whole = lambda x: lax.all_to_all(x, ('row', 'col'), 0, 0, tiled=True)  36.3 us
    all_to_all x2, waiting for transfers between devices, by_channel(): whole = lambda x: lax.all_to_all(x, ('row', 'col'), 0, 0, tiled=True)  21.6 us
    pallas_call x7, Pallas kernels, call(): pl.pallas_call(body, out_shape=tuple(outs + far_outs), in_specs=[near_spe...  13.9 us
    all_to_all x2, starting transfers between devices, by_channel(): whole = lambda x: lax.all_to_all(x, ('row', 'col'), 0, 0, tiled=True)  7.13 us
  transfers between devices with their start and end apart: 2, of which 2 were waited for; matrix products, arithmetic and copies ran while one was open for 0% of the time, Pallas kernels for 5%

profile of v2, /device:TPU:0, one launch (start us, length us, event | category | flops | bytes accessed | tf_op | source)
XLA Modules:
  0.0 79.8 jit_solution(1436311756018379511)
XLA Ops:
  0.6 0.0 copy-start
  0.6 0.0 copy-start.2
  0.7 0.0 copy-start.3
  0.7 0.0 copy-start.4
  0.7 0.0 copy-start.5
  0.7 0.0 copy-start.6
  0.7 2.9 %shard_map.95 = bf16[16,16,1024]{2,1,0:T(8,128)(2,1)} custom-call(bf16[1024,128]{1,0:T(8,128)(2,1)} %bitcast.7, s32[1,128]{1,0:T(1,128)} %bitcast.18, f32[1,128]{1,0:T(1,128)} %bitcast.12, bf16[128,512]{1,0:T(8,128)(2,1)} %refs_5_.3), custom_call_target="tpu_custom_call" | custom-call | flops 134217728 | bytes 918528 | tf_op jit(solution)/shard_map/pallas_call | solution.py:403
  3.6 23.1 %all_to_all.20.refs_0_ = bf16[16,16,1024]{2,1,0:T(8,128)(2,1)S(1)} all-to-all(bf16[16,16,1024]{2,1,0:T(8,128)(2,1)} %shard_map.95), channel_id=1, replica_groups=mesh['replica'=2,'row'=4,'col'=4] {'row','col'}, dimensions={0} | all-to-all | bytes 1048576 | tf_op jit(solution)/shard_map/all_to_all | solution.py:425
  26.7 2.2 %shard_map.96 = (bf16[16,16,512]{2,1,0:T(8,128)(2,1)}, bf16[8,128,128]{2,1,0:T(8,128)(2,1)S(1)}, bf16[8,128,128]{2,1,0:T(8,128)(2,1)S(1)}) custom-call(bf16[16,16,1024]{2,1,0:T(8,128)(2,1)S(1)} %all_to_all.20.refs_0_), custom_call_target="tpu_custom_call" | custom-call | flops 33554432 | bytes 1310720 | tf_op jit(solution)/shard_map/pallas_call | solution.py:403
  28.9 3.5 %all-to-all-start.1 = ((bf16[16,16,512]{2,1,0:T(8,128)(2,1)}), bf16[16,16,512]{2,1,0:T(8,128)(2,1)S(1)}, u32[]{:S(2)}, u32[]{:S(2)}) async-start(bf16[16,16,512]{2,1,0:T(8,128)(2,1)} %get-tuple-element.17), calls=%async_computation.1 | async-start | bytes 524288 | tf_op jit(solution)/shard_map/all_to_all | solution.py:425
  32.4 0.0 copy-done
  32.5 0.0 copy-done.2
  32.5 0.0 copy-done.3
  32.5 0.0 copy-done.4
  32.5 0.0 copy-done.5
  32.5 0.0 copy-done.6
  32.5 1.3 %shard_map.97.refs_1_ = f32[128,1024]{1,0:T(8,128)S(1)} custom-call(bf16[1024,128]{1,0:T(8,128)(2,1)S(1)} %bitcast.8, bf16[1024,128]{1,0:T(8,128)(2,1)S(1)} %bitcast.10, f32[1,128]{1,0:T(1,128)S(1)} %bitcast.13, bf16[128,128]{1,0:T(8,128)(2,1)S(1)} %copy-done.3, f32[1,128]{1,0:T(1,128)S(1)} %bitcast.16, bf16[128,128]{1,0:T(8,128)(2,1)S(1)} %copy-done.4), custom_call_target="tpu_custom_call" | custom-call | flops 67108864 | bytes 1115136 | tf_op jit(solution)/shard_map/pallas_call | solution.py:403
  33.8 8.7 %all-to-all-done.1.refs_0_ = bf16[16,16,512]{2,1,0:T(8,128)(2,1)S(1)} async-done(((bf16[16,16,512]{2,1,0:T(8,128)(2,1)}), bf16[16,16,512]{2,1,0:T(8,128)(2,1)S(1)}, u32[]{:S(2)}, u32[]{:S(2)}) %all-to-all-start.1) | async-done | bytes 262176 | tf_op jit(solution)/shard_map/all_to_all | solution.py:425
  42.5 0.4 shard_map.98
  42.8 13.2 %all_to_all.21.refs_0_ = bf16[16,16,512]{2,1,0:T(8,128)(2,1)S(1)} all-to-all(bf16[16,16,512]{2,1,0:T(8,128)(2,1)S(1)} %shard_map.98), channel_id=1, replica_groups=mesh['replica'=2,'row'=4,'col'=4] {'row','col'}, dimensions={0} | all-to-all | bytes 524288 | tf_op jit(solution)/shard_map/all_to_all | solution.py:425
  56.0 0.0 copy-start.1
  56.0 0.0 copy-start.7
  56.1 2.4 %shard_map.99 = bf16[16,16,1024]{2,1,0:T(8,128)(2,1)} custom-call(bf16[16,16,512]{2,1,0:T(8,128)(2,1)S(1)} %all_to_all.21.refs_0_, bf16[8,128,128]{2,1,0:T(8,128)(2,1)S(1)} %get-tuple-element.20.refs_1_, bf16[8,128,128]{2,1,0:T(8,128)(2,1)S(1)} %get-tuple-element.21.refs_2_), custom_call_target="tpu_custom_call" | custom-call | flops 67108864 | bytes 1310720 | tf_op jit(solution)/shard_map/pallas_call | solution.py:403
  58.5 3.6 %all-to-all-start.3 = ((bf16[16,16,1024]{2,1,0:T(8,128)(2,1)}), bf16[16,16,1024]{2,1,0:T(8,128)(2,1)S(1)}, u32[]{:S(2)}, u32[]{:S(2)}) async-start(bf16[16,16,1024]{2,1,0:T(8,128)(2,1)} %shard_map.99), calls=%async_computation.3 | async-start | bytes 1048576 | tf_op jit(solution)/shard_map/all_to_all | solution.py:425
  62.1 0.0 copy-done.1
  62.1 0.0 copy-done.7
  62.1 2.7 %shard_map.100 = (f32[128,1024]{1,0:T(8,128)S(1)}, f32[1,1024]{1,0:T(1,128)S(1)}, bf16[5,128,1024]{2,1,0:T(8,128)(2,1)S(1)}, bf16[1024,128]{1,0:T(8,128)(2,1)}) custom-call(bf16[16,16,512]{2,1,0:T(8,128)(2,1)S(1)} %all-to-all-done.1.refs_0_, f32[1,128]{1,0:T(1,128)S(1)} %bitcast.17, bf16[128,128]{1,0:T(8,128)(2,1)S(1)} %copy-done.4, ...), custom_call_target="tpu_custom_call" | custom-call | flops 201326592 | bytes 3085824 | tf_op jit(solution)/shard_map/pallas_call | solution.py:403
  64.8 12.9 %all-to-all-done.3.refs_0_ = bf16[16,16,1024]{2,1,0:T(8,128)(2,1)S(1)} async-done(((bf16[16,16,1024]{2,1,0:T(8,128)(2,1)}), bf16[16,16,1024]{2,1,0:T(8,128)(2,1)S(1)}, u32[]{:S(2)}, u32[]{:S(2)}) %all-to-all-start.3) | async-done | bytes 524320 | tf_op jit(solution)/shard_map/all_to_all | solution.py:425
  77.7 2.1 %shard_map.101 = f32[1024,128]{1,0:T(8,128)} custom-call(bf16[16,16,1024]{2,1,0:T(8,128)(2,1)S(1)} %all-to-all-done.3.refs_0_, bf16[5,128,1024]{2,1,0:T(8,128)(2,1)S(1)} %get-tuple-element.27.refs_1_, f32[128,1024]{1,0:T(8,128)S(1)} %get-tuple-element.28.refs_2_, f32[1,1024]{1,0:T(1,128)S(1)} %get-tuple-element.29.refs_3_, f32[1,128]{1,0:T(1,128)S(1)} %bitcast.15, ...), custom_call_target="tpu_custom_call" | custom-call | flops 167772160 | bytes 3052032 | tf_op jit(solution)/shard_map/pallas_call | solution.py:403
Async XLA Ops:
  0.6 31.8 %copy-start = (bf16[32,32,128]{2,1,0:T(8,128)(2,1)S(1)}, bf16[32,32,128]{2,1,0:T(8,128)(2,1)}, u32[]{:S(2)}) copy-start(bf16[32,32,128]{2,1,0:T(8,128)(2,1)} %param.8) | copy-start | bytes 786436
  0.6 31.8 %copy-start.2 = (bf16[32,32,128]{2,1,0:T(8,128)(2,1)S(1)}, bf16[32,32,128]{2,1,0:T(8,128)(2,1)}, u32[]{:S(2)}) copy-start(bf16[32,32,128]{2,1,0:T(8,128)(2,1)} %param.9) | copy-start | bytes 786436
  0.7 31.8 %copy-start.3 = (bf16[128,128]{1,0:T(8,128)(2,1)S(1)}, bf16[128,128]{1,0:T(8,128)(2,1)}, u32[]{:S(2)}) copy-start(bf16[128,128]{1,0:T(8,128)(2,1)} %refs_6_.1) | copy-start | bytes 98308
  0.7 31.8 %copy-start.4 = (bf16[128,128]{1,0:T(8,128)(2,1)S(1)}, bf16[128,128]{1,0:T(8,128)(2,1)}, u32[]{:S(2)}) copy-start(bf16[128,128]{1,0:T(8,128)(2,1)} %refs_2_.1) | copy-start | bytes 98308
  0.7 31.8 %copy-start.5 = (f32[128]{0:T(128)S(1)}, f32[128]{0:T(128)}, u32[]{:S(2)}) copy-start(f32[128]{0:T(128)} %param.11) | copy-start | bytes 1540
  0.7 31.8 %copy-start.6 = (f32[128]{0:T(128)S(1)}, f32[128]{0:T(128)}, u32[]{:S(2)}) copy-start(f32[128]{0:T(128)} %param.14) | copy-start | bytes 1540
  28.9 13.6 %all-to-all-start.1 = ((bf16[16,16,512]{2,1,0:T(8,128)(2,1)}), bf16[16,16,512]{2,1,0:T(8,128)(2,1)S(1)}, u32[]{:S(2)}, u32[]{:S(2)}) async-start(bf16[16,16,512]{2,1,0:T(8,128)(2,1)} %get-tuple-element.17), calls=%async_computation.1 | async-start | bytes 524288 | tf_op jit(solution)/shard_map/all_to_all | solution.py:425
  56.0 6.0 %copy-start.1 = (bf16[128,512]{1,0:T(8,128)(2,1)S(1)}, bf16[128,512]{1,0:T(8,128)(2,1)}, u32[]{:S(2)}) copy-start(bf16[128,512]{1,0:T(8,128)(2,1)} %refs_5_.3) | copy-start | bytes 393220
  56.0 6.0 %copy-start.7 = (s32[128]{0:T(128)S(1)}, s32[128]{0:T(128)}, u32[]{:S(2)}) copy-start(s32[128]{0:T(128)} %param.10) | copy-start | bytes 1540
  58.5 19.2 %all-to-all-start.3 = ((bf16[16,16,1024]{2,1,0:T(8,128)(2,1)}), bf16[16,16,1024]{2,1,0:T(8,128)(2,1)S(1)}, u32[]{:S(2)}, u32[]{:S(2)}) async-start(bf16[16,16,1024]{2,1,0:T(8,128)(2,1)} %shard_map.99), calls=%async_computation.3 | async-start | bytes 1048576 | tf_op jit(solution)/shard_map/all_to_all | solution.py:425

commit v3 on v2

--- a/solution.py
+++ b/solution.py
@@ -107,6 +107,8 @@
 F32 = jnp.float32
 BF16 = jnp.bfloat16
 LANES = 128
+ORDER = (6, 2, 11, 0, 15, 7, 5, 4, 9, 8, 1, 3, 12, 13, 14, 10)
+PLACE = tuple(ORDER.index(device) for device in range(len(ORDER)))
 
 
 def dot(a, b, dims):
@@ -199,7 +201,7 @@
         x = jnp.concatenate(
             [
                 jnp.concatenate(
-                    [recv_ref[grid_rows * r + c, :, g * LANES : (g + 1) * LANES] for c in range(grid_rows)], axis=1
+                    [recv_ref[PLACE[grid_rows * r + c], :, g * LANES : (g + 1) * LANES] for c in range(grid_rows)], axis=1
                 )
                 for g in range(groups)
             ],
@@ -237,7 +239,7 @@
         y = dot(x.astype(BF16), swap, (1, 0)).astype(BF16)
         for g in range(half):
             for c in range(grid_rows):
-                out_ref[grid_rows * r + c, :, g * LANES : (g + 1) * LANES] = y[
+                out_ref[PLACE[grid_rows * r + c], :, g * LANES : (g + 1) * LANES] = y[
                     g * both : (g + 1) * both, c * LANES : (c + 1) * LANES
                 ]
 
@@ -298,7 +300,7 @@
         x = jnp.concatenate(
             [
                 jnp.concatenate(
-                    [recv_ref[grid_rows * r + c, :, g * LANES : (g + 1) * LANES] for c in range(grid_rows)], axis=1
+                    [recv_ref[PLACE[grid_rows * r + c], :, g * LANES : (g + 1) * LANES] for c in range(grid_rows)], axis=1
                 )
                 for g in range(half)
             ],
@@ -335,7 +337,7 @@
         y = dot(x.astype(BF16), swap, (1, 0)).astype(BF16)
         for g in range(groups):
             for c in range(grid_rows):
-                out_ref[grid_rows * r + c, :, g * LANES : (g + 1) * LANES] = y[
+                out_ref[PLACE[grid_rows * r + c], :, g * LANES : (g + 1) * LANES] = y[
                     g * both : (g + 1) * both, c * LANES : (c + 1) * LANES
                 ]
 
@@ -422,7 +424,7 @@
     per = hidden // devices
     n = tile * grid_rows
     shape = lambda dims, dtype: jax.ShapeDtypeStruct(dims, dtype)
-    whole = lambda x: lax.all_to_all(x, ("row", "col"), 0, 0, tiled=True)
+    whole = lambda x: lax.all_to_all(x, ("row", "col"), 0, 0, axis_index_groups=[ORDER], tiled=True)
     flat = pair.reshape(cells, channels)
     flat_cot = cotangent.reshape(cells, channels)
     valid_row = valid.reshape(1, -1)

time: 80.2 us -> 72 us (0.90)
  waiting for transfers between devices: 21.6 us -> 15.6 us
  blocking collectives: 36.3 us -> 31.9 us
  starting transfers between devices: 7.13 us -> 9.24 us
    all_to_all x2, waiting for transfers between devices: 21.6 us -> 15.6 us  [by_channel(): lax.all_to_all(x, ('row', 'col'), 0, 0, axis_index_groups=[ORDER], tiled=...]
    all_to_all x2, blocking collectives: 36.3 us -> 31.9 us  [by_channel(): lax.all_to_all(x, ('row', 'col'), 0, 0, axis_index_groups=[ORDER], tiled=...]
    all_to_all x2, starting transfers between devices: 7.13 us -> 9.24 us  [by_channel(): lax.all_to_all(x, ('row', 'col'), 0, 0, axis_index_groups=[ORDER], tiled=...]
  transfers between devices with their start and end apart: 2 -> 2, of which waited for: 2 -> 2; matrix products, arithmetic and copies ran while one was open for 0% -> 0% of each run, Pallas kernels for 5% -> 6%
where the time goes in v3:
time: 72 us; the launch traced here: 71.5 us
  blocking collectives  31.9 us (44%)
  waiting for transfers between devices  15.6 us (22%)
  Pallas kernels  13.9 us (19%)
  starting transfers between devices  9.24 us (13%)
  between operations  0.78 us (1%)
    all_to_all x2, blocking collectives, by_channel(): lax.all_to_all(x, ('row', 'col'), 0, 0, axis_index_groups=[ORDER], tiled=...  31.9 us
    all_to_all x2, waiting for transfers between devices, by_channel(): lax.all_to_all(x, ('row', 'col'), 0, 0, axis_index_groups=[ORDER], tiled=...  15.6 us
    pallas_call x7, Pallas kernels, call(): pl.pallas_call(body, out_shape=tuple(outs + far_outs), in_specs=[near_spe...  13.9 us
    all_to_all x2, starting transfers between devices, by_channel(): lax.all_to_all(x, ('row', 'col'), 0, 0, axis_index_groups=[ORDER], tiled=...  9.24 us
  transfers between devices with their start and end apart: 2, of which 2 were waited for; matrix products, arithmetic and copies ran while one was open for 0% of the time, Pallas kernels for 6%

profile of v3, /device:TPU:0, one launch (start us, length us, event | category | flops | bytes accessed | tf_op | source)
XLA Modules:
  0.0 71.5 jit_solution(10823479198587813584)
XLA Ops:
  0.6 0.0 copy-start
  0.6 0.0 copy-start.2
  0.7 0.0 copy-start.3
  0.7 0.0 copy-start.4
  0.7 0.0 copy-start.5
  0.7 0.0 copy-start.6
  0.7 2.9 %shard_map.95 = bf16[16,16,1024]{2,1,0:T(8,128)(2,1)} custom-call(bf16[1024,128]{1,0:T(8,128)(2,1)} %bitcast.7, s32[1,128]{1,0:T(1,128)} %bitcast.18, f32[1,128]{1,0:T(1,128)} %bitcast.12, bf16[128,512]{1,0:T(8,128)(2,1)} %refs_5_.3), custom_call_target="tpu_custom_call" | custom-call | flops 134217728 | bytes 918528 | tf_op jit(solution)/shard_map/pallas_call | solution.py:405
  3.6 20.2 %all_to_all.20.refs_0_ = bf16[16,16,1024]{2,1,0:T(8,128)(2,1)S(1)} all-to-all(bf16[16,16,1024]{2,1,0:T(8,128)(2,1)} %shard_map.95), channel_id=1, replica_groups={{6,2,11,0,15,7,5,4,9,8,1,3,12,13,14,10},{22,18,27,16,31,23,21,20,25,24,..., dimensions={0} | all-to-all | bytes 1048576 | tf_op jit(solution)/shard_map/all_to_all | solution.py:427
  23.9 2.2 %shard_map.96 = (bf16[16,16,512]{2,1,0:T(8,128)(2,1)}, bf16[8,128,128]{2,1,0:T(8,128)(2,1)S(1)}, bf16[8,128,128]{2,1,0:T(8,128)(2,1)S(1)}) custom-call(bf16[16,16,1024]{2,1,0:T(8,128)(2,1)S(1)} %all_to_all.20.refs_0_), custom_call_target="tpu_custom_call" | custom-call | flops 33554432 | bytes 1310720 | tf_op jit(solution)/shard_map/pallas_call | solution.py:405
  26.1 4.6 %all-to-all-start.1 = ((bf16[16,16,512]{2,1,0:T(8,128)(2,1)}), bf16[16,16,512]{2,1,0:T(8,128)(2,1)S(1)}, u32[]{:S(2)}, u32[]{:S(2)}) async-start(bf16[16,16,512]{2,1,0:T(8,128)(2,1)} %get-tuple-element.17), calls=%async_computation.1 | async-start | bytes 524288 | tf_op jit(solution)/shard_map/all_to_all | solution.py:427
  30.7 0.0 copy-done
  30.7 0.0 copy-done.2
  30.7 0.0 copy-done.3
  30.7 0.0 copy-done.4
  30.7 0.0 copy-done.5
  30.7 0.0 copy-done.6
  30.7 1.3 %shard_map.97.refs_1_ = f32[128,1024]{1,0:T(8,128)S(1)} custom-call(bf16[1024,128]{1,0:T(8,128)(2,1)S(1)} %bitcast.8, bf16[1024,128]{1,0:T(8,128)(2,1)S(1)} %bitcast.10, f32[1,128]{1,0:T(1,128)S(1)} %bitcast.13, bf16[128,128]{1,0:T(8,128)(2,1)S(1)} %copy-done.3, f32[1,128]{1,0:T(1,128)S(1)} %bitcast.16, bf16[128,128]{1,0:T(8,128)(2,1)S(1)} %copy-done.4), custom_call_target="tpu_custom_call" | custom-call | flops 67108864 | bytes 1115136 | tf_op jit(solution)/shard_map/pallas_call | solution.py:405
  32.0 5.6 %all-to-all-done.1.refs_0_ = bf16[16,16,512]{2,1,0:T(8,128)(2,1)S(1)} async-done(((bf16[16,16,512]{2,1,0:T(8,128)(2,1)}), bf16[16,16,512]{2,1,0:T(8,128)(2,1)S(1)}, u32[]{:S(2)}, u32[]{:S(2)}) %all-to-all-start.1) | async-done | bytes 262176 | tf_op jit(solution)/shard_map/all_to_all | solution.py:427
  37.6 0.4 shard_map.98
  38.0 11.6 %all_to_all.21.refs_0_ = bf16[16,16,512]{2,1,0:T(8,128)(2,1)S(1)} all-to-all(bf16[16,16,512]{2,1,0:T(8,128)(2,1)S(1)} %shard_map.98), channel_id=1, replica_groups={{6,2,11,0,15,7,5,4,9,8,1,3,12,13,14,10},{22,18,27,16,31,23,21,20,25,24,..., dimensions={0} | all-to-all | bytes 524288 | tf_op jit(solution)/shard_map/all_to_all | solution.py:427
  49.6 0.0 copy-start.1
  49.6 0.0 copy-start.7
  49.6 2.4 %shard_map.99 = bf16[16,16,1024]{2,1,0:T(8,128)(2,1)} custom-call(bf16[16,16,512]{2,1,0:T(8,128)(2,1)S(1)} %all_to_all.21.refs_0_, bf16[8,128,128]{2,1,0:T(8,128)(2,1)S(1)} %get-tuple-element.20.refs_1_, bf16[8,128,128]{2,1,0:T(8,128)(2,1)S(1)} %get-tuple-element.21.refs_2_), custom_call_target="tpu_custom_call" | custom-call | flops 67108864 | bytes 1310720 | tf_op jit(solution)/shard_map/pallas_call | solution.py:405
  52.0 4.7 %all-to-all-start.3 = ((bf16[16,16,1024]{2,1,0:T(8,128)(2,1)}), bf16[16,16,1024]{2,1,0:T(8,128)(2,1)S(1)}, u32[]{:S(2)}, u32[]{:S(2)}) async-start(bf16[16,16,1024]{2,1,0:T(8,128)(2,1)} %shard_map.99), calls=%async_computation.3 | async-start | bytes 1048576 | tf_op jit(solution)/shard_map/all_to_all | solution.py:427
  56.7 0.0 copy-done.1
  56.7 0.0 copy-done.7
  56.7 2.7 %shard_map.100 = (f32[128,1024]{1,0:T(8,128)S(1)}, f32[1,1024]{1,0:T(1,128)S(1)}, bf16[5,128,1024]{2,1,0:T(8,128)(2,1)S(1)}, bf16[1024,128]{1,0:T(8,128)(2,1)}) custom-call(bf16[16,16,512]{2,1,0:T(8,128)(2,1)S(1)} %all-to-all-done.1.refs_0_, f32[1,128]{1,0:T(1,128)S(1)} %bitcast.17, bf16[128,128]{1,0:T(8,128)(2,1)S(1)} %copy-done.4, ...), custom_call_target="tpu_custom_call" | custom-call | flops 201326592 | bytes 3085824 | tf_op jit(solution)/shard_map/pallas_call | solution.py:405
  59.4 10.0 %all-to-all-done.3.refs_0_ = bf16[16,16,1024]{2,1,0:T(8,128)(2,1)S(1)} async-done(((bf16[16,16,1024]{2,1,0:T(8,128)(2,1)}), bf16[16,16,1024]{2,1,0:T(8,128)(2,1)S(1)}, u32[]{:S(2)}, u32[]{:S(2)}) %all-to-all-start.3) | async-done | bytes 524320 | tf_op jit(solution)/shard_map/all_to_all | solution.py:427
  69.4 2.1 %shard_map.101 = f32[1024,128]{1,0:T(8,128)} custom-call(bf16[16,16,1024]{2,1,0:T(8,128)(2,1)S(1)} %all-to-all-done.3.refs_0_, bf16[5,128,1024]{2,1,0:T(8,128)(2,1)S(1)} %get-tuple-element.27.refs_1_, f32[128,1024]{1,0:T(8,128)S(1)} %get-tuple-element.28.refs_2_, f32[1,1024]{1,0:T(1,128)S(1)} %get-tuple-element.29.refs_3_, f32[1,128]{1,0:T(1,128)S(1)} %bitcast.15, ...), custom_call_target="tpu_custom_call" | custom-call | flops 167772160 | bytes 3052032 | tf_op jit(solution)/shard_map/pallas_call | solution.py:405
Async XLA Ops:
  0.6 30.0 %copy-start = (bf16[32,32,128]{2,1,0:T(8,128)(2,1)S(1)}, bf16[32,32,128]{2,1,0:T(8,128)(2,1)}, u32[]{:S(2)}) copy-start(bf16[32,32,128]{2,1,0:T(8,128)(2,1)} %param.8) | copy-start | bytes 786436
  0.6 30.0 %copy-start.2 = (bf16[32,32,128]{2,1,0:T(8,128)(2,1)S(1)}, bf16[32,32,128]{2,1,0:T(8,128)(2,1)}, u32[]{:S(2)}) copy-start(bf16[32,32,128]{2,1,0:T(8,128)(2,1)} %param.9) | copy-start | bytes 786436
  0.7 30.0 %copy-start.3 = (bf16[128,128]{1,0:T(8,128)(2,1)S(1)}, bf16[128,128]{1,0:T(8,128)(2,1)}, u32[]{:S(2)}) copy-start(bf16[128,128]{1,0:T(8,128)(2,1)} %refs_6_.1) | copy-start | bytes 98308
  0.7 30.0 %copy-start.4 = (bf16[128,128]{1,0:T(8,128)(2,1)S(1)}, bf16[128,128]{1,0:T(8,128)(2,1)}, u32[]{:S(2)}) copy-start(bf16[128,128]{1,0:T(8,128)(2,1)} %refs_2_.1) | copy-start | bytes 98308
  0.7 30.0 %copy-start.5 = (f32[128]{0:T(128)S(1)}, f32[128]{0:T(128)}, u32[]{:S(2)}) copy-start(f32[128]{0:T(128)} %param.11) | copy-start | bytes 1540
  0.7 30.0 %copy-start.6 = (f32[128]{0:T(128)S(1)}, f32[128]{0:T(128)}, u32[]{:S(2)}) copy-start(f32[128]{0:T(128)} %param.14) | copy-start | bytes 1540
  26.1 11.5 %all-to-all-start.1 = ((bf16[16,16,512]{2,1,0:T(8,128)(2,1)}), bf16[16,16,512]{2,1,0:T(8,128)(2,1)S(1)}, u32[]{:S(2)}, u32[]{:S(2)}) async-start(bf16[16,16,512]{2,1,0:T(8,128)(2,1)} %get-tuple-element.17), calls=%async_computation.1 | async-start | bytes 524288 | tf_op jit(solution)/shard_map/all_to_all | solution.py:427
  49.6 7.1 %copy-start.1 = (bf16[128,512]{1,0:T(8,128)(2,1)S(1)}, bf16[128,512]{1,0:T(8,128)(2,1)}, u32[]{:S(2)}) copy-start(bf16[128,512]{1,0:T(8,128)(2,1)} %refs_5_.3) | copy-start | bytes 393220
  49.6 7.1 %copy-start.7 = (s32[128]{0:T(128)S(1)}, s32[128]{0:T(128)}, u32[]{:S(2)}) copy-start(s32[128]{0:T(128)} %param.10) | copy-start | bytes 1540
  52.0 17.4 %all-to-all-start.3 = ((bf16[16,16,1024]{2,1,0:T(8,128)(2,1)}), bf16[16,16,1024]{2,1,0:T(8,128)(2,1)S(1)}, u32[]{:S(2)}, u32[]{:S(2)}) async-start(bf16[16,16,1024]{2,1,0:T(8,128)(2,1)} %shard_map.99), calls=%async_computation.3 | async-start | bytes 1048576 | tf_op jit(solution)/shard_map/all_to_all | solution.py:427

commit v4 on v3

--- a/solution.py
+++ b/solution.py
@@ -107,7 +107,7 @@
 F32 = jnp.float32
 BF16 = jnp.bfloat16
 LANES = 128
-ORDER = (6, 2, 11, 0, 15, 7, 5, 4, 9, 8, 1, 3, 12, 13, 14, 10)
+ORDER = (6, 4, 11, 7, 5, 0, 15, 12, 14, 8, 1, 10, 9, 13, 2, 3)
 PLACE = tuple(ORDER.index(device) for device in range(len(ORDER)))
 
 
@@ -138,22 +138,36 @@
     return inv * (q - first - unit * second)
 
 
+def one_hot(at):
+    return jnp.where(at, 1.0, 0.0).astype(BF16)
+
+
 def block_swap():
-    size, width = 4 * LANES, LANES // 4
-    row = lax.broadcasted_iota(jnp.int32, (size, LANES), 0)
-    col = lax.broadcasted_iota(jnp.int32, (size, LANES), 1)
-    target = (row // width % 4) * LANES + (row // LANES) * width + row % width - col
-    return jnp.concatenate([(target == n * LANES).astype(F32) for n in range(4)], axis=1).astype(BF16)
+    width = LANES // 4
+    row = lax.broadcasted_iota(jnp.int32, (width, LANES), 0)
+    lane = lax.broadcasted_iota(jnp.int32, (width, LANES), 1)
+    none = jnp.zeros((width, LANES), BF16)
+    to = [one_hot(row + width * c == lane) for c in range(4)]
+    return jnp.concatenate(
+        [jnp.concatenate([to[c] if n == p else none for n in range(4)], axis=1) for c in range(4) for p in range(4)],
+        axis=0,
+    )
 
 
 def keep_row(valid, tile, cells):
     n = valid.ref.shape[1]
-    token = lax.broadcasted_iota(jnp.int32, (n, cells), 0)
-    cell = lax.broadcasted_iota(jnp.int32, (n, cells), 1)
-    first = (token == lax.axis_index("row") * tile + cell // tile).astype(F32).astype(BF16)
-    second = (token == lax.axis_index("col") * tile + cell % tile).astype(F32).astype(BF16)
-    v = jnp.broadcast_to(valid.ready()[...].astype(F32), (8, n)).astype(BF16)
-    return (dot(v, first, (1, 0)) * dot(v, second, (1, 0)))[:1]
+    groups, rows = cells // n, n // tile
+    token = lax.broadcasted_iota(jnp.int32, (n, n), 0)
+    lane = lax.broadcasted_iota(jnp.int32, (n, n), 1)
+    place = lax.broadcasted_iota(jnp.int32, (groups, n), 1) - lax.axis_index("row") * tile
+    group = rows * lax.broadcasted_iota(jnp.int32, (groups, n), 0)
+    inside = jnp.logical_and(place >= group, place < group + rows)
+    first = one_hot(lax.rem(token, rows) == lax.div(lane, tile))
+    second = one_hot(token - lax.axis_index("col") * tile == lax.rem(lane, tile))
+    v = jnp.broadcast_to(valid.ready()[...].astype(F32), (groups, n))
+    own = jnp.where(inside, v, 0.0).astype(BF16)
+    keep = dot(own, first, (1, 0)) * dot(v.astype(BF16), second, (1, 0))
+    return jnp.concatenate([keep[g : g + 1] for g in range(groups)], axis=1)
 
 
 def normed_of(pair, in_gain):
@@ -162,20 +176,24 @@
     return normed, unit, inv
 
 
-def project_kernel(tile, pair, valid, in_gain, proj_weight, out_ref):
+def project_kernel(tile, parts, valid, in_gain, proj_weight, pair, out):
+    cells, channels = pair.ref.shape
     hidden = proj_weight.ref.shape[1] // 4
-    shards, both, cells = out_ref.shape
+    shards, both, _ = out.ref.shape
+    per = both // 2
+    keep = keep_row(valid, tile, cells)
     normed, _, _ = normed_of(pair, in_gain)
-    keep = keep_row(valid, tile, cells)
-    weights = proj_weight.ready()
-    sides = []
-    for side in range(2):
-        weight = weights[:, 2 * hidden * side : 2 * hidden * (side + 1)].T
-        proj = dot(weight, normed, (1, 0))
-        sides.append(jax.nn.sigmoid(proj[:hidden]) * proj[hidden:] * keep)
-    for s in range(shards):
-        rows = slice(s * both // 2, (s + 1) * both // 2)
-        out_ref[s] = jnp.concatenate([sides[0][rows], sides[1][rows]], axis=0).astype(BF16)
+    weights = proj_weight.ready()[...].T
+    share = hidden // parts
+    for part in range(parts):
+        rows = [weights[block * hidden + part * share : block * hidden + (part + 1) * share] for block in range(4)]
+        proj = dot(jnp.concatenate(rows, axis=0), normed, (1, 0))
+        left = jax.nn.sigmoid(proj[:share]) * proj[share : 2 * share] * keep
+        right = jax.nn.sigmoid(proj[2 * share : 3 * share]) * proj[3 * share :] * keep
+        for s in range(shards // parts):
+            own = slice(s * per, (s + 1) * per)
+            out.ref[part * shards // parts + s] = jnp.concatenate([left[own], right[own]], axis=0).astype(BF16)
+        out.send(part)
 
 
 def gate_of(normed, cot, gate_weight):
@@ -288,8 +306,8 @@
         factor_ref[2 * side + 1] = (keep * sig).astype(BF16)
 
 
-def sides_kernel(grid_rows, recv_ref, left, right, out_ref, d_tri, rows):
-    devices, both, cells = out_ref.shape
+def sides_kernel(grid_rows, recv_ref, left, right, out, d_tri, rows):
+    devices, both, cells = out.ref.shape
     per = both // 2
     n = left.ref.shape[1]
     tile = n // grid_rows
@@ -335,84 +353,109 @@
             axis=0,
         )
         y = dot(x.astype(BF16), swap, (1, 0)).astype(BF16)
-        for g in range(groups):
-            for c in range(grid_rows):
-                out_ref[PLACE[grid_rows * r + c], :, g * LANES : (g + 1) * LANES] = y[
+        for c in range(grid_rows):
+            place = PLACE[grid_rows * r + c]
+            for g in range(groups):
+                out.ref[place, :, g * LANES : (g + 1) * LANES] = y[
                     g * both : (g + 1) * both, c * LANES : (c + 1) * LANES
                 ]
-
-
-def pair_grad_kernel(recv_ref, factor_ref, unit_ref, inv_ref, in_gain, proj_weight, gate_weight, out):
+            out.send(place)
+
+
+def pair_grad_kernel(parts, recv_ref, factor_ref, unit_ref, inv_ref, in_gain, proj_weight, gate_weight, out):
     shards, both, cells = recv_ref.shape
     hidden = shards * both // 2
-    x = recv_ref[...].astype(F32)
-    d_left = x[:, : both // 2].reshape(hidden, cells)
-    d_right = x[:, both // 2 :].reshape(hidden, cells)
-    d_proj = jnp.concatenate(
-        [(grad * factor_ref[2 * side + part].astype(F32)).astype(BF16) for side, grad in enumerate((d_left, d_right)) for part in range(2)],
-        axis=0,
-    )
-    d_normed = dot(proj_weight.ready()[...], d_proj, (1, 0))
-    d_normed = d_normed + dot(gate_weight.ready()[...], factor_ref[4], (1, 0))
-    q = d_normed * spread(column(in_gain.ready()[...]), cells)
-    out.ref[...] = unit_back(q, unit_ref[...], inv_ref[...]).T
-    out.send()
+    width = cells // parts
+    gain = spread(column(in_gain.ready()[...]), width)
+    weights, gate_weights = proj_weight.ready()[...], gate_weight.ready()[...]
+    for part in range(parts):
+        lanes = slice(part * width, (part + 1) * width)
+        x = recv_ref[:, :, lanes].astype(F32)
+        grads = (x[:, : both // 2].reshape(hidden, width), x[:, both // 2 :].reshape(hidden, width))
+        d_proj = jnp.concatenate(
+            [
+                (grad * factor_ref[2 * side + k, :, lanes].astype(F32)).astype(BF16)
+                for side, grad in enumerate(grads)
+                for k in range(2)
+            ],
+            axis=0,
+        )
+        d_normed = dot(weights, d_proj, (1, 0)) + dot(gate_weights, factor_ref[4, :, lanes], (1, 0))
+        out.ref[lanes, :] = unit_back(d_normed * gain, unit_ref[:, lanes], inv_ref[:, lanes]).T
+        out.send(part)
 
 
 class Arriving:
-    def __init__(self, source, ref, sem):
-        self.ref, self.copy = ref, pltpu.make_async_copy(source, ref, sem)
-        self.copy.start()
-
-    def ready(self):
-        if self.copy is not None:
-            self.copy.wait()
-            self.copy = None
+    def __init__(self, source, ref, sems, parts):
+        size = ref.shape[0] // parts
+        cuts = [pl.ds(part * size, size) for part in range(parts)]
+        self.ref = ref
+        self.copies = [pltpu.make_async_copy(source.at[cut], ref.at[cut], sem) for cut, sem in zip(cuts, sems)]
+        for copy in self.copies:
+            copy.start()
+        self.waiting = set(range(parts))
+
+    def ready(self, part=None):
+        for one in sorted(self.waiting) if part is None else [part]:
+            if one in self.waiting:
+                self.copies[one].wait()
+                self.waiting.remove(one)
         return self.ref
 
 
 class Leaving:
-    def __init__(self, target, ref, sem):
-        self.ref, self.copy = ref, pltpu.make_async_copy(ref, target, sem)
-
-    def send(self):
-        self.copy.start()
+    def __init__(self, target, ref, sems, parts, dim):
+        size = ref.shape[dim] // parts
+        cuts = [(slice(None),) * dim + (pl.ds(part * size, size),) for part in range(parts)]
+        self.ref = ref
+        self.copies = [pltpu.make_async_copy(ref.at[cut], target.at[cut], sem) for cut, sem in zip(cuts, sems)]
+
+    def send(self, part=0):
+        self.copies[part].start()
 
 
 def call(kernel, outs, args, flops, scratch=(), far=(), far_outs=(), room=24):
-    outs, args, far, far_outs, scratch = (list(x) for x in (outs, args, far, far_outs, scratch))
+    outs, args, scratch = list(outs), list(args), list(scratch)
+    far = [one if isinstance(one, tuple) else (one, 1) for one in far]
+    far_outs = [one if isinstance(one, tuple) else (one, 1, 0) for one in far_outs]
+    far_arrays, far_shapes = [one[0] for one in far], [one[0] for one in far_outs]
     counts = [len(args), len(far), len(outs), len(far_outs), len(far), len(far_outs), len(scratch)]
 
     def body(*refs):
-        parts, at = [], 0
+        groups, at = [], 0
         for count in counts:
-            parts.append(list(refs[at : at + count]))
+            groups.append(list(refs[at : at + count]))
             at += count
-        near_in, far_in, near_out, far_out, held, leaving, rest = parts
+        near_in, far_in, near_out, far_out, held, leaving, rest = groups
         sems = refs[at]
-        arrivals = [Arriving(a, b, sems.at[i]) for i, (a, b) in enumerate(zip(far_in, held))]
-        departures = [
-            Leaving(a, b, sems.at[len(held) + i]) for i, (a, b) in enumerate(zip(far_out, leaving))
-        ]
+        used = 0
+        arrivals, departures = [], []
+        for source, ref, (_, parts) in zip(far_in, held, far):
+            arrivals.append(Arriving(source, ref, [sems.at[used + k] for k in range(parts)], parts))
+            used += parts
+        for target, ref, (_, parts, dim) in zip(far_out, leaving, far_outs):
+            departures.append(Leaving(target, ref, [sems.at[used + k] for k in range(parts)], parts, dim))
+            used += parts
         kernel(*near_in, *arrivals, *near_out, *departures, *rest)
         for one in arrivals:
             one.ready()
         for one in departures:
-            one.copy.wait()
+            for copy in one.copies:
+                copy.wait()
 
     near_spec, far_spec = pl.BlockSpec(memory_space=pltpu.VMEM), pl.BlockSpec(memory_space=pltpu.HBM)
-    moved = sum(a.size * a.dtype.itemsize for a in args + far + outs + far_outs)
+    moved = sum(a.size * a.dtype.itemsize for a in args + far_arrays + outs + far_shapes)
     return pl.pallas_call(
         body,
-        out_shape=tuple(outs + far_outs),
+        out_shape=tuple(outs + far_shapes),
         in_specs=[near_spec] * len(args) + [far_spec] * len(far),
         out_specs=tuple([near_spec] * len(outs) + [far_spec] * len(far_outs)),
-        scratch_shapes=[pltpu.VMEM(a.shape, a.dtype) for a in far + far_outs]
+        scratch_shapes=[pltpu.VMEM(a.shape, a.dtype) for a in far_arrays + far_shapes]
         + scratch
-        + [pltpu.SemaphoreType.DMA((max(1, len(far) + len(far_outs)),))],
+        + [pltpu.SemaphoreType.DMA((max(1, sum(one[1] for one in far + far_outs)),))],
         compiler_params=pltpu.CompilerParams(vmem_limit_bytes=int(room * 2**20)),
         cost_estimate=pl.CostEstimate(flops=flops, bytes_accessed=moved, transcendentals=0),
-    )(*args, *far)
+    )(*args, *far_arrays)
 
 
 def by_channel(pair, cotangent, valid, in_gain, proj_weight, gate_weight, out_gain, out_weight):
@@ -434,14 +477,24 @@
     plane = shape((channels, cells), F32)
 
     (sides,) = call(
-        functools.partial(project_kernel, tile),
-        [shape((devices, both, cells), BF16)],
+        functools.partial(project_kernel, tile, 4),
+        [],
         (),
         2 * cells * channels * 4 * hidden,
-        far=(flat, valid_row, in_row, proj_weight),
+        far=(valid_row, in_row, proj_weight, flat),
+        far_outs=[(shape((devices, both, cells), BF16), 4, 0)],
         room=62,
     )
+    sides, flat_2, flat_cot_2 = lax.optimization_barrier((sides, flat, flat_cot))
     sides = whole(sides)
+    (q,) = call(
+        gate_kernel,
+        [plane],
+        (),
+        2 * cells * channels * 2 * hidden,
+        far=(flat_2, flat_cot_2, in_row, gate_weight, out_row, out_weight),
+    )
+    sides, q = lax.optimization_barrier((sides, q))
     tri, left, right = call(
         functools.partial(tri_kernel, grid_rows),
         [shape((devices, both, cells // 2), BF16)],
@@ -450,15 +503,7 @@
         [pltpu.VMEM((n * both, n), F32), pltpu.VMEM((n * per, n), F32)],
         far_outs=[shape((per, n, n), BF16)] * 2,
     )
-    tri, flat_2, flat_cot_2 = lax.optimization_barrier((tri, flat, flat_cot))
     tri = whole(tri)
-    (q,) = call(
-        gate_kernel,
-        [plane],
-        (),
-        2 * cells * channels * 2 * hidden,
-        far=(flat_2, flat_cot_2, in_row, gate_weight, out_row, out_weight),
-    )
     (d_tri,) = call(
         d_tri_kernel,
         [shape((devices, both, cells // 2), BF16)],
@@ -468,11 +513,12 @@
     d_tri = whole(d_tri)
     (d_sides,) = call(
         functools.partial(sides_kernel, grid_rows),
-        [shape((devices, both, cells), BF16)],
+        [],
         (d_tri,),
         4 * per * n * n * n,
         [pltpu.VMEM((n * per, n), F32), pltpu.VMEM((n * both, n), F32)],
         far=(left, right),
+        far_outs=[(shape((devices, both, cells), BF16), devices, 0)],
     )
     d_sides, flat_4, flat_cot_4, tri = lax.optimization_barrier((d_sides, flat, flat_cot, tri))
     d_sides = whole(d_sides)
@@ -485,12 +531,12 @@
         far_outs=[shape((cells, channels), BF16)],
     )
     (pair_grad,) = call(
-        pair_grad_kernel,
+        functools.partial(pair_grad_kernel, 4),
         [],
         (d_sides, factors, unit, inv),
         2 * cells * channels * 5 * hidden,
         far=(in_row, proj_weight, gate_weight),
-        far_outs=[shape((cells, channels), F32)],
+        far_outs=[(shape((cells, channels), F32), 4, 0)],
     )
     return (update.reshape(pair.shape), pair_grad.reshape(pair.shape))
 

time: 72 us -> 69.2 us (0.961)
  blocking collectives: 31.9 us -> 24.3 us
  waiting for transfers between devices: 15.6 us -> 19 us
  starting transfers between devices: 9.24 us -> 12.4 us
  Pallas kernels: 13.9 us -> 12.2 us
    all_to_all x2, blocking collectives: 31.9 us -> 24.3 us  [by_channel(): lax.all_to_all(x, ('row', 'col'), 0, 0, axis_index_groups=[ORDER], tiled=...]
    all_to_all x2, waiting for transfers between devices: 15.6 us -> 19 us  [by_channel(): lax.all_to_all(x, ('row', 'col'), 0, 0, axis_index_groups=[ORDER], tiled=...]
    all_to_all x2, starting transfers between devices: 9.24 us -> 12.4 us  [by_channel(): lax.all_to_all(x, ('row', 'col'), 0, 0, axis_index_groups=[ORDER], tiled=...]
    pallas_call x7, Pallas kernels: 13.9 us -> 12.2 us  [call(): pl.pallas_call(body, out_shape=tuple(outs + far_shapes), in_specs=[near_s...]
where the time goes in v4:
time: 69.2 us; the launch traced here: 68.7 us
  blocking collectives  24.3 us (35%)
  waiting for transfers between devices  19 us (27%)
  starting transfers between devices  12.4 us (18%)
  Pallas kernels  12.2 us (18%)
  between operations  0.78 us (1%)
    all_to_all x2, blocking collectives, by_channel(): lax.all_to_all(x, ('row', 'col'), 0, 0, axis_index_groups=[ORDER], tiled=...  24.3 us
    all_to_all x2, waiting for transfers between devices, by_channel(): lax.all_to_all(x, ('row', 'col'), 0, 0, axis_index_groups=[ORDER], tiled=...  19 us
    all_to_all x2, starting transfers between devices, by_channel(): lax.all_to_all(x, ('row', 'col'), 0, 0, axis_index_groups=[ORDER], tiled=...  12.4 us
    pallas_call x7, Pallas kernels, call(): pl.pallas_call(body, out_shape=tuple(outs + far_shapes), in_specs=[near_s...  12.2 us
  transfers between devices with their start and end apart: 2, of which 2 were waited for; matrix products, arithmetic and copies ran while one was open for 0% of the time, Pallas kernels for 6%

profile of v4, /device:TPU:0, one launch (start us, length us, event | category | flops | bytes accessed | tf_op | source)
XLA Modules:
  0.0 68.7 jit_solution(1776385222061708341)
XLA Ops:
  0.6 0.0 copy-start.5
  0.6 0.0 copy-start
  0.7 0.0 copy-start.2
  0.7 0.0 copy-start.3
  0.7 0.0 copy-start.4
  0.7 0.0 copy-start.6
  0.7 2.6 %shard_map.95 = bf16[16,16,1024]{2,1,0:T(8,128)(2,1)} custom-call(s32[1,128]{1,0:T(1,128)} %bitcast.18, f32[1,128]{1,0:T(1,128)} %bitcast.12, bf16[128,512]{1,0:T(8,128)(2,1)} %refs_5_.3, bf16[1024,128]{1,0:T(8,128)(2,1)} %bitcast.7), custom_call_target="tpu_custom_call" | custom-call | flops 134217728 | bytes 918528 | tf_op jit(solution)/shard_map/pallas_call | solution.py:448
  3.3 7.6 %all-to-all-start = ((bf16[16,16,1024]{2,1,0:T(8,128)(2,1)}), bf16[16,16,1024]{2,1,0:T(8,128)(2,1)S(1)}, u32[]{:S(2)}, u32[]{:S(2)}) async-start(bf16[16,16,1024]{2,1,0:T(8,128)(2,1)} %shard_map.95), calls=%async_computation | async-start | bytes 1048576 | tf_op jit(solution)/shard_map/all_to_all | solution.py:470
  10.9 0.0 copy-done.5
  10.9 0.0 copy-done
  11.0 0.0 copy-done.2
  11.0 0.0 copy-done.3
  11.0 0.0 copy-done.4
  11.0 0.0 copy-done.6
  11.0 1.3 %shard_map.96.refs_1_ = f32[128,1024]{1,0:T(8,128)S(1)} custom-call(bf16[1024,128]{1,0:T(8,128)(2,1)S(1)} %bitcast.8, bf16[1024,128]{1,0:T(8,128)(2,1)S(1)} %bitcast.10, f32[1,128]{1,0:T(1,128)S(1)} %bitcast.13, bf16[128,128]{1,0:T(8,128)(2,1)S(1)} %copy-done.3, f32[1,128]{1,0:T(1,128)S(1)} %bitcast.16, bf16[128,128]{1,0:T(8,128)(2,1)S(1)} %copy-done.4), custom_call_target="tpu_custom_call" | custom-call | flops 67108864 | bytes 1115136 | tf_op jit(solution)/shard_map/pallas_call | solution.py:448
  12.3 10.0 %all-to-all-done.refs_0_ = bf16[16,16,1024]{2,1,0:T(8,128)(2,1)S(1)} async-done(((bf16[16,16,1024]{2,1,0:T(8,128)(2,1)}), bf16[16,16,1024]{2,1,0:T(8,128)(2,1)S(1)}, u32[]{:S(2)}, u32[]{:S(2)}) %all-to-all-start) | async-done | bytes 524320 | tf_op jit(solution)/shard_map/all_to_all | solution.py:470
  22.3 1.4 %shard_map.97 = (bf16[16,16,512]{2,1,0:T(8,128)(2,1)S(1)}, bf16[8,128,128]{2,1,0:T(8,128)(2,1)S(1)}, bf16[8,128,128]{2,1,0:T(8,128)(2,1)S(1)}) custom-call(bf16[16,16,1024]{2,1,0:T(8,128)(2,1)S(1)} %all-to-all-done.refs_0_), custom_call_target="tpu_custom_call" | custom-call | flops 33554432 | bytes 1310720 | tf_op jit(solution)/shard_map/pallas_call | solution.py:448
  23.6 12.8 %all_to_all.20.refs_0_ = bf16[16,16,512]{2,1,0:T(8,128)(2,1)S(1)} all-to-all(bf16[16,16,512]{2,1,0:T(8,128)(2,1)S(1)} %get-tuple-element.22), channel_id=1, replica_groups={{6,4,11,7,5,0,15,12,14,8,1,10,9,13,2,3},{22,20,27,23,21,16,31,28,30,24,..., dimensions={0} | all-to-all | bytes 524288 | tf_op jit(solution)/shard_map/all_to_all | solution.py:470
  36.4 0.4 shard_map.98
  36.8 11.5 %all_to_all.21.refs_0_ = bf16[16,16,512]{2,1,0:T(8,128)(2,1)S(1)} all-to-all(bf16[16,16,512]{2,1,0:T(8,128)(2,1)S(1)} %shard_map.98), channel_id=1, replica_groups={{6,4,11,7,5,0,15,12,14,8,1,10,9,13,2,3},{22,20,27,23,21,16,31,28,30,24,..., dimensions={0} | all-to-all | bytes 524288 | tf_op jit(solution)/shard_map/all_to_all | solution.py:470
  48.3 0.0 copy-start.1
  48.3 0.0 copy-start.7
  48.3 2.3 %shard_map.99 = bf16[16,16,1024]{2,1,0:T(8,128)(2,1)} custom-call(bf16[16,16,512]{2,1,0:T(8,128)(2,1)S(1)} %all_to_all.21.refs_0_, bf16[8,128,128]{2,1,0:T(8,128)(2,1)S(1)} %get-tuple-element.24.refs_1_, bf16[8,128,128]{2,1,0:T(8,128)(2,1)S(1)} %get-tuple-element.25.refs_2_), custom_call_target="tpu_custom_call" | custom-call | flops 67108864 | bytes 1310720 | tf_op jit(solution)/shard_map/pallas_call | solution.py:448
  50.6 4.8 %all-to-all-start.3 = ((bf16[16,16,1024]{2,1,0:T(8,128)(2,1)}), bf16[16,16,1024]{2,1,0:T(8,128)(2,1)S(1)}, u32[]{:S(2)}, u32[]{:S(2)}) async-start(bf16[16,16,1024]{2,1,0:T(8,128)(2,1)} %shard_map.99), calls=%async_computation.3 | async-start | bytes 1048576 | tf_op jit(solution)/shard_map/all_to_all | solution.py:470
  55.4 0.0 copy-done.1
  55.4 0.0 copy-done.7
  55.4 2.6 %shard_map.100 = (f32[128,1024]{1,0:T(8,128)S(1)}, f32[1,1024]{1,0:T(1,128)S(1)}, bf16[5,128,1024]{2,1,0:T(8,128)(2,1)S(1)}, bf16[1024,128]{1,0:T(8,128)(2,1)}) custom-call(bf16[16,16,512]{2,1,0:T(8,128)(2,1)S(1)} %all_to_all.20.refs_0_, f32[1,128]{1,0:T(1,128)S(1)} %bitcast.17, bf16[128,128]{1,0:T(8,128)(2,1)S(1)} %copy-done.4, ...), custom_call_target="tpu_custom_call" | custom-call | flops 201326592 | bytes 3085824 | tf_op jit(solution)/shard_map/pallas_call | solution.py:448
  58.0 9.1 %all-to-all-done.3.refs_0_ = bf16[16,16,1024]{2,1,0:T(8,128)(2,1)S(1)} async-done(((bf16[16,16,1024]{2,1,0:T(8,128)(2,1)}), bf16[16,16,1024]{2,1,0:T(8,128)(2,1)S(1)}, u32[]{:S(2)}, u32[]{:S(2)}) %all-to-all-start.3) | async-done | bytes 524320 | tf_op jit(solution)/shard_map/all_to_all | solution.py:470
  67.1 1.7 %shard_map.101 = f32[1024,128]{1,0:T(8,128)} custom-call(bf16[16,16,1024]{2,1,0:T(8,128)(2,1)S(1)} %all-to-all-done.3.refs_0_, bf16[5,128,1024]{2,1,0:T(8,128)(2,1)S(1)} %get-tuple-element.31.refs_1_, f32[128,1024]{1,0:T(8,128)S(1)} %get-tuple-element.32.refs_2_, f32[1,1024]{1,0:T(1,128)S(1)} %get-tuple-element.33.refs_3_, f32[1,128]{1,0:T(1,128)S(1)} %bitcast.15, ...), custom_call_target="tpu_custom_call" | custom-call | flops 167772160 | bytes 3052032 | tf_op jit(solution)/shard_map/pallas_call | solution.py:448
Async XLA Ops:
  0.6 10.3 %copy-start.5 = (f32[128]{0:T(128)S(1)}, f32[128]{0:T(128)}, u32[]{:S(2)}) copy-start(f32[128]{0:T(128)} %param.11) | copy-start | bytes 1540
  0.6 10.3 %copy-start = (bf16[32,32,128]{2,1,0:T(8,128)(2,1)S(1)}, bf16[32,32,128]{2,1,0:T(8,128)(2,1)}, u32[]{:S(2)}) copy-start(bf16[32,32,128]{2,1,0:T(8,128)(2,1)} %param.8) | copy-start | bytes 786436
  0.7 10.3 %copy-start.2 = (bf16[32,32,128]{2,1,0:T(8,128)(2,1)S(1)}, bf16[32,32,128]{2,1,0:T(8,128)(2,1)}, u32[]{:S(2)}) copy-start(bf16[32,32,128]{2,1,0:T(8,128)(2,1)} %param.9) | copy-start | bytes 786436
  0.7 10.3 %copy-start.3 = (bf16[128,128]{1,0:T(8,128)(2,1)S(1)}, bf16[128,128]{1,0:T(8,128)(2,1)}, u32[]{:S(2)}) copy-start(bf16[128,128]{1,0:T(8,128)(2,1)} %refs_6_.1) | copy-start | bytes 98308
  0.7 10.3 %copy-start.4 = (bf16[128,128]{1,0:T(8,128)(2,1)S(1)}, bf16[128,128]{1,0:T(8,128)(2,1)}, u32[]{:S(2)}) copy-start(bf16[128,128]{1,0:T(8,128)(2,1)} %refs_2_.3) | copy-start | bytes 98308
  0.7 10.3 %copy-start.6 = (f32[128]{0:T(128)S(1)}, f32[128]{0:T(128)}, u32[]{:S(2)}) copy-start(f32[128]{0:T(128)} %param.14) | copy-start | bytes 1540
  3.3 18.9 %all-to-all-start = ((bf16[16,16,1024]{2,1,0:T(8,128)(2,1)}), bf16[16,16,1024]{2,1,0:T(8,128)(2,1)S(1)}, u32[]{:S(2)}, u32[]{:S(2)}) async-start(bf16[16,16,1024]{2,1,0:T(8,128)(2,1)} %shard_map.95), calls=%async_computation | async-start | bytes 1048576 | tf_op jit(solution)/shard_map/all_to_all | solution.py:470
  48.3 7.1 %copy-start.1 = (bf16[128,512]{1,0:T(8,128)(2,1)S(1)}, bf16[128,512]{1,0:T(8,128)(2,1)}, u32[]{:S(2)}) copy-start(bf16[128,512]{1,0:T(8,128)(2,1)} %refs_5_.3) | copy-start | bytes 393220
  48.3 7.1 %copy-start.7 = (s32[128]{0:T(128)S(1)}, s32[128]{0:T(128)}, u32[]{:S(2)}) copy-start(s32[128]{0:T(128)} %param.10) | copy-start | bytes 1540
  50.6 16.5 %all-to-all-start.3 = ((bf16[16,16,1024]{2,1,0:T(8,128)(2,1)}), bf16[16,16,1024]{2,1,0:T(8,128)(2,1)S(1)}, u32[]{:S(2)}, u32[]{:S(2)}) async-start(bf16[16,16,1024]{2,1,0:T(8,128)(2,1)} %shard_map.99), calls=%async_computation.3 | async-start | bytes 1048576 | tf_op jit(solution)/shard_map/all_to_all | solution.py:470

commit v5 on v4

--- a/solution.py
+++ b/solution.py
@@ -107,7 +107,7 @@
 F32 = jnp.float32
 BF16 = jnp.bfloat16
 LANES = 128
-ORDER = (6, 4, 11, 7, 5, 0, 15, 12, 14, 8, 1, 10, 9, 13, 2, 3)
+ORDER = (6, 7, 11, 0, 12, 2, 3, 5, 14, 8, 1, 10, 9, 13, 4, 15)
 PLACE = tuple(ORDER.index(device) for device in range(len(ORDER)))
 
 
@@ -208,10 +208,10 @@
     q_ref[...] = q * spread(column(out_gain.ready()[...]), q.shape[1])
 
 
-def tri_kernel(grid_rows, recv_ref, out_ref, left, right, rows, tri):
+def tri_kernel(grid_rows, recv_ref, out_ref, left_ref, right_ref, rows, tri):
     devices, both, cells = recv_ref.shape
     per = both // 2
-    n = left.ref.shape[1]
+    n = left_ref.shape[1]
     tile = n // grid_rows
     groups = cells // LANES
     swap = block_swap()
@@ -231,12 +231,11 @@
                 at = (r * tile + g * grid_rows + p) * both
                 rows[at : at + both, :] = y[g * both : (g + 1) * both, p * LANES : (p + 1) * LANES]
     for h in range(per):
-        left.ref[h] = rows[pl.ds(h, n, stride=both), :].astype(BF16)
-        right.ref[h] = rows[pl.ds(per + h, n, stride=both), :].astype(BF16)
-    left.send()
-    right.send()
-    for h in range(per):
-        tri[pl.ds(h, n, stride=per), :] = dot(left.ref[h], right.ref[h], (1, 1))
+        left = rows[pl.ds(h, n, stride=both), :].astype(BF16)
+        right = rows[pl.ds(per + h, n, stride=both), :].astype(BF16)
+        left_ref[h] = left
+        right_ref[h] = right
+        tri[pl.ds(h, n, stride=per), :] = dot(left, right, (1, 1))
     half = groups // 2
     for r in range(grid_rows):
         x = jnp.concatenate(
@@ -306,10 +305,10 @@
         factor_ref[2 * side + 1] = (keep * sig).astype(BF16)
 
 
-def sides_kernel(grid_rows, recv_ref, left, right, out, d_tri, rows):
+def sides_kernel(grid_rows, recv_ref, left_ref, right_ref, out, d_tri, rows):
     devices, both, cells = out.ref.shape
     per = both // 2
-    n = left.ref.shape[1]
+    n = left_ref.shape[1]
     tile = n // grid_rows
     groups = cells // LANES
     half = groups // 2
@@ -332,7 +331,6 @@
                     d_tri[at : at + per, :] = y[
                         g * both + k * per : g * both + (k + 1) * per, p * LANES : (p + 1) * LANES
                     ]
-    left_ref, right_ref = left.ready(), right.ready()
     for h in range(per):
         grad = d_tri[pl.ds(h, n, stride=per), :].astype(BF16)
         rows[pl.ds(h, n, stride=both), :] = dot(grad, right_ref[h], (1, 0))
@@ -497,11 +495,10 @@
     sides, q = lax.optimization_barrier((sides, q))
     tri, left, right = call(
         functools.partial(tri_kernel, grid_rows),
-        [shape((devices, both, cells // 2), BF16)],
+        [shape((devices, both, cells // 2), BF16), shape((per, n, n), BF16), shape((per, n, n), BF16)],
         (sides,),
         2 * per * n * n * n,
         [pltpu.VMEM((n * both, n), F32), pltpu.VMEM((n * per, n), F32)],
-        far_outs=[shape((per, n, n), BF16)] * 2,
     )
     tri = whole(tri)
     (d_tri,) = call(
@@ -514,10 +511,9 @@
     (d_sides,) = call(
         functools.partial(sides_kernel, grid_rows),
         [],
-        (d_tri,),
+        (d_tri, left, right),
         4 * per * n * n * n,
         [pltpu.VMEM((n * per, n), F32), pltpu.VMEM((n * both, n), F32)],
-        far=(left, right),
         far_outs=[(shape((devices, both, cells), BF16), devices, 0)],
     )
     d_sides, flat_4, flat_cot_4, tri = lax.optimization_barrier((d_sides, flat, flat_cot, tri))

time: 69.2 us -> 68.2 us (0.986)
  waiting for transfers between devices: 19 us -> 18.2 us
  blocking collectives: 24.3 us -> 23.6 us
    all_to_all x2, waiting for transfers between devices: 19 us -> 18.2 us  [by_channel(): lax.all_to_all(x, ('row', 'col'), 0, 0, axis_index_groups=[ORDER], tiled=...]
    all_to_all x2, blocking collectives: 24.3 us -> 23.6 us  [by_channel(): lax.all_to_all(x, ('row', 'col'), 0, 0, axis_index_groups=[ORDER], tiled=...]
where the time goes in v5:
time: 68.2 us; the launch traced here: 67.1 us
  blocking collectives  23.6 us (35%)
  waiting for transfers between devices  18.2 us (27%)
  starting transfers between devices  12.6 us (18%)
  Pallas kernels  11.9 us (17%)
  between operations  0.78 us (1%)
    all_to_all x2, blocking collectives, by_channel(): lax.all_to_all(x, ('row', 'col'), 0, 0, axis_index_groups=[ORDER], tiled=...  23.6 us
    all_to_all x2, waiting for transfers between devices, by_channel(): lax.all_to_all(x, ('row', 'col'), 0, 0, axis_index_groups=[ORDER], tiled=...  18.2 us
    all_to_all x2, starting transfers between devices, by_channel(): lax.all_to_all(x, ('row', 'col'), 0, 0, axis_index_groups=[ORDER], tiled=...  12.6 us
    pallas_call x7, Pallas kernels, call(): pl.pallas_call(body, out_shape=tuple(outs + far_shapes), in_specs=[near_s...  11.9 us
  transfers between devices with their start and end apart: 2, of which 2 were waited for; matrix products, arithmetic and copies ran while one was open for 0% of the time, Pallas kernels for 6%

profile of v5, /device:TPU:0, one launch (start us, length us, event | category | flops | bytes accessed | tf_op | source)
XLA Modules:
  0.0 67.1 jit_solution(15930539573887233231)
XLA Ops:
  0.6 0.0 copy-start.5
  0.6 0.0 copy-start
  0.7 0.0 copy-start.2
  0.7 0.0 copy-start.3
  0.7 0.0 copy-start.4
  0.7 0.0 copy-start.6
  0.7 2.6 %shard_map.95 = bf16[16,16,1024]{2,1,0:T(8,128)(2,1)} custom-call(s32[1,128]{1,0:T(1,128)} %bitcast.18, f32[1,128]{1,0:T(1,128)} %bitcast.12, bf16[128,512]{1,0:T(8,128)(2,1)} %refs_5_.3, bf16[1024,128]{1,0:T(8,128)(2,1)} %bitcast.7), custom_call_target="tpu_custom_call" | custom-call | flops 134217728 | bytes 918528 | tf_op jit(solution)/shard_map/pallas_call | solution.py:446
  3.3 7.6 %all-to-all-start = ((bf16[16,16,1024]{2,1,0:T(8,128)(2,1)}), bf16[16,16,1024]{2,1,0:T(8,128)(2,1)S(1)}, u32[]{:S(2)}, u32[]{:S(2)}) async-start(bf16[16,16,1024]{2,1,0:T(8,128)(2,1)} %shard_map.95), calls=%async_computation | async-start | bytes 1048576 | tf_op jit(solution)/shard_map/all_to_all | solution.py:468
  10.9 0.0 copy-done.5
  10.9 0.0 copy-done
  10.9 0.0 copy-done.2
  10.9 0.0 copy-done.3
  10.9 0.0 copy-done.4
  11.0 0.0 copy-done.6
  11.0 1.3 %shard_map.96.refs_1_ = f32[128,1024]{1,0:T(8,128)S(1)} custom-call(bf16[1024,128]{1,0:T(8,128)(2,1)S(1)} %bitcast.8, bf16[1024,128]{1,0:T(8,128)(2,1)S(1)} %bitcast.10, f32[1,128]{1,0:T(1,128)S(1)} %bitcast.13, bf16[128,128]{1,0:T(8,128)(2,1)S(1)} %copy-done.3, f32[1,128]{1,0:T(1,128)S(1)} %bitcast.16, bf16[128,128]{1,0:T(8,128)(2,1)S(1)} %copy-done.4), custom_call_target="tpu_custom_call" | custom-call | flops 67108864 | bytes 1115136 | tf_op jit(solution)/shard_map/pallas_call | solution.py:446
  12.3 9.6 %all-to-all-done.refs_0_ = bf16[16,16,1024]{2,1,0:T(8,128)(2,1)S(1)} async-done(((bf16[16,16,1024]{2,1,0:T(8,128)(2,1)}), bf16[16,16,1024]{2,1,0:T(8,128)(2,1)S(1)}, u32[]{:S(2)}, u32[]{:S(2)}) %all-to-all-start) | async-done | bytes 524320 | tf_op jit(solution)/shard_map/all_to_all | solution.py:468
  21.9 1.2 %shard_map.97 = (bf16[16,16,512]{2,1,0:T(8,128)(2,1)S(1)}, bf16[8,128,128]{2,1,0:T(8,128)(2,1)S(1)}, bf16[8,128,128]{2,1,0:T(8,128)(2,1)S(1)}) custom-call(bf16[16,16,1024]{2,1,0:T(8,128)(2,1)S(1)} %all-to-all-done.refs_0_), custom_call_target="tpu_custom_call" | custom-call | flops 33554432 | bytes 1310720 | tf_op jit(solution)/shard_map/pallas_call | solution.py:446
  23.1 12.2 %all_to_all.20.refs_0_ = bf16[16,16,512]{2,1,0:T(8,128)(2,1)S(1)} all-to-all(bf16[16,16,512]{2,1,0:T(8,128)(2,1)S(1)} %get-tuple-element.22), channel_id=1, replica_groups={{6,7,11,0,12,2,3,5,14,8,1,10,9,13,4,15},{22,23,27,16,28,18,19,21,30,24,..., dimensions={0} | all-to-all | bytes 524288 | tf_op jit(solution)/shard_map/all_to_all | solution.py:468
  35.4 0.4 shard_map.98
  35.7 11.3 %all_to_all.21.refs_0_ = bf16[16,16,512]{2,1,0:T(8,128)(2,1)S(1)} all-to-all(bf16[16,16,512]{2,1,0:T(8,128)(2,1)S(1)} %shard_map.98), channel_id=1, replica_groups={{6,7,11,0,12,2,3,5,14,8,1,10,9,13,4,15},{22,23,27,16,28,18,19,21,30,24,..., dimensions={0} | all-to-all | bytes 524288 | tf_op jit(solution)/shard_map/all_to_all | solution.py:468
  47.0 0.0 copy-start.1
  47.0 0.0 copy-start.7
  47.0 2.2 %shard_map.99 = bf16[16,16,1024]{2,1,0:T(8,128)(2,1)} custom-call(bf16[16,16,512]{2,1,0:T(8,128)(2,1)S(1)} %all_to_all.21.refs_0_, bf16[8,128,128]{2,1,0:T(8,128)(2,1)S(1)} %get-tuple-element.24.refs_1_, bf16[8,128,128]{2,1,0:T(8,128)(2,1)S(1)} %get-tuple-element.25.refs_2_), custom_call_target="tpu_custom_call" | custom-call | flops 67108864 | bytes 1310720 | tf_op jit(solution)/shard_map/pallas_call | solution.py:446
  49.2 5.1 %all-to-all-start.3 = ((bf16[16,16,1024]{2,1,0:T(8,128)(2,1)}), bf16[16,16,1024]{2,1,0:T(8,128)(2,1)S(1)}, u32[]{:S(2)}, u32[]{:S(2)}) async-start(bf16[16,16,1024]{2,1,0:T(8,128)(2,1)} %shard_map.99), calls=%async_computation.3 | async-start | bytes 1048576 | tf_op jit(solution)/shard_map/all_to_all | solution.py:468
  54.3 0.0 copy-done.1
  54.3 0.0 copy-done.7
  54.3 2.6 %shard_map.100 = (f32[128,1024]{1,0:T(8,128)S(1)}, f32[1,1024]{1,0:T(1,128)S(1)}, bf16[5,128,1024]{2,1,0:T(8,128)(2,1)S(1)}, bf16[1024,128]{1,0:T(8,128)(2,1)}) custom-call(bf16[16,16,512]{2,1,0:T(8,128)(2,1)S(1)} %all_to_all.20.refs_0_, f32[1,128]{1,0:T(1,128)S(1)} %bitcast.17, bf16[128,128]{1,0:T(8,128)(2,1)S(1)} %copy-done.4, ...), custom_call_target="tpu_custom_call" | custom-call | flops 201326592 | bytes 3085824 | tf_op jit(solution)/shard_map/pallas_call | solution.py:446
  56.9 8.6 %all-to-all-done.3.refs_0_ = bf16[16,16,1024]{2,1,0:T(8,128)(2,1)S(1)} async-done(((bf16[16,16,1024]{2,1,0:T(8,128)(2,1)}), bf16[16,16,1024]{2,1,0:T(8,128)(2,1)S(1)}, u32[]{:S(2)}, u32[]{:S(2)}) %all-to-all-start.3) | async-done | bytes 524320 | tf_op jit(solution)/shard_map/all_to_all | solution.py:468
  65.4 1.7 %shard_map.101 = f32[1024,128]{1,0:T(8,128)} custom-call(bf16[16,16,1024]{2,1,0:T(8,128)(2,1)S(1)} %all-to-all-done.3.refs_0_, bf16[5,128,1024]{2,1,0:T(8,128)(2,1)S(1)} %get-tuple-element.31.refs_1_, f32[128,1024]{1,0:T(8,128)S(1)} %get-tuple-element.32.refs_2_, f32[1,1024]{1,0:T(1,128)S(1)} %get-tuple-element.33.refs_3_, f32[1,128]{1,0:T(1,128)S(1)} %bitcast.15, ...), custom_call_target="tpu_custom_call" | custom-call | flops 167772160 | bytes 3052032 | tf_op jit(solution)/shard_map/pallas_call | solution.py:446
Async XLA Ops:
  0.6 10.3 %copy-start.5 = (f32[128]{0:T(128)S(1)}, f32[128]{0:T(128)}, u32[]{:S(2)}) copy-start(f32[128]{0:T(128)} %param.11) | copy-start | bytes 1540
  0.6 10.3 %copy-start = (bf16[32,32,128]{2,1,0:T(8,128)(2,1)S(1)}, bf16[32,32,128]{2,1,0:T(8,128)(2,1)}, u32[]{:S(2)}) copy-start(bf16[32,32,128]{2,1,0:T(8,128)(2,1)} %param.8) | copy-start | bytes 786436
  0.7 10.3 %copy-start.2 = (bf16[32,32,128]{2,1,0:T(8,128)(2,1)S(1)}, bf16[32,32,128]{2,1,0:T(8,128)(2,1)}, u32[]{:S(2)}) copy-start(bf16[32,32,128]{2,1,0:T(8,128)(2,1)} %param.9) | copy-start | bytes 786436
  0.7 10.3 %copy-start.3 = (bf16[128,128]{1,0:T(8,128)(2,1)S(1)}, bf16[128,128]{1,0:T(8,128)(2,1)}, u32[]{:S(2)}) copy-start(bf16[128,128]{1,0:T(8,128)(2,1)} %refs_6_.1) | copy-start | bytes 98308
  0.7 10.3 %copy-start.4 = (bf16[128,128]{1,0:T(8,128)(2,1)S(1)}, bf16[128,128]{1,0:T(8,128)(2,1)}, u32[]{:S(2)}) copy-start(bf16[128,128]{1,0:T(8,128)(2,1)} %refs_2_.3) | copy-start | bytes 98308
  0.7 10.3 %copy-start.6 = (f32[128]{0:T(128)S(1)}, f32[128]{0:T(128)}, u32[]{:S(2)}) copy-start(f32[128]{0:T(128)} %param.14) | copy-start | bytes 1540
  3.3 18.5 %all-to-all-start = ((bf16[16,16,1024]{2,1,0:T(8,128)(2,1)}), bf16[16,16,1024]{2,1,0:T(8,128)(2,1)S(1)}, u32[]{:S(2)}, u32[]{:S(2)}) async-start(bf16[16,16,1024]{2,1,0:T(8,128)(2,1)} %shard_map.95), calls=%async_computation | async-start | bytes 1048576 | tf_op jit(solution)/shard_map/all_to_all | solution.py:468
  47.0 7.3 %copy-start.1 = (bf16[128,512]{1,0:T(8,128)(2,1)S(1)}, bf16[128,512]{1,0:T(8,128)(2,1)}, u32[]{:S(2)}) copy-start(bf16[128,512]{1,0:T(8,128)(2,1)} %refs_5_.3) | copy-start | bytes 393220
  47.0 7.3 %copy-start.7 = (s32[128]{0:T(128)S(1)}, s32[128]{0:T(128)}, u32[]{:S(2)}) copy-start(s32[128]{0:T(128)} %param.10) | copy-start | bytes 1540
  49.2 16.2 %all-to-all-start.3 = ((bf16[16,16,1024]{2,1,0:T(8,128)(2,1)}), bf16[16,16,1024]{2,1,0:T(8,128)(2,1)S(1)}, u32[]{:S(2)}, u32[]{:S(2)}) async-start(bf16[16,16,1024]{2,1,0:T(8,128)(2,1)} %shard_map.99), calls=%async_computation.3 | async-start | bytes 1048576 | tf_op jit(solution)/shard_map/all_to_all | solution.py:468

commit v6 on v5

--- a/solution.py
+++ b/solution.py
@@ -107,8 +107,11 @@
 F32 = jnp.float32
 BF16 = jnp.bfloat16
 LANES = 128
-ORDER = (6, 7, 11, 0, 12, 2, 3, 5, 14, 8, 1, 10, 9, 13, 4, 15)
-PLACE = tuple(ORDER.index(device) for device in range(len(ORDER)))
+FIRST = (14, 15, 3, 12, 4, 10, 11, 13, 6, 0, 9, 2, 1, 5, 8, 7)
+LATER = (6, 7, 11, 0, 12, 2, 3, 5, 14, 8, 1, 10, 9, 13, 4, 15)
+FIRST_PLACE = tuple(FIRST.index(device) for device in range(len(FIRST)))
+LATER_PLACE = tuple(LATER.index(device) for device in range(len(LATER)))
+HOLDER = tuple(LATER.index(device) for device in FIRST)
 
 
 def dot(a, b, dims):
@@ -176,7 +179,7 @@
     return normed, unit, inv
 
 
-def project_kernel(tile, parts, valid, in_gain, proj_weight, pair, out):
+def project_kernel(tile, parts, pair, proj_weight, valid, in_gain, out):
     cells, channels = pair.ref.shape
     hidden = proj_weight.ref.shape[1] // 4
     shards, both, _ = out.ref.shape
@@ -219,7 +222,7 @@
         x = jnp.concatenate(
             [
                 jnp.concatenate(
-                    [recv_ref[PLACE[grid_rows * r + c], :, g * LANES : (g + 1) * LANES] for c in range(grid_rows)], axis=1
+                    [recv_ref[FIRST_PLACE[grid_rows * r + c], :, g * LANES : (g + 1) * LANES] for c in range(grid_rows)], axis=1
                 )
                 for g in range(groups)
             ],
@@ -256,28 +259,27 @@
         y = dot(x.astype(BF16), swap, (1, 0)).astype(BF16)
         for g in range(half):
             for c in range(grid_rows):
-                out_ref[PLACE[grid_rows * r + c], :, g * LANES : (g + 1) * LANES] = y[
+                out_ref[LATER_PLACE[grid_rows * r + c], :, g * LANES : (g + 1) * LANES] = y[
                     g * both : (g + 1) * both, c * LANES : (c + 1) * LANES
                 ]
 
 
 def halves_of(recv_ref):
-    shards, both, width = recv_ref.shape
-    x = recv_ref[...].astype(F32)
-    rows = shards * both // 2
+    per = recv_ref.shape[1] // 2
+    blocks = [recv_ref[holder].astype(F32) for holder in HOLDER]
     return jnp.concatenate(
-        [x[:, : both // 2].reshape(rows, width), x[:, both // 2 :].reshape(rows, width)], axis=1
+        [jnp.concatenate([b[k * per : (k + 1) * per] for b in blocks], axis=0) for k in range(2)], axis=1
     )
 
 
 def d_tri_kernel(recv_ref, q_ref, out_ref):
-    shards, both, width = recv_ref.shape
+    _, both, width = recv_ref.shape
+    per = both // 2
     unit, inv = unit_rows(halves_of(recv_ref))
     d_tri = unit_back(q_ref[...], unit, inv)
-    out_ref[...] = jnp.concatenate(
-        [d_tri[:, :width].reshape(shards, both // 2, width), d_tri[:, width:].reshape(shards, both // 2, width)],
-        axis=1,
-    ).astype(BF16)
+    for shard, holder in enumerate(HOLDER):
+        rows = d_tri[shard * per : (shard + 1) * per]
+        out_ref[holder] = jnp.concatenate([rows[:, :width], rows[:, width:]], axis=0).astype(BF16)
 
 
 def update_kernel(
@@ -317,7 +319,7 @@
         x = jnp.concatenate(
             [
                 jnp.concatenate(
-                    [recv_ref[PLACE[grid_rows * r + c], :, g * LANES : (g + 1) * LANES] for c in range(grid_rows)], axis=1
+                    [recv_ref[LATER_PLACE[grid_rows * r + c], :, g * LANES : (g + 1) * LANES] for c in range(grid_rows)], axis=1
                 )
                 for g in range(half)
             ],
@@ -352,7 +354,7 @@
         )
         y = dot(x.astype(BF16), swap, (1, 0)).astype(BF16)
         for c in range(grid_rows):
-            place = PLACE[grid_rows * r + c]
+            place = LATER_PLACE[grid_rows * r + c]
             for g in range(groups):
                 out.ref[place, :, g * LANES : (g + 1) * LANES] = y[
                     g * both : (g + 1) * both, c * LANES : (c + 1) * LANES
@@ -361,15 +363,16 @@
 
 
 def pair_grad_kernel(parts, recv_ref, factor_ref, unit_ref, inv_ref, in_gain, proj_weight, gate_weight, out):
-    shards, both, cells = recv_ref.shape
-    hidden = shards * both // 2
+    _, both, cells = recv_ref.shape
     width = cells // parts
     gain = spread(column(in_gain.ready()[...]), width)
     weights, gate_weights = proj_weight.ready()[...], gate_weight.ready()[...]
     for part in range(parts):
         lanes = slice(part * width, (part + 1) * width)
-        x = recv_ref[:, :, lanes].astype(F32)
-        grads = (x[:, : both // 2].reshape(hidden, width), x[:, both // 2 :].reshape(hidden, width))
+        blocks = [recv_ref[holder, :, lanes].astype(F32) for holder in HOLDER]
+        grads = [
+            jnp.concatenate([b[k * both // 2 : (k + 1) * both // 2] for b in blocks], axis=0) for k in range(2)
+        ]
         d_proj = jnp.concatenate(
             [
                 (grad * factor_ref[2 * side + k, :, lanes].astype(F32)).astype(BF16)
@@ -465,7 +468,7 @@
     per = hidden // devices
     n = tile * grid_rows
     shape = lambda dims, dtype: jax.ShapeDtypeStruct(dims, dtype)
-    whole = lambda x: lax.all_to_all(x, ("row", "col"), 0, 0, axis_index_groups=[ORDER], tiled=True)
+    exchange = lambda x, order: lax.all_to_all(x, ("row", "col"), 0, 0, axis_index_groups=[order], tiled=True)
     flat = pair.reshape(cells, channels)
     flat_cot = cotangent.reshape(cells, channels)
     valid_row = valid.reshape(1, -1)
@@ -479,12 +482,12 @@
         [],
         (),
         2 * cells * channels * 4 * hidden,
-        far=(valid_row, in_row, proj_weight, flat),
+        far=(flat, proj_weight, valid_row, in_row),
         far_outs=[(shape((devices, both, cells), BF16), 4, 0)],
         room=62,
     )
     sides, flat_2, flat_cot_2 = lax.optimization_barrier((sides, flat, flat_cot))
-    sides = whole(sides)
+    sides = exchange(sides, FIRST)
     (q,) = call(
         gate_kernel,
         [plane],
@@ -500,14 +503,14 @@
         2 * per * n * n * n,
         [pltpu.VMEM((n * both, n), F32), pltpu.VMEM((n * per, n), F32)],
     )
-    tri = whole(tri)
+    tri = exchange(tri, LATER)
     (d_tri,) = call(
         d_tri_kernel,
         [shape((devices, both, cells // 2), BF16)],
         (tri, q),
         20 * cells * hidden,
     )
-    d_tri = whole(d_tri)
+    d_tri = exchange(d_tri, LATER)
     (d_sides,) = call(
         functools.partial(sides_kernel, grid_rows),
         [],
@@ -517,7 +520,7 @@
         far_outs=[(shape((devices, both, cells), BF16), devices, 0)],
     )
     d_sides, flat_4, flat_cot_4, tri = lax.optimization_barrier((d_sides, flat, flat_cot, tri))
-    d_sides = whole(d_sides)
+    d_sides = exchange(d_sides, LATER)
     unit, inv, factors, update = call(
         functools.partial(update_kernel, tile),
         [plane, shape((1, cells), F32), shape((5, hidden, cells), BF16)],

time: 68.2 us -> 68 us (level)
  blocking collectives: 23.6 us -> 22.9 us
where the time goes in v6:
time: 68 us; the launch traced here: 66.9 us
  blocking collectives  22.9 us (34%)
  waiting for transfers between devices  18.5 us (27%)
  starting transfers between devices  12.9 us (19%)
  Pallas kernels  11.8 us (17%)
  between operations  0.78 us (1%)
    all_to_all x2, blocking collectives, by_channel(): lax.all_to_all(x, ('row', 'col'), 0, 0, axis_index_groups=[order], tiled=...  22.9 us
    all_to_all x2, waiting for transfers between devices, by_channel(): lax.all_to_all(x, ('row', 'col'), 0, 0, axis_index_groups=[order], tiled=...  18.5 us
    all_to_all x2, starting transfers between devices, by_channel(): lax.all_to_all(x, ('row', 'col'), 0, 0, axis_index_groups=[order], tiled=...  12.9 us
    pallas_call x7, Pallas kernels, call(): pl.pallas_call(body, out_shape=tuple(outs + far_shapes), in_specs=[near_s...  11.8 us
  transfers between devices with their start and end apart: 2, of which 2 were waited for; matrix products, arithmetic and copies ran while one was open for 0% of the time, Pallas kernels for 6%

profile of v6, /device:TPU:0, one launch (start us, length us, event | category | flops | bytes accessed | tf_op | source)
XLA Modules:
  0.0 66.9 jit_solution(5545911468881064247)
XLA Ops:
  0.6 0.0 copy-start.5
  0.6 0.0 copy-start
  0.7 0.0 copy-start.2
  0.7 0.0 copy-start.3
  0.7 0.0 copy-start.4
  0.7 0.0 copy-start.6
  0.7 2.6 %shard_map.95 = bf16[16,16,1024]{2,1,0:T(8,128)(2,1)} custom-call(bf16[1024,128]{1,0:T(8,128)(2,1)} %bitcast.7, bf16[128,512]{1,0:T(8,128)(2,1)} %refs_5_.3, s32[1,128]{1,0:T(1,128)} %bitcast.18, f32[1,128]{1,0:T(1,128)} %bitcast.12), custom_call_target="tpu_custom_call" | custom-call | flops 134217728 | bytes 918528 | tf_op jit(solution)/shard_map/pallas_call | solution.py:449
  3.3 7.8 %all-to-all-start = ((bf16[16,16,1024]{2,1,0:T(8,128)(2,1)}), bf16[16,16,1024]{2,1,0:T(8,128)(2,1)S(1)}, u32[]{:S(2)}, u32[]{:S(2)}) async-start(bf16[16,16,1024]{2,1,0:T(8,128)(2,1)} %shard_map.95), calls=%async_computation | async-start | bytes 1048576 | tf_op jit(solution)/shard_map/all_to_all | solution.py:471
  11.1 0.0 copy-done.5
  11.1 0.0 copy-done
  11.1 0.0 copy-done.2
  11.1 0.0 copy-done.3
  11.1 0.0 copy-done.4
  11.1 0.0 copy-done.6
  11.2 1.3 %shard_map.96.refs_1_ = f32[128,1024]{1,0:T(8,128)S(1)} custom-call(bf16[1024,128]{1,0:T(8,128)(2,1)S(1)} %bitcast.8, bf16[1024,128]{1,0:T(8,128)(2,1)S(1)} %bitcast.10, f32[1,128]{1,0:T(1,128)S(1)} %bitcast.13, bf16[128,128]{1,0:T(8,128)(2,1)S(1)} %copy-done.3, f32[1,128]{1,0:T(1,128)S(1)} %bitcast.16, bf16[128,128]{1,0:T(8,128)(2,1)S(1)} %copy-done.4), custom_call_target="tpu_custom_call" | custom-call | flops 67108864 | bytes 1115136 | tf_op jit(solution)/shard_map/pallas_call | solution.py:449
  12.4 10.0 %all-to-all-done.refs_0_ = bf16[16,16,1024]{2,1,0:T(8,128)(2,1)S(1)} async-done(((bf16[16,16,1024]{2,1,0:T(8,128)(2,1)}), bf16[16,16,1024]{2,1,0:T(8,128)(2,1)S(1)}, u32[]{:S(2)}, u32[]{:S(2)}) %all-to-all-start) | async-done | bytes 524320 | tf_op jit(solution)/shard_map/all_to_all | solution.py:471
  22.4 1.2 %shard_map.97 = (bf16[16,16,512]{2,1,0:T(8,128)(2,1)S(1)}, bf16[8,128,128]{2,1,0:T(8,128)(2,1)S(1)}, bf16[8,128,128]{2,1,0:T(8,128)(2,1)S(1)}) custom-call(bf16[16,16,1024]{2,1,0:T(8,128)(2,1)S(1)} %all-to-all-done.refs_0_), custom_call_target="tpu_custom_call" | custom-call | flops 33554432 | bytes 1310720 | tf_op jit(solution)/shard_map/pallas_call | solution.py:449
  23.6 11.6 %all_to_all.20.refs_0_ = bf16[16,16,512]{2,1,0:T(8,128)(2,1)S(1)} all-to-all(bf16[16,16,512]{2,1,0:T(8,128)(2,1)S(1)} %get-tuple-element.22), channel_id=1, replica_groups={{6,7,11,0,12,2,3,5,14,8,1,10,9,13,4,15},{22,23,27,16,28,18,19,21,30,24,..., dimensions={0} | all-to-all | bytes 524288 | tf_op jit(solution)/shard_map/all_to_all | solution.py:471
  35.2 0.4 shard_map.98
  35.5 11.3 %all_to_all.21.refs_0_ = bf16[16,16,512]{2,1,0:T(8,128)(2,1)S(1)} all-to-all(bf16[16,16,512]{2,1,0:T(8,128)(2,1)S(1)} %shard_map.98), channel_id=1, replica_groups={{6,7,11,0,12,2,3,5,14,8,1,10,9,13,4,15},{22,23,27,16,28,18,19,21,30,24,..., dimensions={0} | all-to-all | bytes 524288 | tf_op jit(solution)/shard_map/all_to_all | solution.py:471
  46.9 0.0 copy-start.1
  46.9 0.0 copy-start.7
  46.9 2.2 %shard_map.99 = bf16[16,16,1024]{2,1,0:T(8,128)(2,1)} custom-call(bf16[16,16,512]{2,1,0:T(8,128)(2,1)S(1)} %all_to_all.21.refs_0_, bf16[8,128,128]{2,1,0:T(8,128)(2,1)S(1)} %get-tuple-element.24.refs_1_, bf16[8,128,128]{2,1,0:T(8,128)(2,1)S(1)} %get-tuple-element.25.refs_2_), custom_call_target="tpu_custom_call" | custom-call | flops 67108864 | bytes 1310720 | tf_op jit(solution)/shard_map/pallas_call | solution.py:449
  49.1 5.1 %all-to-all-start.3 = ((bf16[16,16,1024]{2,1,0:T(8,128)(2,1)}), bf16[16,16,1024]{2,1,0:T(8,128)(2,1)S(1)}, u32[]{:S(2)}, u32[]{:S(2)}) async-start(bf16[16,16,1024]{2,1,0:T(8,128)(2,1)} %shard_map.99), calls=%async_computation.3 | async-start | bytes 1048576 | tf_op jit(solution)/shard_map/all_to_all | solution.py:471
  54.1 0.0 copy-done.1
  54.1 0.0 copy-done.7
  54.1 2.6 %shard_map.100 = (f32[128,1024]{1,0:T(8,128)S(1)}, f32[1,1024]{1,0:T(1,128)S(1)}, bf16[5,128,1024]{2,1,0:T(8,128)(2,1)S(1)}, bf16[1024,128]{1,0:T(8,128)(2,1)}) custom-call(bf16[16,16,512]{2,1,0:T(8,128)(2,1)S(1)} %all_to_all.20.refs_0_, f32[1,128]{1,0:T(1,128)S(1)} %bitcast.17, bf16[128,128]{1,0:T(8,128)(2,1)S(1)} %copy-done.4, ...), custom_call_target="tpu_custom_call" | custom-call | flops 201326592 | bytes 3085824 | tf_op jit(solution)/shard_map/pallas_call | solution.py:449
  56.7 8.6 %all-to-all-done.3.refs_0_ = bf16[16,16,1024]{2,1,0:T(8,128)(2,1)S(1)} async-done(((bf16[16,16,1024]{2,1,0:T(8,128)(2,1)}), bf16[16,16,1024]{2,1,0:T(8,128)(2,1)S(1)}, u32[]{:S(2)}, u32[]{:S(2)}) %all-to-all-start.3) | async-done | bytes 524320 | tf_op jit(solution)/shard_map/all_to_all | solution.py:471
  65.3 1.7 %shard_map.101 = f32[1024,128]{1,0:T(8,128)} custom-call(bf16[16,16,1024]{2,1,0:T(8,128)(2,1)S(1)} %all-to-all-done.3.refs_0_, bf16[5,128,1024]{2,1,0:T(8,128)(2,1)S(1)} %get-tuple-element.31.refs_1_, f32[128,1024]{1,0:T(8,128)S(1)} %get-tuple-element.32.refs_2_, f32[1,1024]{1,0:T(1,128)S(1)} %get-tuple-element.33.refs_3_, f32[1,128]{1,0:T(1,128)S(1)} %bitcast.15, ...), custom_call_target="tpu_custom_call" | custom-call | flops 167772160 | bytes 3052032 | tf_op jit(solution)/shard_map/pallas_call | solution.py:449
Async XLA Ops:
  0.6 10.5 %copy-start.5 = (f32[128]{0:T(128)S(1)}, f32[128]{0:T(128)}, u32[]{:S(2)}) copy-start(f32[128]{0:T(128)} %param.11) | copy-start | bytes 1540
  0.6 10.5 %copy-start = (bf16[32,32,128]{2,1,0:T(8,128)(2,1)S(1)}, bf16[32,32,128]{2,1,0:T(8,128)(2,1)}, u32[]{:S(2)}) copy-start(bf16[32,32,128]{2,1,0:T(8,128)(2,1)} %param.8) | copy-start | bytes 786436
  0.7 10.5 %copy-start.2 = (bf16[32,32,128]{2,1,0:T(8,128)(2,1)S(1)}, bf16[32,32,128]{2,1,0:T(8,128)(2,1)}, u32[]{:S(2)}) copy-start(bf16[32,32,128]{2,1,0:T(8,128)(2,1)} %param.9) | copy-start | bytes 786436
  0.7 10.5 %copy-start.3 = (bf16[128,128]{1,0:T(8,128)(2,1)S(1)}, bf16[128,128]{1,0:T(8,128)(2,1)}, u32[]{:S(2)}) copy-start(bf16[128,128]{1,0:T(8,128)(2,1)} %refs_6_.1) | copy-start | bytes 98308
  0.7 10.5 %copy-start.4 = (bf16[128,128]{1,0:T(8,128)(2,1)S(1)}, bf16[128,128]{1,0:T(8,128)(2,1)}, u32[]{:S(2)}) copy-start(bf16[128,128]{1,0:T(8,128)(2,1)} %refs_2_.1) | copy-start | bytes 98308
  0.7 10.5 %copy-start.6 = (f32[128]{0:T(128)S(1)}, f32[128]{0:T(128)}, u32[]{:S(2)}) copy-start(f32[128]{0:T(128)} %param.14) | copy-start | bytes 1540
  3.3 19.1 %all-to-all-start = ((bf16[16,16,1024]{2,1,0:T(8,128)(2,1)}), bf16[16,16,1024]{2,1,0:T(8,128)(2,1)S(1)}, u32[]{:S(2)}, u32[]{:S(2)}) async-start(bf16[16,16,1024]{2,1,0:T(8,128)(2,1)} %shard_map.95), calls=%async_computation | async-start | bytes 1048576 | tf_op jit(solution)/shard_map/all_to_all | solution.py:471
  46.9 7.3 %copy-start.1 = (bf16[128,512]{1,0:T(8,128)(2,1)S(1)}, bf16[128,512]{1,0:T(8,128)(2,1)}, u32[]{:S(2)}) copy-start(bf16[128,512]{1,0:T(8,128)(2,1)} %refs_5_.3) | copy-start | bytes 393220
  46.9 7.3 %copy-start.7 = (s32[128]{0:T(128)S(1)}, s32[128]{0:T(128)}, u32[]{:S(2)}) copy-start(s32[128]{0:T(128)} %param.10) | copy-start | bytes 1540
  49.1 16.2 %all-to-all-start.3 = ((bf16[16,16,1024]{2,1,0:T(8,128)(2,1)}), bf16[16,16,1024]{2,1,0:T(8,128)(2,1)S(1)}, u32[]{:S(2)}, u32[]{:S(2)}) async-start(bf16[16,16,1024]{2,1,0:T(8,128)(2,1)} %shard_map.99), calls=%async_computation.3 | async-start | bytes 1048576 | tf_op jit(solution)/shard_map/all_to_all | solution.py:471

commit v7 on v6

--- a/solution.py
+++ b/solution.py
@@ -108,7 +108,7 @@
 BF16 = jnp.bfloat16
 LANES = 128
 FIRST = (14, 15, 3, 12, 4, 10, 11, 13, 6, 0, 9, 2, 1, 5, 8, 7)
-LATER = (6, 7, 11, 0, 12, 2, 3, 5, 14, 8, 1, 10, 9, 13, 4, 15)
+LATER = (14, 15, 3, 4, 13, 10, 11, 12, 6, 0, 9, 2, 1, 5, 8, 7)
 FIRST_PLACE = tuple(FIRST.index(device) for device in range(len(FIRST)))
 LATER_PLACE = tuple(LATER.index(device) for device in range(len(LATER)))
 HOLDER = tuple(LATER.index(device) for device in FIRST)

time: 68 us -> 66.9 us (0.984)
  the two profiles are of different devices: /device:TPU:0 before, /device:TPU:1 now
where the time goes in v7:
time: 66.9 us; the launch traced here: 66.5 us
  blocking collectives  22 us (33%)
  waiting for transfers between devices  19.2 us (29%)
  starting transfers between devices  12.7 us (19%)
  Pallas kernels  11.8 us (18%)
  between operations  0.78 us (1%)
    all_to_all x2, blocking collectives, by_channel(): lax.all_to_all(x, ('row', 'col'), 0, 0, axis_index_groups=[order], tiled=...  22 us
    all_to_all x2, waiting for transfers between devices, by_channel(): lax.all_to_all(x, ('row', 'col'), 0, 0, axis_index_groups=[order], tiled=...  19.2 us
    all_to_all x2, starting transfers between devices, by_channel(): lax.all_to_all(x, ('row', 'col'), 0, 0, axis_index_groups=[order], tiled=...  12.7 us
    pallas_call x7, Pallas kernels, call(): pl.pallas_call(body, out_shape=tuple(outs + far_shapes), in_specs=[near_s...  11.8 us
  transfers between devices with their start and end apart: 2, of which 2 were waited for; matrix products, arithmetic and copies ran while one was open for 0% of the time, Pallas kernels for 6%

profile of v7, /device:TPU:1, one launch (start us, length us, event | category | flops | bytes accessed | tf_op | source)
XLA Modules:
  0.0 66.5 jit_solution(17247507129307146068)
XLA Ops:
  0.6 0.0 copy-start.5
  0.6 0.0 copy-start
  0.7 0.0 copy-start.2
  0.7 0.0 copy-start.3
  0.7 0.0 copy-start.4
  0.7 0.0 copy-start.6
  0.7 2.6 %shard_map.95 = bf16[16,16,1024]{2,1,0:T(8,128)(2,1)} custom-call(bf16[1024,128]{1,0:T(8,128)(2,1)} %bitcast.7, bf16[128,512]{1,0:T(8,128)(2,1)} %refs_5_.3, s32[1,128]{1,0:T(1,128)} %bitcast.18, f32[1,128]{1,0:T(1,128)} %bitcast.12), custom_call_target="tpu_custom_call" | custom-call | flops 134217728 | bytes 918528 | tf_op jit(solution)/shard_map/pallas_call | solution.py:449
  3.3 7.5 %all-to-all-start = ((bf16[16,16,1024]{2,1,0:T(8,128)(2,1)}), bf16[16,16,1024]{2,1,0:T(8,128)(2,1)S(1)}, u32[]{:S(2)}, u32[]{:S(2)}) async-start(bf16[16,16,1024]{2,1,0:T(8,128)(2,1)} %shard_map.95), calls=%async_computation | async-start | bytes 1048576 | tf_op jit(solution)/shard_map/all_to_all | solution.py:471
  10.7 0.0 copy-done.5
  10.7 0.0 copy-done
  10.7 0.0 copy-done.2
  10.7 0.0 copy-done.3
  10.7 0.0 copy-done.4
  10.8 0.0 copy-done.6
  10.8 1.3 %shard_map.96.refs_1_ = f32[128,1024]{1,0:T(8,128)S(1)} custom-call(bf16[1024,128]{1,0:T(8,128)(2,1)S(1)} %bitcast.8, bf16[1024,128]{1,0:T(8,128)(2,1)S(1)} %bitcast.10, f32[1,128]{1,0:T(1,128)S(1)} %bitcast.13, bf16[128,128]{1,0:T(8,128)(2,1)S(1)} %copy-done.3, f32[1,128]{1,0:T(1,128)S(1)} %bitcast.16, bf16[128,128]{1,0:T(8,128)(2,1)S(1)} %copy-done.4), custom_call_target="tpu_custom_call" | custom-call | flops 67108864 | bytes 1115136 | tf_op jit(solution)/shard_map/pallas_call | solution.py:449
  12.1 10.8 %all-to-all-done.refs_0_ = bf16[16,16,1024]{2,1,0:T(8,128)(2,1)S(1)} async-done(((bf16[16,16,1024]{2,1,0:T(8,128)(2,1)}), bf16[16,16,1024]{2,1,0:T(8,128)(2,1)S(1)}, u32[]{:S(2)}, u32[]{:S(2)}) %all-to-all-start) | async-done | bytes 524320 | tf_op jit(solution)/shard_map/all_to_all | solution.py:471
  22.8 1.2 %shard_map.97 = (bf16[16,16,512]{2,1,0:T(8,128)(2,1)S(1)}, bf16[8,128,128]{2,1,0:T(8,128)(2,1)S(1)}, bf16[8,128,128]{2,1,0:T(8,128)(2,1)S(1)}) custom-call(bf16[16,16,1024]{2,1,0:T(8,128)(2,1)S(1)} %all-to-all-done.refs_0_), custom_call_target="tpu_custom_call" | custom-call | flops 33554432 | bytes 1310720 | tf_op jit(solution)/shard_map/pallas_call | solution.py:449
  24.1 10.9 %all_to_all.20.refs_0_ = bf16[16,16,512]{2,1,0:T(8,128)(2,1)S(1)} all-to-all(bf16[16,16,512]{2,1,0:T(8,128)(2,1)S(1)} %get-tuple-element.22), channel_id=1, replica_groups={{14,15,3,4,13,10,11,12,6,0,9,2,1,5,8,7},{30,31,19,20,29,26,27,28,22,16,..., dimensions={0} | all-to-all | bytes 524288 | tf_op jit(solution)/shard_map/all_to_all | solution.py:471
  34.9 0.4 shard_map.98
  35.3 11.1 %all_to_all.21.refs_0_ = bf16[16,16,512]{2,1,0:T(8,128)(2,1)S(1)} all-to-all(bf16[16,16,512]{2,1,0:T(8,128)(2,1)S(1)} %shard_map.98), channel_id=1, replica_groups={{14,15,3,4,13,10,11,12,6,0,9,2,1,5,8,7},{30,31,19,20,29,26,27,28,22,16,..., dimensions={0} | all-to-all | bytes 524288 | tf_op jit(solution)/shard_map/all_to_all | solution.py:471
  46.4 0.0 copy-start.1
  46.4 0.0 copy-start.7
  46.4 2.2 %shard_map.99 = bf16[16,16,1024]{2,1,0:T(8,128)(2,1)} custom-call(bf16[16,16,512]{2,1,0:T(8,128)(2,1)S(1)} %all_to_all.21.refs_0_, bf16[8,128,128]{2,1,0:T(8,128)(2,1)S(1)} %get-tuple-element.24.refs_1_, bf16[8,128,128]{2,1,0:T(8,128)(2,1)S(1)} %get-tuple-element.25.refs_2_), custom_call_target="tpu_custom_call" | custom-call | flops 67108864 | bytes 1310720 | tf_op jit(solution)/shard_map/pallas_call | solution.py:449
  48.6 5.2 %all-to-all-start.3 = ((bf16[16,16,1024]{2,1,0:T(8,128)(2,1)}), bf16[16,16,1024]{2,1,0:T(8,128)(2,1)S(1)}, u32[]{:S(2)}, u32[]{:S(2)}) async-start(bf16[16,16,1024]{2,1,0:T(8,128)(2,1)} %shard_map.99), calls=%async_computation.3 | async-start | bytes 1048576 | tf_op jit(solution)/shard_map/all_to_all | solution.py:471
  53.8 0.0 copy-done.1
  53.9 0.0 copy-done.7
  53.9 2.6 %shard_map.100 = (f32[128,1024]{1,0:T(8,128)S(1)}, f32[1,1024]{1,0:T(1,128)S(1)}, bf16[5,128,1024]{2,1,0:T(8,128)(2,1)S(1)}, bf16[1024,128]{1,0:T(8,128)(2,1)}) custom-call(bf16[16,16,512]{2,1,0:T(8,128)(2,1)S(1)} %all_to_all.20.refs_0_, f32[1,128]{1,0:T(1,128)S(1)} %bitcast.17, bf16[128,128]{1,0:T(8,128)(2,1)S(1)} %copy-done.4, ...), custom_call_target="tpu_custom_call" | custom-call | flops 201326592 | bytes 3085824 | tf_op jit(solution)/shard_map/pallas_call | solution.py:449
  56.4 8.4 %all-to-all-done.3.refs_0_ = bf16[16,16,1024]{2,1,0:T(8,128)(2,1)S(1)} async-done(((bf16[16,16,1024]{2,1,0:T(8,128)(2,1)}), bf16[16,16,1024]{2,1,0:T(8,128)(2,1)S(1)}, u32[]{:S(2)}, u32[]{:S(2)}) %all-to-all-start.3) | async-done | bytes 524320 | tf_op jit(solution)/shard_map/all_to_all | solution.py:471
  64.8 1.7 %shard_map.101 = f32[1024,128]{1,0:T(8,128)} custom-call(bf16[16,16,1024]{2,1,0:T(8,128)(2,1)S(1)} %all-to-all-done.3.refs_0_, bf16[5,128,1024]{2,1,0:T(8,128)(2,1)S(1)} %get-tuple-element.31.refs_1_, f32[128,1024]{1,0:T(8,128)S(1)} %get-tuple-element.32.refs_2_, f32[1,1024]{1,0:T(1,128)S(1)} %get-tuple-element.33.refs_3_, f32[1,128]{1,0:T(1,128)S(1)} %bitcast.15, ...), custom_call_target="tpu_custom_call" | custom-call | flops 167772160 | bytes 3052032 | tf_op jit(solution)/shard_map/pallas_call | solution.py:449
Async XLA Ops:
  0.6 10.1 %copy-start.5 = (f32[128]{0:T(128)S(1)}, f32[128]{0:T(128)}, u32[]{:S(2)}) copy-start(f32[128]{0:T(128)} %param.11) | copy-start | bytes 1540
  0.6 10.1 %copy-start = (bf16[32,32,128]{2,1,0:T(8,128)(2,1)S(1)}, bf16[32,32,128]{2,1,0:T(8,128)(2,1)}, u32[]{:S(2)}) copy-start(bf16[32,32,128]{2,1,0:T(8,128)(2,1)} %param.8) | copy-start | bytes 786436
  0.7 10.1 %copy-start.2 = (bf16[32,32,128]{2,1,0:T(8,128)(2,1)S(1)}, bf16[32,32,128]{2,1,0:T(8,128)(2,1)}, u32[]{:S(2)}) copy-start(bf16[32,32,128]{2,1,0:T(8,128)(2,1)} %param.9) | copy-start | bytes 786436
  0.7 10.1 %copy-start.3 = (bf16[128,128]{1,0:T(8,128)(2,1)S(1)}, bf16[128,128]{1,0:T(8,128)(2,1)}, u32[]{:S(2)}) copy-start(bf16[128,128]{1,0:T(8,128)(2,1)} %refs_6_.1) | copy-start | bytes 98308
  0.7 10.1 %copy-start.4 = (bf16[128,128]{1,0:T(8,128)(2,1)S(1)}, bf16[128,128]{1,0:T(8,128)(2,1)}, u32[]{:S(2)}) copy-start(bf16[128,128]{1,0:T(8,128)(2,1)} %refs_2_.1) | copy-start | bytes 98308
  0.7 10.1 %copy-start.6 = (f32[128]{0:T(128)S(1)}, f32[128]{0:T(128)}, u32[]{:S(2)}) copy-start(f32[128]{0:T(128)} %param.14) | copy-start | bytes 1540
  3.3 19.6 %all-to-all-start = ((bf16[16,16,1024]{2,1,0:T(8,128)(2,1)}), bf16[16,16,1024]{2,1,0:T(8,128)(2,1)S(1)}, u32[]{:S(2)}, u32[]{:S(2)}) async-start(bf16[16,16,1024]{2,1,0:T(8,128)(2,1)} %shard_map.95), calls=%async_computation | async-start | bytes 1048576 | tf_op jit(solution)/shard_map/all_to_all | solution.py:471
  46.4 7.4 %copy-start.1 = (bf16[128,512]{1,0:T(8,128)(2,1)S(1)}, bf16[128,512]{1,0:T(8,128)(2,1)}, u32[]{:S(2)}) copy-start(bf16[128,512]{1,0:T(8,128)(2,1)} %refs_5_.3) | copy-start | bytes 393220
  46.4 7.4 %copy-start.7 = (s32[128]{0:T(128)S(1)}, s32[128]{0:T(128)}, u32[]{:S(2)}) copy-start(s32[128]{0:T(128)} %param.10) | copy-start | bytes 1540
  48.6 16.2 %all-to-all-start.3 = ((bf16[16,16,1024]{2,1,0:T(8,128)(2,1)}), bf16[16,16,1024]{2,1,0:T(8,128)(2,1)S(1)}, u32[]{:S(2)}, u32[]{:S(2)}) async-start(bf16[16,16,1024]{2,1,0:T(8,128)(2,1)} %shard_map.99), calls=%async_computation.3 | async-start | bytes 1048576 | tf_op jit(solution)/shard_map/all_to_all | solution.py:471

commit v8 on v7

--- a/solution.py
+++ b/solution.py
@@ -107,7 +107,7 @@
 F32 = jnp.float32
 BF16 = jnp.bfloat16
 LANES = 128
-FIRST = (14, 15, 3, 12, 4, 10, 11, 13, 6, 0, 9, 2, 1, 5, 8, 7)
+FIRST = (14, 15, 3, 4, 13, 10, 11, 12, 6, 0, 9, 2, 1, 5, 8, 7)
 LATER = (14, 15, 3, 4, 13, 10, 11, 12, 6, 0, 9, 2, 1, 5, 8, 7)
 FIRST_PLACE = tuple(FIRST.index(device) for device in range(len(FIRST)))
 LATER_PLACE = tuple(LATER.index(device) for device in range(len(LATER)))

time: 66.9 us -> 66.9 us (level)
  blocking collectives: 22 us -> 24 us
  waiting for transfers between devices: 19.2 us -> 17.2 us
    all_to_all x2, blocking collectives: 22 us -> 24 us  [by_channel(): lax.all_to_all(x, ('row', 'col'), 0, 0, axis_index_groups=[order], tiled=...]
    all_to_all x2, waiting for transfers between devices: 19.2 us -> 17.2 us  [by_channel(): lax.all_to_all(x, ('row', 'col'), 0, 0, axis_index_groups=[order], tiled=...]
where the time goes in v8:
time: 66.9 us; the launch traced here: 66.5 us
  blocking collectives  24 us (36%)
  waiting for transfers between devices  17.2 us (26%)
  starting transfers between devices  12.7 us (19%)
  Pallas kernels  11.8 us (18%)
  between operations  0.78 us (1%)
    all_to_all x2, blocking collectives, by_channel(): lax.all_to_all(x, ('row', 'col'), 0, 0, axis_index_groups=[order], tiled=...  24 us
    all_to_all x2, waiting for transfers between devices, by_channel(): lax.all_to_all(x, ('row', 'col'), 0, 0, axis_index_groups=[order], tiled=...  17.2 us
    all_to_all x2, starting transfers between devices, by_channel(): lax.all_to_all(x, ('row', 'col'), 0, 0, axis_index_groups=[order], tiled=...  12.7 us
    pallas_call x7, Pallas kernels, call(): pl.pallas_call(body, out_shape=tuple(outs + far_shapes), in_specs=[near_s...  11.8 us
  transfers between devices with their start and end apart: 2, of which 2 were waited for; matrix products, arithmetic and copies ran while one was open for 0% of the time, Pallas kernels for 6%

profile of v8, /device:TPU:1, one launch (start us, length us, event | category | flops | bytes accessed | tf_op | source)
XLA Modules:
  0.0 66.5 jit_solution(14822843865852225435)
XLA Ops:
  0.6 0.0 copy-start.5
  0.6 0.0 copy-start
  0.7 0.0 copy-start.2
  0.7 0.0 copy-start.3
  0.7 0.0 copy-start.4
  0.7 0.0 copy-start.6
  0.7 2.6 %shard_map.95 = bf16[16,16,1024]{2,1,0:T(8,128)(2,1)} custom-call(bf16[1024,128]{1,0:T(8,128)(2,1)} %bitcast.7, bf16[128,512]{1,0:T(8,128)(2,1)} %refs_5_.3, s32[1,128]{1,0:T(1,128)} %bitcast.18, f32[1,128]{1,0:T(1,128)} %bitcast.12), custom_call_target="tpu_custom_call" | custom-call | flops 134217728 | bytes 918528 | tf_op jit(solution)/shard_map/pallas_call | solution.py:449
  3.3 7.4 %all-to-all-start = ((bf16[16,16,1024]{2,1,0:T(8,128)(2,1)}), bf16[16,16,1024]{2,1,0:T(8,128)(2,1)S(1)}, u32[]{:S(2)}, u32[]{:S(2)}) async-start(bf16[16,16,1024]{2,1,0:T(8,128)(2,1)} %shard_map.95), calls=%async_computation | async-start | bytes 1048576 | tf_op jit(solution)/shard_map/all_to_all | solution.py:471
  10.7 0.0 copy-done.5
  10.7 0.0 copy-done
  10.7 0.0 copy-done.2
  10.7 0.0 copy-done.3
  10.7 0.0 copy-done.4
  10.7 0.0 copy-done.6
  10.8 1.3 %shard_map.96.refs_1_ = f32[128,1024]{1,0:T(8,128)S(1)} custom-call(bf16[1024,128]{1,0:T(8,128)(2,1)S(1)} %bitcast.8, bf16[1024,128]{1,0:T(8,128)(2,1)S(1)} %bitcast.10, f32[1,128]{1,0:T(1,128)S(1)} %bitcast.13, bf16[128,128]{1,0:T(8,128)(2,1)S(1)} %copy-done.3, f32[1,128]{1,0:T(1,128)S(1)} %bitcast.16, bf16[128,128]{1,0:T(8,128)(2,1)S(1)} %copy-done.4), custom_call_target="tpu_custom_call" | custom-call | flops 67108864 | bytes 1115136 | tf_op jit(solution)/shard_map/pallas_call | solution.py:449
  12.0 8.8 %all-to-all-done.refs_0_ = bf16[16,16,1024]{2,1,0:T(8,128)(2,1)S(1)} async-done(((bf16[16,16,1024]{2,1,0:T(8,128)(2,1)}), bf16[16,16,1024]{2,1,0:T(8,128)(2,1)S(1)}, u32[]{:S(2)}, u32[]{:S(2)}) %all-to-all-start) | async-done | bytes 524320 | tf_op jit(solution)/shard_map/all_to_all | solution.py:471
  20.8 1.2 %shard_map.97 = (bf16[16,16,512]{2,1,0:T(8,128)(2,1)S(1)}, bf16[8,128,128]{2,1,0:T(8,128)(2,1)S(1)}, bf16[8,128,128]{2,1,0:T(8,128)(2,1)S(1)}) custom-call(bf16[16,16,1024]{2,1,0:T(8,128)(2,1)S(1)} %all-to-all-done.refs_0_), custom_call_target="tpu_custom_call" | custom-call | flops 33554432 | bytes 1310720 | tf_op jit(solution)/shard_map/pallas_call | solution.py:449
  22.1 12.8 %all_to_all.20.refs_0_ = bf16[16,16,512]{2,1,0:T(8,128)(2,1)S(1)} all-to-all(bf16[16,16,512]{2,1,0:T(8,128)(2,1)S(1)} %get-tuple-element.22), channel_id=1, replica_groups={{14,15,3,4,13,10,11,12,6,0,9,2,1,5,8,7},{30,31,19,20,29,26,27,28,22,16,..., dimensions={0} | all-to-all | bytes 524288 | tf_op jit(solution)/shard_map/all_to_all | solution.py:471
  34.9 0.4 shard_map.98
  35.3 11.1 %all_to_all.21.refs_0_ = bf16[16,16,512]{2,1,0:T(8,128)(2,1)S(1)} all-to-all(bf16[16,16,512]{2,1,0:T(8,128)(2,1)S(1)} %shard_map.98), channel_id=1, replica_groups={{14,15,3,4,13,10,11,12,6,0,9,2,1,5,8,7},{30,31,19,20,29,26,27,28,22,16,..., dimensions={0} | all-to-all | bytes 524288 | tf_op jit(solution)/shard_map/all_to_all | solution.py:471
  46.4 0.0 copy-start.1
  46.4 0.0 copy-start.7
  46.4 2.2 %shard_map.99 = bf16[16,16,1024]{2,1,0:T(8,128)(2,1)} custom-call(bf16[16,16,512]{2,1,0:T(8,128)(2,1)S(1)} %all_to_all.21.refs_0_, bf16[8,128,128]{2,1,0:T(8,128)(2,1)S(1)} %get-tuple-element.24.refs_1_, bf16[8,128,128]{2,1,0:T(8,128)(2,1)S(1)} %get-tuple-element.25.refs_2_), custom_call_target="tpu_custom_call" | custom-call | flops 67108864 | bytes 1310720 | tf_op jit(solution)/shard_map/pallas_call | solution.py:449
  48.6 5.2 %all-to-all-start.3 = ((bf16[16,16,1024]{2,1,0:T(8,128)(2,1)}), bf16[16,16,1024]{2,1,0:T(8,128)(2,1)S(1)}, u32[]{:S(2)}, u32[]{:S(2)}) async-start(bf16[16,16,1024]{2,1,0:T(8,128)(2,1)} %shard_map.99), calls=%async_computation.3 | async-start | bytes 1048576 | tf_op jit(solution)/shard_map/all_to_all | solution.py:471
  53.8 0.0 copy-done.1
  53.9 0.0 copy-done.7
  53.9 2.6 %shard_map.100 = (f32[128,1024]{1,0:T(8,128)S(1)}, f32[1,1024]{1,0:T(1,128)S(1)}, bf16[5,128,1024]{2,1,0:T(8,128)(2,1)S(1)}, bf16[1024,128]{1,0:T(8,128)(2,1)}) custom-call(bf16[16,16,512]{2,1,0:T(8,128)(2,1)S(1)} %all_to_all.20.refs_0_, f32[1,128]{1,0:T(1,128)S(1)} %bitcast.17, bf16[128,128]{1,0:T(8,128)(2,1)S(1)} %copy-done.4, ...), custom_call_target="tpu_custom_call" | custom-call | flops 201326592 | bytes 3085824 | tf_op jit(solution)/shard_map/pallas_call | solution.py:449
  56.4 8.4 %all-to-all-done.3.refs_0_ = bf16[16,16,1024]{2,1,0:T(8,128)(2,1)S(1)} async-done(((bf16[16,16,1024]{2,1,0:T(8,128)(2,1)}), bf16[16,16,1024]{2,1,0:T(8,128)(2,1)S(1)}, u32[]{:S(2)}, u32[]{:S(2)}) %all-to-all-start.3) | async-done | bytes 524320 | tf_op jit(solution)/shard_map/all_to_all | solution.py:471
  64.8 1.7 %shard_map.101 = f32[1024,128]{1,0:T(8,128)} custom-call(bf16[16,16,1024]{2,1,0:T(8,128)(2,1)S(1)} %all-to-all-done.3.refs_0_, bf16[5,128,1024]{2,1,0:T(8,128)(2,1)S(1)} %get-tuple-element.31.refs_1_, f32[128,1024]{1,0:T(8,128)S(1)} %get-tuple-element.32.refs_2_, f32[1,1024]{1,0:T(1,128)S(1)} %get-tuple-element.33.refs_3_, f32[1,128]{1,0:T(1,128)S(1)} %bitcast.15, ...), custom_call_target="tpu_custom_call" | custom-call | flops 167772160 | bytes 3052032 | tf_op jit(solution)/shard_map/pallas_call | solution.py:449
Async XLA Ops:
  0.6 10.1 %copy-start.5 = (f32[128]{0:T(128)S(1)}, f32[128]{0:T(128)}, u32[]{:S(2)}) copy-start(f32[128]{0:T(128)} %param.11) | copy-start | bytes 1540
  0.6 10.1 %copy-start = (bf16[32,32,128]{2,1,0:T(8,128)(2,1)S(1)}, bf16[32,32,128]{2,1,0:T(8,128)(2,1)}, u32[]{:S(2)}) copy-start(bf16[32,32,128]{2,1,0:T(8,128)(2,1)} %param.8) | copy-start | bytes 786436
  0.7 10.1 %copy-start.2 = (bf16[32,32,128]{2,1,0:T(8,128)(2,1)S(1)}, bf16[32,32,128]{2,1,0:T(8,128)(2,1)}, u32[]{:S(2)}) copy-start(bf16[32,32,128]{2,1,0:T(8,128)(2,1)} %param.9) | copy-start | bytes 786436
  0.7 10.1 %copy-start.3 = (bf16[128,128]{1,0:T(8,128)(2,1)S(1)}, bf16[128,128]{1,0:T(8,128)(2,1)}, u32[]{:S(2)}) copy-start(bf16[128,128]{1,0:T(8,128)(2,1)} %refs_6_.1) | copy-start | bytes 98308
  0.7 10.1 %copy-start.4 = (bf16[128,128]{1,0:T(8,128)(2,1)S(1)}, bf16[128,128]{1,0:T(8,128)(2,1)}, u32[]{:S(2)}) copy-start(bf16[128,128]{1,0:T(8,128)(2,1)} %refs_2_.1) | copy-start | bytes 98308
  0.7 10.1 %copy-start.6 = (f32[128]{0:T(128)S(1)}, f32[128]{0:T(128)}, u32[]{:S(2)}) copy-start(f32[128]{0:T(128)} %param.14) | copy-start | bytes 1540
  3.3 17.6 %all-to-all-start = ((bf16[16,16,1024]{2,1,0:T(8,128)(2,1)}), bf16[16,16,1024]{2,1,0:T(8,128)(2,1)S(1)}, u32[]{:S(2)}, u32[]{:S(2)}) async-start(bf16[16,16,1024]{2,1,0:T(8,128)(2,1)} %shard_map.95), calls=%async_computation | async-start | bytes 1048576 | tf_op jit(solution)/shard_map/all_to_all | solution.py:471
  46.4 7.4 %copy-start.1 = (bf16[128,512]{1,0:T(8,128)(2,1)S(1)}, bf16[128,512]{1,0:T(8,128)(2,1)}, u32[]{:S(2)}) copy-start(bf16[128,512]{1,0:T(8,128)(2,1)} %refs_5_.3) | copy-start | bytes 393220
  46.4 7.4 %copy-start.7 = (s32[128]{0:T(128)S(1)}, s32[128]{0:T(128)}, u32[]{:S(2)}) copy-start(s32[128]{0:T(128)} %param.10) | copy-start | bytes 1540
  48.6 16.2 %all-to-all-start.3 = ((bf16[16,16,1024]{2,1,0:T(8,128)(2,1)}), bf16[16,16,1024]{2,1,0:T(8,128)(2,1)S(1)}, u32[]{:S(2)}, u32[]{:S(2)}) async-start(bf16[16,16,1024]{2,1,0:T(8,128)(2,1)} %shard_map.99), calls=%async_computation.3 | async-start | bytes 1048576 | tf_op jit(solution)/shard_map/all_to_all | solution.py:471
